TPU v7x, 512 devices: a whole 4x8x8 slice. The times are simulated.
512 devices in a mesh: ep: 128 (over z, y, core), dp: 4 (over x).
Axes of the slice: x: 4, y: 8, z: 8, core: 2. Of those that a mesh axis runs over, the one named last changes fastest.
Arguments:
- tokens: bfloat16 [4, 512, 3584], P(None, ('ep', 'dp')), may hold values from -6 to 6
- route_weight: bfloat16 [4, 512, 8], P(None, ('ep', 'dp')), may hold values from 0.049804688 to 0.5
- expert_ids: int32 [4, 512, 8], P(None, ('ep', 'dp')), may hold values from 0 to 55, all different within a row; in each aligned block of 4 rows (0 to 3, 4 to 7, ..., all dimensions but the last counted through in order) at most 2 rows name the same one
- replica: int32 [4, 512, 8], P(None, ('ep', 'dp')), may hold values from 0 to 1
- placement: int32 [56, 2], replicated, may hold values from 0 to 63, as said below
- w_gate: bfloat16 [128, 3584, 512], P('ep', None, 'dp'), as said below
- w_up: bfloat16 [128, 3584, 512], P('ep', None, 'dp'), as said below
- w_down: bfloat16 [128, 512, 3584], P('ep', 'dp'), as said below
Outputs:
- moe_out: bfloat16 [4, 512, 3584], P(None, ('ep', 'dp'))
- slot_rows: int32 [4, 128], P(None, 'ep')
Inputs may be any that keep to these rules, and one draw needn't show every extreme that they name: `expert_ids`: in each aligned block of 4 rows (the tokens of one ep index at one step), no expert is named by more than 2 tokens; in some blocks one expert is named by exactly 2. `placement`: every slot holds exactly one expert; 8 experts have two different slots, the others have the same slot in both columns. `w_gate`: two slots of one expert hold equal weights. `w_up`: two slots of one expert hold equal weights. `w_down`: two slots of one expert hold equal weights.
All inputs are finite; a program needn't handle non-finite values.
Results may differ from a plain program's by a relative error of at most 0.0059.
Values may be sent and summed in bfloat16 or wider, within the bound.
No kernel may reach another device: no remote copies, remote signals or barrier semaphores. Data moves between devices by JAX's collectives and lax.ppermute only.
A program may use at most 128 MiB of HBM per device.

v0:
```python
import jax
import jax.numpy as jnp
from jax import lax
from jax.sharding import PartitionSpec as P


def pick_slots(expert_ids, replica, placement):
    logical = placement.shape[0]
    chosen = jnp.where(replica[..., None] == 0, placement[:, 0], placement[:, 1])
    matches = expert_ids[..., None] == jnp.arange(logical, dtype=jnp.int32)
    return jnp.sum(jnp.where(matches, chosen, 0), axis=-1)


def place_rows(group_slots, slot_count):
    flat_slots = group_slots.reshape(-1)
    matches = (flat_slots[:, None] == jnp.arange(slot_count, dtype=jnp.int32)[None, :]).astype(
        jnp.int32
    )
    earlier = jnp.cumsum(matches, axis=0) - matches
    position = jnp.sum(earlier * matches, axis=1)
    counts = jnp.sum(matches, axis=0)
    return (position.reshape(group_slots.shape), counts)


def pack_rows(rows, slots, slot_count, capacity, top_count):
    position, counts = place_rows(slots, slot_count)
    target = (slots * capacity + position).reshape(-1)
    repeated = jnp.repeat(rows, top_count, axis=0)
    packed = jnp.zeros((slot_count * capacity, rows.shape[1]), rows.dtype).at[target].set(repeated)
    return (packed.reshape(slot_count, capacity, rows.shape[1]), target)


def expert_block(expert_rows, w_gate, w_up, w_down):
    gate_out = jnp.dot(expert_rows, w_gate[0], preferred_element_type=jnp.float32)
    up_out = jnp.dot(expert_rows, w_up[0], preferred_element_type=jnp.float32)
    hidden = (jax.nn.silu(gate_out) * up_out).astype(jnp.bfloat16)
    return jnp.dot(hidden, w_down[0], preferred_element_type=jnp.float32).astype(jnp.bfloat16)


def combine_rows(
    returned, target, weight_rows, row_count, top_count, slot_count, capacity, model_width
):
    paired = returned.reshape(slot_count, 2, capacity, model_width)
    first_half = paired[:, 0].reshape(-1, model_width)[target].astype(jnp.float32)
    second_half = paired[:, 1].reshape(-1, model_width)[target].astype(jnp.float32)
    weighted = (first_half + second_half) * weight_rows.reshape(-1, 1).astype(jnp.float32)
    return jnp.sum(weighted.reshape(row_count, top_count, model_width), axis=1)


def local(tokens, route_weight, expert_ids, replica, placement, w_gate, w_up, w_down):
    steps_total = tokens.shape[0]
    model_width = tokens.shape[2]
    ep_count = lax.axis_size("ep")
    dp_count = lax.axis_size("dp")
    slot_count = ep_count // 2
    logical = placement.shape[0]
    top_count = expert_ids.shape[2]
    own_count = expert_ids.shape[1]
    group_size = own_count * dp_count
    capacity = 2 * ((group_size * top_count + logical) // (2 * logical)) + 2
    own_slots = pick_slots(expert_ids, replica, placement)
    outputs = []
    load_rows = []
    for step_index in range(steps_total):
        group_slots = lax.all_gather(own_slots[step_index], "dp", axis=0, tiled=True)
        group_counts = place_rows(group_slots, slot_count)[1]
        arrived_counts = lax.all_to_all(
            jnp.repeat(group_counts, 2), "ep", split_axis=0, concat_axis=0, tiled=True
        )
        grouped, group_weight = (
            lax.all_gather(tokens[step_index], "dp", axis=0, tiled=True),
            lax.all_gather(route_weight[step_index], "dp", axis=0, tiled=True),
        )
        send_rows, target = pack_rows(grouped, group_slots, slot_count, capacity, top_count)
        arrived = lax.all_to_all(
            jnp.repeat(send_rows, 2, axis=0), "ep", split_axis=0, concat_axis=0, tiled=True
        )
        block_out = expert_block(arrived.reshape(-1, model_width), w_gate, w_up, w_down)
        returned = lax.all_to_all(
            block_out.reshape(ep_count, capacity, model_width),
            "ep",
            split_axis=0,
            concat_axis=0,
            tiled=True,
        )
        partial_tokens = combine_rows(
            returned, target, group_weight, group_size, top_count, slot_count, capacity, model_width
        )
        token_out = lax.psum_scatter(partial_tokens, "dp", scatter_dimension=0, tiled=True)
        outputs.append(token_out.astype(jnp.bfloat16))
        load_rows.append(jnp.sum(arrived_counts).reshape(1))
    return (jnp.stack(outputs), jnp.stack(load_rows))


def solution(mesh):
    return jax.shard_map(
        local,
        mesh=mesh,
        in_specs=(
            P(None, ("ep", "dp"), None),
            P(None, ("ep", "dp"), None),
            P(None, ("ep", "dp"), None),
            P(None, ("ep", "dp"), None),
            P(),
            P("ep", None, "dp"),
            P("ep", None, "dp"),
            P("ep", "dp", None),
        ),
        out_specs=(P(None, ("ep", "dp"), None), P(None, "ep")),
        check_vma=False,
    )
```

profile of v0, /device:TPU:8, one launch (start us, length us, event | category | flops | bytes accessed | tf_op | source)
XLA Modules:
  0.0 614.9 jit_solution(3537007303325450442)
XLA Ops:
  3.0 9.7 %all-gather.8 = s32[4,1,8]{2,1,0:T(1,128)S(1)} all-gather(s32[1,1,8]{2,1,0:T(1,128)S(1)} %get-tuple-element.28), channel_id=1, replica_groups=mesh['ep'=128,'dp'=4] {'dp'}, dimensions={0}, use_global_device_ids=true | all-gather | bytes 160 | tf_op jit(solution)/shard_map/all_gather | solution.py:65
  12.7 6.9 %all-gather.9 = s32[4,1,8]{2,1,0:T(1,128)S(1)} all-gather(s32[1,1,8]{2,1,0:T(1,128)S(1)} %get-tuple-element.31), channel_id=1, replica_groups=mesh['ep'=128,'dp'=4] {'dp'}, dimensions={0}, use_global_device_ids=true | all-gather | bytes 160 | tf_op jit(solution)/shard_map/all_gather | solution.py:65
  22.0 17.4 %all-to-all-start.8 = ((s32[128,1,1]{2,1,0:T(1,128)}), s32[128,1,1]{2,1,0:T(1,128)S(1)}, u32[]{:S(2)}, u32[]{:S(2)}) async-start(s32[128,1,1]{2,1,0:T(1,128)} %all_to_all.64), calls=%async_computation.8 | async-start | bytes 131072 | tf_op jit(solution)/shard_map/all_to_all | solution.py:67
  40.9 8.9 %all-gather.10 = s32[4,1,8]{2,1,0:T(1,128)S(1)} all-gather(s32[1,1,8]{2,1,0:T(1,128)S(1)} %get-tuple-element.30), channel_id=1, replica_groups=mesh['ep'=128,'dp'=4] {'dp'}, dimensions={0}, use_global_device_ids=true | all-gather | bytes 160 | tf_op jit(solution)/shard_map/all_gather | solution.py:65
  49.8 6.9 %all-gather.11 = s32[4,1,8]{2,1,0:T(1,128)S(1)} all-gather(s32[1,1,8]{2,1,0:T(1,128)S(1)} %get-tuple-element.29), channel_id=1, replica_groups=mesh['ep'=128,'dp'=4] {'dp'}, dimensions={0}, use_global_device_ids=true | all-gather | bytes 160 | tf_op jit(solution)/shard_map/all_gather | solution.py:65
  58.6 13.7 %all-to-all-start.9 = ((s32[128,1,1]{2,1,0:T(1,128)}), s32[128,1,1]{2,1,0:T(1,128)S(1)}, u32[]{:S(2)}, u32[]{:S(2)}) async-start(s32[128,1,1]{2,1,0:T(1,128)} %all_to_all.65), calls=%async_computation.9 | async-start | bytes 131072 | tf_op jit(solution)/shard_map/all_to_all | solution.py:67
  73.4 9.7 %all-to-all-done.9 = s32[128,1,1]{2,1,0:T(1,128)S(1)} async-done(((s32[128,1,1]{2,1,0:T(1,128)}), s32[128,1,1]{2,1,0:T(1,128)S(1)}, u32[]{:S(2)}, u32[]{:S(2)}) %all-to-all-start.9) | async-done | bytes 544 | tf_op jit(solution)/shard_map/all_to_all | solution.py:67
  83.1 6.4 %all-to-all-start.10 = ((s32[128,1,1]{2,1,0:T(1,128)}), s32[128,1,1]{2,1,0:T(1,128)S(1)}, u32[]{:S(2)}, u32[]{:S(2)}) async-start(s32[128,1,1]{2,1,0:T(1,128)} %all_to_all.66), calls=%async_computation.10 | async-start | bytes 131072 | tf_op jit(solution)/shard_map/all_to_all | solution.py:67
  90.5 9.9 %all-to-all-done.10 = s32[128,1,1]{2,1,0:T(1,128)S(1)} async-done(((s32[128,1,1]{2,1,0:T(1,128)}), s32[128,1,1]{2,1,0:T(1,128)S(1)}, u32[]{:S(2)}, u32[]{:S(2)}) %all-to-all-start.10) | async-done | bytes 544 | tf_op jit(solution)/shard_map/all_to_all | solution.py:67
  106.8 11.9 %all-gather.2 = bf16[4,1,3584]{2,1,0:T(2,128)(2,1)S(1)} all-gather(bf16[1,1,3584]{2,1,0:T(2,128)(2,1)S(1)} %get-tuple-element.24), channel_id=4, replica_groups=mesh['ep'=128,'dp'=4] {'dp'}, dimensions={0}, use_global_device_ids=true | all-gather | bytes 35840 | tf_op jit(solution)/shard_map/all_gather | solution.py:71
  122.5 14.0 %all-to-all-start.2 = ((bf16[128,2,3584]{2,1,0:T(2,128)(2,1)}), bf16[128,2,3584]{2,1,0:T(2,128)(2,1)S(1)}, u32[]{:S(2)}, u32[]{:S(2)}) async-start(bf16[128,2,3584]{2,1,0:T(2,128)(2,1)} %bitcast.181), calls=%async_computation.2 | async-start | bytes 3670016 | tf_op jit(solution)/shard_map/all_to_all | solution.py:75
  136.8 11.9 %all-gather = bf16[4,1,3584]{2,1,0:T(2,128)(2,1)S(1)} all-gather(bf16[1,1,3584]{2,1,0:T(2,128)(2,1)S(1)} %get-tuple-element.22), channel_id=2, replica_groups=mesh['ep'=128,'dp'=4] {'dp'}, dimensions={0}, use_global_device_ids=true | all-gather | bytes 35840 | tf_op jit(solution)/shard_map/all_gather | solution.py:71
  153.7 31.1 %all-to-all-done.2 = bf16[128,2,3584]{2,1,0:T(2,128)(2,1)S(1)} async-done(((bf16[128,2,3584]{2,1,0:T(2,128)(2,1)}), bf16[128,2,3584]{2,1,0:T(2,128)(2,1)S(1)}, u32[]{:S(2)}, u32[]{:S(2)}) %all-to-all-start.2) | async-done | bytes 1835040 | tf_op jit(solution)/shard_map/all_to_all | solution.py:75
  188.9 6.6 %all-to-all-start = ((bf16[128,2,3584]{2,1,0:T(2,128)(2,1)}), bf16[128,2,3584]{2,1,0:T(2,128)(2,1)}, u32[]{:S(2)}, u32[]{:S(2)}) async-start(bf16[128,2,3584]{2,1,0:T(2,128)(2,1)} %bitcast.182), calls=%async_computation | async-start | bytes 3670016 | tf_op jit(solution)/shard_map/all_to_all | solution.py:75
  195.7 11.9 %all-gather.4 = bf16[4,1,3584]{2,1,0:T(2,128)(2,1)S(1)} all-gather(bf16[1,1,3584]{2,1,0:T(2,128)(2,1)S(1)} %get-tuple-element.23), channel_id=6, replica_groups=mesh['ep'=128,'dp'=4] {'dp'}, dimensions={0}, use_global_device_ids=true | all-gather | bytes 35840 | tf_op jit(solution)/shard_map/all_gather | solution.py:71
  209.2 34.3 %all-to-all-done = bf16[128,2,3584]{2,1,0:T(2,128)(2,1)} async-done(((bf16[128,2,3584]{2,1,0:T(2,128)(2,1)}), bf16[128,2,3584]{2,1,0:T(2,128)(2,1)}, u32[]{:S(2)}, u32[]{:S(2)}) %all-to-all-start) | async-done | bytes 1835040 | tf_op jit(solution)/shard_map/all_to_all | solution.py:75
  252.0 11.9 %all-gather.6 = bf16[4,1,3584]{2,1,0:T(2,128)(2,1)S(1)} all-gather(bf16[1,1,3584]{2,1,0:T(2,128)(2,1)S(1)} %get-tuple-element.25), channel_id=8, replica_groups=mesh['ep'=128,'dp'=4] {'dp'}, dimensions={0}, use_global_device_ids=true | all-gather | bytes 35840 | tf_op jit(solution)/shard_map/all_gather | solution.py:71
  269.4 30.7 %all-to-all-done.4 = bf16[128,2,3584]{2,1,0:T(2,128)(2,1)S(1)} async-done(((bf16[128,2,3584]{2,1,0:T(2,128)(2,1)}), bf16[128,2,3584]{2,1,0:T(2,128)(2,1)S(1)}, u32[]{:S(2)}, u32[]{:S(2)}) %all-to-all-start.4) | async-done | bytes 1835040 | tf_op jit(solution)/shard_map/all_to_all | solution.py:75
  304.2 6.6 %all-to-all-start.6 = ((bf16[128,2,3584]{2,1,0:T(2,128)(2,1)}), bf16[128,2,3584]{2,1,0:T(2,128)(2,1)}, u32[]{:S(2)}, u32[]{:S(2)}) async-start(bf16[128,2,3584]{2,1,0:T(2,128)(2,1)} %bitcast.183), calls=%async_computation.6 | async-start | bytes 3670016 | tf_op jit(solution)/shard_map/all_to_all | solution.py:75
  325.1 33.7 %all-to-all-done.6 = bf16[128,2,3584]{2,1,0:T(2,128)(2,1)} async-done(((bf16[128,2,3584]{2,1,0:T(2,128)(2,1)}), bf16[128,2,3584]{2,1,0:T(2,128)(2,1)}, u32[]{:S(2)}, u32[]{:S(2)}) %all-to-all-start.6) | async-done | bytes 1835040 | tf_op jit(solution)/shard_map/all_to_all | solution.py:75
  358.7 7.0 %all-to-all-start.3 = ((bf16[128,2,3584]{2,1,0:T(2,128)(2,1)}), bf16[128,2,3584]{2,1,0:T(2,128)(2,1)}, u32[]{:S(2)}, u32[]{:S(2)}) async-start(bf16[128,2,3584]{2,1,0:T(2,128)(2,1)} %reshape.357), calls=%async_computation.3 | async-start | bytes 3670016 | tf_op jit(solution)/shard_map/all_to_all | solution.py:79
  380.0 33.5 %all-to-all-done.3 = bf16[128,2,3584]{2,1,0:T(2,128)(2,1)} async-done(((bf16[128,2,3584]{2,1,0:T(2,128)(2,1)}), bf16[128,2,3584]{2,1,0:T(2,128)(2,1)}, u32[]{:S(2)}, u32[]{:S(2)}) %all-to-all-start.3) | async-done | bytes 1835040 | tf_op jit(solution)/shard_map/all_to_all | solution.py:79
  413.5 6.6 %all-to-all-start.1 = ((bf16[128,2,3584]{2,1,0:T(2,128)(2,1)}), bf16[128,2,3584]{2,1,0:T(2,128)(2,1)}, u32[]{:S(2)}, u32[]{:S(2)}) async-start(bf16[128,2,3584]{2,1,0:T(2,128)(2,1)} %reshape.349), calls=%async_computation.1 | async-start | bytes 3670016 | tf_op jit(solution)/shard_map/all_to_all | solution.py:79
  434.4 33.7 %all-to-all-done.1 = bf16[128,2,3584]{2,1,0:T(2,128)(2,1)} async-done(((bf16[128,2,3584]{2,1,0:T(2,128)(2,1)}), bf16[128,2,3584]{2,1,0:T(2,128)(2,1)}, u32[]{:S(2)}, u32[]{:S(2)}) %all-to-all-start.1) | async-done | bytes 1835040 | tf_op jit(solution)/shard_map/all_to_all | solution.py:79
  468.1 6.6 %all-to-all-start.5 = ((bf16[128,2,3584]{2,1,0:T(2,128)(2,1)}), bf16[128,2,3584]{2,1,0:T(2,128)(2,1)}, u32[]{:S(2)}, u32[]{:S(2)}) async-start(bf16[128,2,3584]{2,1,0:T(2,128)(2,1)} %reshape.365), calls=%async_computation.5 | async-start | bytes 3670016 | tf_op jit(solution)/shard_map/all_to_all | solution.py:79
  474.7 8.9 %all-gather.3 = bf16[4,1,8]{2,1,0:T(2,128)(2,1)S(1)} all-gather(bf16[1,1,8]{2,1,0:T(2,128)(2,1)S(1)} %get-tuple-element.40), channel_id=5, replica_groups=mesh['ep'=128,'dp'=4] {'dp'}, dimensions={0}, use_global_device_ids=true | all-gather | bytes 80 | tf_op jit(solution)/shard_map/all_gather | solution.py:72
  483.6 6.9 %all-gather.1 = bf16[4,1,8]{2,1,0:T(2,128)(2,1)S(1)} all-gather(bf16[1,1,8]{2,1,0:T(2,128)(2,1)S(1)} %get-tuple-element.38), channel_id=3, replica_groups=mesh['ep'=128,'dp'=4] {'dp'}, dimensions={0}, use_global_device_ids=true | all-gather | bytes 80 | tf_op jit(solution)/shard_map/all_gather | solution.py:72
  490.5 8.9 %all-gather.5 = bf16[4,1,8]{2,1,0:T(2,128)(2,1)S(1)} all-gather(bf16[1,1,8]{2,1,0:T(2,128)(2,1)S(1)} %get-tuple-element.39), channel_id=7, replica_groups=mesh['ep'=128,'dp'=4] {'dp'}, dimensions={0}, use_global_device_ids=true | all-gather | bytes 80 | tf_op jit(solution)/shard_map/all_gather | solution.py:72
  499.5 7.1 %all-gather.7 = bf16[4,1,8]{2,1,0:T(2,128)(2,1)S(1)} all-gather(bf16[1,1,8]{2,1,0:T(2,128)(2,1)S(1)} %get-tuple-element.41), channel_id=9, replica_groups=mesh['ep'=128,'dp'=4] {'dp'}, dimensions={0}, use_global_device_ids=true | all-gather | bytes 80 | tf_op jit(solution)/shard_map/all_gather | solution.py:72
  522.6 13.7 %all-to-all-start.7 = ((bf16[128,2,3584]{2,1,0:T(2,128)(2,1)}), bf16[128,2,3584]{2,1,0:T(2,128)(2,1)}, u32[]{:S(2)}, u32[]{:S(2)}) async-start(bf16[128,2,3584]{2,1,0:T(2,128)(2,1)} %reshape.373), calls=%async_computation.7 | async-start | bytes 3670016 | tf_op jit(solution)/shard_map/all_to_all | solution.py:79
  567.0 17.3 %all-to-all-done.7 = bf16[128,2,3584]{2,1,0:T(2,128)(2,1)} async-done(((bf16[128,2,3584]{2,1,0:T(2,128)(2,1)}), bf16[128,2,3584]{2,1,0:T(2,128)(2,1)}, u32[]{:S(2)}, u32[]{:S(2)}) %all-to-all-start.7) | async-done | bytes 1835040 | tf_op jit(solution)/shard_map/all_to_all | solution.py:79
  592.3 18.7 %all-reduce.6 = (bf16[4,3584]{1,0:T(4,128)(2,1)S(1)}, bf16[4,3584]{1,0:T(4,128)(2,1)S(1)}, bf16[4,3584]{1,0:T(4,128)(2,1)S(1)}, bf16[4,3584]{1,0:T(4,128)(2,1)S(1)}) all-reduce(f32[4,3584]{1,0:T(4,128)S(1)} %fusion.24, f32[4,3584]{1,0:T(4,128)S(1)} %fusion.25, ...), channel_id=13, replica_groups=mesh['ep'=128,'dp'=4] {'dp'}, use_global_device_ids=true, to_apply=%region_20.21.clone | all-reduce | flops 57344 | bytes 344064
  (138 shorter events, 150.4 us)
Async XLA Ops:
  0.6 316.0 %copy-start = (bf16[1,128,3584]{2,1,0:T(8,128)(2,1)S(1)}, bf16[1,128,3584]{2,1,0:T(8,128)(2,1)}, u32[]{:S(2)}) copy-start(bf16[1,128,3584]{2,1,0:T(8,128)(2,1)} %param.15) | copy-start | bytes 2752516
  22.0 36.6 %all-to-all-start.8 = ((s32[128,1,1]{2,1,0:T(1,128)}), s32[128,1,1]{2,1,0:T(1,128)S(1)}, u32[]{:S(2)}, u32[]{:S(2)}) async-start(s32[128,1,1]{2,1,0:T(1,128)} %all_to_all.64), calls=%async_computation.8 | async-start | bytes 131072 | tf_op jit(solution)/shard_map/all_to_all | solution.py:67
  58.6 24.5 %all-to-all-start.9 = ((s32[128,1,1]{2,1,0:T(1,128)}), s32[128,1,1]{2,1,0:T(1,128)S(1)}, u32[]{:S(2)}, u32[]{:S(2)}) async-start(s32[128,1,1]{2,1,0:T(1,128)} %all_to_all.65), calls=%async_computation.9 | async-start | bytes 131072 | tf_op jit(solution)/shard_map/all_to_all | solution.py:67
  83.1 17.3 %all-to-all-start.10 = ((s32[128,1,1]{2,1,0:T(1,128)}), s32[128,1,1]{2,1,0:T(1,128)S(1)}, u32[]{:S(2)}, u32[]{:S(2)}) async-start(s32[128,1,1]{2,1,0:T(1,128)} %all_to_all.66), calls=%async_computation.10 | async-start | bytes 131072 | tf_op jit(solution)/shard_map/all_to_all | solution.py:67
  100.4 19.9 %all-to-all-start.11 = ((s32[128,1,1]{2,1,0:T(1,128)}), s32[128,1,1]{2,1,0:T(1,128)S(1)}, u32[]{:S(2)}, u32[]{:S(2)}) async-start(s32[128,1,1]{2,1,0:T(1,128)} %all_to_all.67), calls=%async_computation.11 | async-start | bytes 131072 | tf_op jit(solution)/shard_map/all_to_all | solution.py:67
  122.5 62.3 %all-to-all-start.2 = ((bf16[128,2,3584]{2,1,0:T(2,128)(2,1)}), bf16[128,2,3584]{2,1,0:T(2,128)(2,1)S(1)}, u32[]{:S(2)}, u32[]{:S(2)}) async-start(bf16[128,2,3584]{2,1,0:T(2,128)(2,1)} %bitcast.181), calls=%async_computation.2 | async-start | bytes 3670016 | tf_op jit(solution)/shard_map/all_to_all | solution.py:75
  184.9 4.0 copy-start.1
  188.9 54.6 %all-to-all-start = ((bf16[128,2,3584]{2,1,0:T(2,128)(2,1)}), bf16[128,2,3584]{2,1,0:T(2,128)(2,1)}, u32[]{:S(2)}, u32[]{:S(2)}) async-start(bf16[128,2,3584]{2,1,0:T(2,128)(2,1)} %bitcast.182), calls=%async_computation | async-start | bytes 3670016 | tf_op jit(solution)/shard_map/all_to_all | solution.py:75
  245.7 54.5 %all-to-all-start.4 = ((bf16[128,2,3584]{2,1,0:T(2,128)(2,1)}), bf16[128,2,3584]{2,1,0:T(2,128)(2,1)S(1)}, u32[]{:S(2)}, u32[]{:S(2)}) async-start(bf16[128,2,3584]{2,1,0:T(2,128)(2,1)} %bitcast.180), calls=%async_computation.4 | async-start | bytes 3670016 | tf_op jit(solution)/shard_map/all_to_all | solution.py:75
  300.1 4.0 copy-start.2
  304.2 54.6 %all-to-all-start.6 = ((bf16[128,2,3584]{2,1,0:T(2,128)(2,1)}), bf16[128,2,3584]{2,1,0:T(2,128)(2,1)}, u32[]{:S(2)}, u32[]{:S(2)}) async-start(bf16[128,2,3584]{2,1,0:T(2,128)(2,1)} %bitcast.183), calls=%async_computation.6 | async-start | bytes 3670016 | tf_op jit(solution)/shard_map/all_to_all | solution.py:75
  358.7 54.7 %all-to-all-start.3 = ((bf16[128,2,3584]{2,1,0:T(2,128)(2,1)}), bf16[128,2,3584]{2,1,0:T(2,128)(2,1)}, u32[]{:S(2)}, u32[]{:S(2)}) async-start(bf16[128,2,3584]{2,1,0:T(2,128)(2,1)} %reshape.357), calls=%async_computation.3 | async-start | bytes 3670016 | tf_op jit(solution)/shard_map/all_to_all | solution.py:79
  413.5 54.6 %all-to-all-start.1 = ((bf16[128,2,3584]{2,1,0:T(2,128)(2,1)}), bf16[128,2,3584]{2,1,0:T(2,128)(2,1)}, u32[]{:S(2)}, u32[]{:S(2)}) async-start(bf16[128,2,3584]{2,1,0:T(2,128)(2,1)} %reshape.349), calls=%async_computation.1 | async-start | bytes 3670016 | tf_op jit(solution)/shard_map/all_to_all | solution.py:79
  434.4 40.3 %copy-start.3 = (bf16[4,1,8]{2,0,1:T(4,128)(2,1)S(1)}, bf16[4,1,8]{2,0,1:T(4,128)(2,1)}, u32[]{:S(2)}) copy-start(bf16[4,1,8]{2,0,1:T(4,128)(2,1)} %param.9) | copy-start | bytes 196
  468.1 54.6 %all-to-all-start.5 = ((bf16[128,2,3584]{2,1,0:T(2,128)(2,1)}), bf16[128,2,3584]{2,1,0:T(2,128)(2,1)}, u32[]{:S(2)}, u32[]{:S(2)}) async-start(bf16[128,2,3584]{2,1,0:T(2,128)(2,1)} %reshape.365), calls=%async_computation.5 | async-start | bytes 3670016 | tf_op jit(solution)/shard_map/all_to_all | solution.py:79
  522.6 61.6 %all-to-all-start.7 = ((bf16[128,2,3584]{2,1,0:T(2,128)(2,1)}), bf16[128,2,3584]{2,1,0:T(2,128)(2,1)}, u32[]{:S(2)}, u32[]{:S(2)}) async-start(bf16[128,2,3584]{2,1,0:T(2,128)(2,1)} %reshape.373), calls=%async_computation.7 | async-start | bytes 3670016 | tf_op jit(solution)/shard_map/all_to_all | solution.py:79
where the time goes:
time: 626 us; the launch traced here: 615 us
  waiting for transfers between devices  234 us (37%)
  blocking collectives  131 us (21%)
  starting transfers between devices  111 us (18%)
  local copies, waits for them, and re-layouts  104 us (17%)
  matrix products  21.7 us (3%)
  other arithmetic  12 us (2%)
    all_to_all x4, waiting for transfers between devices, local(): lax.all_to_all(jnp.repeat(send_rows, 2, axis=0), 'ep', split_axis=0, conc...  130 us
    all_to_all x4, waiting for transfers between devices, local(): lax.all_to_all(block_out.reshape(ep_count, capacity, model_width), 'ep',...  84.9 us
    all_gather x4, blocking collectives, local(): lax.all_gather(tokens[step_index], 'dp', axis=0, tiled=True)  47.5 us
    all_to_all x4, starting transfers between devices, local(): lax.all_to_all(jnp.repeat(group_counts, 2), 'ep', split_axis=0, concat_ax...  43.9 us
    all_to_all x4, starting transfers between devices, local(): lax.all_to_all(block_out.reshape(ep_count, capacity, model_width), 'ep',...  33.9 us
    all_to_all x4, starting transfers between devices, local(): lax.all_to_all(jnp.repeat(send_rows, 2, axis=0), 'ep', split_axis=0, conc...  33.4 us
    all_gather x4, blocking collectives, local(): lax.all_gather(own_slots[step_index], 'dp', axis=0, tiled=True)  32.4 us
    all_gather x4, blocking collectives, local(): lax.all_gather(route_weight[step_index], 'dp', axis=0, tiled=True)  31.9 us
  transfers between devices with their start and end apart: 12, of which 10 were waited for; matrix products, arithmetic and copies ran while one was open for 17% of the time, Pallas kernels for 0%

commit v1 on v0

v1 whole, which is shorter than its diff:
```python
import functools

import jax
import jax.numpy as jnp
from jax import lax
from jax.experimental import pallas as pl
from jax.experimental.pallas import tpu as pltpu
from jax.sharding import PartitionSpec as P

BF16 = jnp.bfloat16
F32 = jnp.float32
EMPTY = 256.0


VMEM = pl.BlockSpec(memory_space=pltpu.VMEM)
HBM = pl.BlockSpec(memory_space=pltpu.HBM)
SMEM = pl.BlockSpec(memory_space=pltpu.SMEM)


def call(body, outs, args, flops=0, in_specs=None, out_specs=None, scratch=()):
    moved = sum(a.size * a.dtype.itemsize for a in args)
    moved += sum(o.size * o.dtype.itemsize for o in outs)
    return pl.pallas_call(
        body,
        out_shape=tuple(outs),
        in_specs=in_specs or [VMEM] * len(args),
        out_specs=tuple(out_specs or [VMEM] * len(outs)),
        scratch_shapes=list(scratch),
        compiler_params=pltpu.CompilerParams(vmem_limit_bytes=40 * 1024 * 1024),
        cost_estimate=pl.CostEstimate(flops=flops, bytes_accessed=moved, transcendentals=0),
    )(*args)


def route_body(
    tok_hbm, weight_hbm, ids_hbm, replica_hbm, place_hbm, send_hbm,
    tok_ref, weight_ref, ids_ref, replica_ref, place_ref, send_ref, sems,
):
    pairs = [
        (place_hbm, place_ref),
        (ids_hbm, ids_ref),
        (replica_hbm, replica_ref),
        (weight_hbm, weight_ref),
        (tok_hbm, tok_ref),
    ]
    copies = [pltpu.make_async_copy(a, b, sems.at[i]) for i, (a, b) in enumerate(pairs)]
    for c in copies:
        c.start()
    for c in copies:
        c.wait()
    dp, steps, wide = send_ref.shape
    piece = wide - 128
    top = ids_ref.shape[2]
    logical = place_ref.shape[1]
    ids, replica = ids_ref[:, 0, :], replica_ref[:, 0, :]
    first = jnp.broadcast_to(place_ref[0:1, :], (steps, logical))
    second = jnp.broadcast_to(place_ref[1:2, :], (steps, logical))
    expert = lax.broadcasted_iota(jnp.int32, (steps, logical), 1)
    lane = lax.broadcasted_iota(jnp.int32, (steps, 128), 1)
    tail = jnp.zeros((steps, 128), F32)
    for k in range(top):
        chosen = jnp.where(replica[:, k : k + 1] == 0, first, second)
        picked = jnp.where(expert == ids[:, k : k + 1], chosen, 0)
        slot = jnp.sum(picked.astype(F32), axis=1, keepdims=True)
        tail = jnp.where(lane == k, slot, tail)
        tail = jnp.where(lane == top + k, weight_ref[:, k : k + 1].astype(F32), tail)
    tail = tail.astype(BF16)
    for x in range(dp):
        send_ref[x, :, :piece] = tok_ref[:, x * piece : (x + 1) * piece]
        send_ref[x, :, piece:] = tail
    out = pltpu.make_async_copy(send_ref, send_hbm, sems.at[len(pairs)])
    out.start()
    out.wait()


def pack_body(steps, capacity, top, got_ref, rows_hbm, weight_ref, rows_ref, sems):
    tokens = got_ref.shape[0]
    piece = got_ref.shape[1] - 128
    count = rows_ref.shape[0]
    per_slot = steps * capacity
    info = got_ref[:, piece:].astype(F32).T
    row = lax.broadcasted_iota(jnp.int32, (count, tokens), 0)
    col = lax.broadcasted_iota(jnp.int32, (count, tokens), 1)
    slot = (row // per_slot).astype(F32)
    same_step = (row % per_slot) // capacity == col % steps
    place = row % capacity
    weight = jnp.zeros((count, tokens), F32)
    match = jnp.zeros((count, tokens), F32)
    for k in range(top):
        here = slot == info[k : k + 1, :]
        match += here.astype(F32)
        weight += jnp.where(here, info[top + k : top + k + 1, :], 0.0)
    match = jnp.where(same_step, match, 0.0)
    a = lax.broadcasted_iota(jnp.int32, (tokens, tokens), 0)
    b = lax.broadcasted_iota(jnp.int32, (tokens, tokens), 1)
    earlier = ((a % steps == b % steps) & (a < b)).astype(F32).astype(BF16)
    before = jnp.dot(match.astype(BF16), earlier, preferred_element_type=F32)
    taken = (match > 0.5) & (before.astype(jnp.int32) == place)
    weight_ref[...] = jnp.where(taken, weight, 0.0).astype(BF16)
    pick = taken.astype(F32)
    used = jnp.sum(pick, axis=1, keepdims=True)
    pick = pick.astype(BF16)
    head = jnp.dot(pick, got_ref[:, :128], preferred_element_type=F32)
    lane = lax.broadcasted_iota(jnp.int32, (count, 128), 1)
    head = jnp.where((lane == 0) & (used < 0.5), EMPTY, head)
    rows_ref[:, :128] = head.astype(BF16)
    rows_ref[:, 128:] = jnp.dot(pick, got_ref[:, 128:piece], preferred_element_type=F32).astype(BF16)
    out = pltpu.make_async_copy(rows_ref, rows_hbm, sems.at[0])
    out.start()
    out.wait()


def gate_up_body(steps, capacity, here_ref, x_ref, *refs):
    dp = (len(refs) - 4) // 2
    w_refs = refs[: 2 * dp]
    out_hbm, count_ref, part_ref, sems = refs[2 * dp :]
    total = x_ref.shape[0]
    rows = total // dp
    cols = w_refs[0].shape[1]
    head = x_ref[:, :128]
    used = (head[:, 0:1].astype(F32) < EMPTY).astype(F32)
    row = lax.broadcasted_iota(jnp.int32, (total, 128), 0)
    lane = lax.broadcasted_iota(jnp.int32, (total, 128), 1)
    counted = jnp.where((row // capacity) % steps == lane, used, 0.0)
    count = jnp.sum(counted, axis=0, keepdims=True)
    count_ref[...] = jnp.broadcast_to(count, count_ref.shape)
    head = jnp.where(lane == 0, head.astype(F32) * used, head.astype(F32)).astype(BF16)
    x = jnp.concatenate([head, x_ref[:, 128:]], axis=1)
    copies = []
    for b, w_ref in enumerate(w_refs):
        h, d = b // dp, b % dp
        block = lax.rem(here_ref[0] - d + dp, dp) + h * dp
        part = jnp.dot(x, w_ref[...], preferred_element_type=F32).astype(BF16)
        for i in range(dp):
            part_ref[b, i] = part[i * rows : (i + 1) * rows]
        at = pl.multiple_of(block * cols, cols)
        out = pltpu.make_async_copy(part_ref.at[b], out_hbm.at[:, :, pl.ds(at, cols)], sems.at[b])
        out.start()
        copies.append(out)
    for out in copies:
        out.wait()


def hidden_body(got_ref, out_ref):
    parts, rows, cols = got_ref.shape
    for b in range(cols // 256):
        gate = jnp.zeros((rows, 128), F32)
        up = jnp.zeros((rows, 128), F32)
        for i in range(parts):
            gate += got_ref[i, :, b * 256 : b * 256 + 128].astype(F32)
            up += got_ref[i, :, b * 256 + 128 : b * 256 + 256].astype(F32)
        hidden = (gate / (1.0 + jnp.exp(-gate)) * up).astype(BF16)
        for i in range(parts):
            out_ref[i, :, b * 128 : b * 128 + 128] = hidden


def down_body(here_ref, hid_ref, *refs):
    dp = (len(refs) - 4) // 2
    w_refs = refs[: 2 * dp]
    out_hbm, w_all, out_ref = refs[2 * dp : 2 * dp + 3]
    sems = refs[2 * dp + 3]
    hid = w_refs[0].shape[0]
    for b, w_ref in enumerate(w_refs):
        h, d = b // dp, b % dp
        block = lax.rem(here_ref[0] - d + dp, dp) + h * dp
        w_all[pl.ds(pl.multiple_of(block * hid, hid), hid), :] = w_ref[...]
    total = out_ref.shape[0]
    pieces = 2
    rows = total // pieces
    copies = []
    for i in range(pieces):
        at = slice(i * rows, (i + 1) * rows)
        out_ref[at] = jnp.dot(hid_ref[at], w_all[...], preferred_element_type=F32).astype(BF16)
        out = pltpu.make_async_copy(out_ref.at[at], out_hbm.at[at], sems.at[i])
        out.start()
        copies.append(out)
    for out in copies:
        out.wait()


def combine_body(weight_ref, got_ref, out_ref):
    out = lax.dot_general(
        weight_ref[...], got_ref[...], (((0,), (0,)), ((), ())), preferred_element_type=F32
    )
    out_ref[...] = out.astype(BF16)


def blocks_over_dp(pick, here, dp):
    out = [pick(here)]
    for d in range(1, dp):
        block = pick(lax.rem(here + d, dp))
        out.append(lax.ppermute(block, "dp", [(x, (x + d) % dp) for x in range(dp)]))
    return out


def local(tokens, route_weight, expert_ids, replica, placement, w_gate, w_up, w_down):
    steps, _, width = tokens.shape
    top = expert_ids.shape[2]
    ep = lax.axis_size("ep")
    dp = lax.axis_size("dp")
    here = lax.axis_index("dp").astype(jnp.int32)
    slots = ep // 2
    piece = width // dp
    hid = w_gate.shape[2]
    capacity = 2
    per_slot = steps * capacity
    count = slots * per_slot
    same_core = [list(range(c, ep, 2)) for c in range(2)]
    swap = [(e, e ^ 1) for e in range(ep)]
    shape = jax.ShapeDtypeStruct
    here_at = here.reshape(1)

    (send,) = call(
        route_body,
        [shape((dp, steps, piece + 128), BF16)],
        [
            tokens.reshape(steps, width),
            route_weight.reshape(steps, top),
            expert_ids,
            replica,
            placement.T,
        ],
        in_specs=[HBM] * 5,
        out_specs=[HBM],
        scratch=[
            pltpu.VMEM((steps, width), BF16),
            pltpu.VMEM((steps, top), BF16),
            pltpu.VMEM((steps, 1, top), jnp.int32),
            pltpu.VMEM((steps, 1, top), jnp.int32),
            pltpu.VMEM(placement.shape[::-1], jnp.int32),
            pltpu.VMEM((dp, steps, piece + 128), BF16),
            pltpu.SemaphoreType.DMA((6,)),
        ],
    )
    got = lax.all_to_all(send, "dp", 0, 0)

    gate, up, down = w_gate[0], w_up[0], w_down[0]

    def gate_up_of(x):
        at = (x * piece, 0)
        size = (piece, hid)
        return jnp.concatenate([lax.dynamic_slice(gate, at, size), lax.dynamic_slice(up, at, size)], axis=1)

    gate_up = blocks_over_dp(gate_up_of, here, dp)
    gate_up_all = gate_up + [lax.ppermute(w, "ep", swap) for w in gate_up]
    down_of = lambda x: lax.dynamic_slice(down, (0, x * piece), (hid, piece))
    down_own = blocks_over_dp(down_of, here, dp)
    down_all = down_own + [lax.ppermute(w, "ep", swap) for w in down_own]

    rows, weight = call(
        functools.partial(pack_body, steps, capacity, top),
        [shape((count, piece), BF16), shape((count, dp * steps), BF16)],
        [got.reshape(dp * steps, piece + 128)],
        out_specs=[HBM, VMEM],
        scratch=[pltpu.VMEM((count, piece), BF16), pltpu.SemaphoreType.DMA((1,))],
    )
    arrived = lax.all_to_all(
        rows.reshape(slots, per_slot, piece), "ep", 0, 0, axis_index_groups=same_core
    ).reshape(count, piece)

    partial, used = call(
        functools.partial(gate_up_body, steps, capacity),
        [shape((dp, count // dp, 4 * dp * hid), BF16), shape((8, 128), F32)],
        [here_at, arrived, *gate_up_all],
        2 * count * piece * 4 * dp * hid,
        in_specs=[SMEM] + [VMEM] * (2 * dp + 1),
        out_specs=[HBM, VMEM],
        scratch=[
            pltpu.VMEM((2 * dp, dp, count // dp, 2 * hid), BF16),
            pltpu.SemaphoreType.DMA((2 * dp,)),
        ],
    )
    partial = lax.all_to_all(partial, "dp", 0, 0)
    (hidden,) = call(hidden_body, [shape((dp, count // dp, 2 * dp * hid), BF16)], [partial])
    hidden = lax.all_to_all(hidden, "dp", 0, 0).reshape(count, 2 * dp * hid)
    (out,) = call(
        down_body,
        [shape((count, piece), BF16)],
        [here_at, hidden, *down_all],
        4 * count * piece * dp * hid,
        in_specs=[SMEM] + [VMEM] * (2 * dp + 1),
        out_specs=[HBM],
        scratch=[
            pltpu.VMEM((2 * dp * hid, piece), BF16),
            pltpu.VMEM((count, piece), BF16),
            pltpu.SemaphoreType.DMA((2,)),
        ],
    )
    returned = lax.all_to_all(
        out.reshape(slots, per_slot, piece), "ep", 0, 0, axis_index_groups=same_core
    ).reshape(count, piece)
    (mine,) = call(combine_body, [shape((dp * steps, piece), BF16)], [weight, returned])
    mine = lax.all_to_all(mine.reshape(dp, steps, piece), "dp", 0, 0)
    moe_out = jnp.transpose(mine, (1, 0, 2)).reshape(steps, 1, width)

    used_there = lax.ppermute(used, "ep", swap)
    slot_rows = (used + used_there)[0, :steps].astype(jnp.int32).reshape(steps, 1)
    return (moe_out, slot_rows)


def solution(mesh):
    return jax.shard_map(
        local,
        mesh=mesh,
        in_specs=(
            P(None, ("ep", "dp"), None),
            P(None, ("ep", "dp"), None),
            P(None, ("ep", "dp"), None),
            P(None, ("ep", "dp"), None),
            P(),
            P("ep", None, "dp"),
            P("ep", None, "dp"),
            P("ep", "dp", None),
        ),
        out_specs=(P(None, ("ep", "dp"), None), P(None, "ep")),
        check_vma=False,
    )
```

time: 626 us -> 193 us (0.31); the launches traced: 615 us -> 192 us
  waiting for transfers between devices: 234 us -> 51.9 us
  local copies, waits for them, and re-layouts: 104 us -> 10.4 us
  blocking collectives: 131 us -> 39.1 us
  starting transfers between devices: 111 us -> 76.2 us
  matrix products: 21.7 us -> 0 us
  Pallas kernels: 0 us -> 12.4 us
  other arithmetic: 12 us -> 0.73 us
    all_to_all x12 -> x4, waiting for transfers between devices: 234 us -> 28.9 us  [the longest x1 24 us: local(): lax.all_to_all(out.reshape(slots, per_slot, piece), 'ep', 0, 0, axis_inde...]
    all_gather x12 -> x0, blocking collectives: 112 us -> none  [the longest x4 47.5 us: local(): lax.all_gather(tokens[step_index], 'dp', axis=0, tiled=True)]
    all_to_all x12 -> x4, starting transfers between devices: 111 us -> 36.7 us  [the longest x1 16.6 us: local(): lax.all_to_all(rows.reshape(slots, per_slot, piece), 'ep', 0, 0, axis_ind...]
    reshape x20 -> x2, local copies, waits for them, and re-layouts: 42.9 us -> 0.66 us  [the longest x1 0.65 us: local(): mine = lax.all_to_all(mine.reshape(dp, steps, piece), 'dp', 0, 0)]
    ppermute x0 -> x15, starting transfers between devices: none -> 39.5 us  [the longest x6 21.3 us: blocks_over_dp(): lax.ppermute(block, 'dp', [(x, (x + d) % dp) for x in range(dp)])]
    all_to_all x0 -> x2, blocking collectives: none -> 39.1 us  [the longest x1 29.5 us: local(): partial = lax.all_to_all(partial, 'dp', 0, 0)]
    ppermute x0 -> x15, waiting for transfers between devices: none -> 23 us  [the longest x6 20.5 us: blocks_over_dp(): lax.ppermute(block, 'dp', [(x, (x + d) % dp) for x in range(dp)])]
    dot_general x8 -> x0, matrix products: 21.7 us -> none  [the longest x4 14.5 us: expert_block(): jnp.dot(hidden, w_down[0], preferred_element_type=jnp.float32)]
  transfers between devices with their start and end apart: 12 -> 19, of which waited for: 10 -> 8; matrix products, arithmetic and copies ran while one was open for 17% -> 1% of each run, Pallas kernels for 0% -> 0%
where the time goes in v1:
time: 193 us; the launch traced here: 192 us
  starting transfers between devices  76.2 us (39%)
  waiting for transfers between devices  51.9 us (27%)
  blocking collectives  39.1 us (20%)
  Pallas kernels  12.4 us (6%)
  local copies, waits for them, and re-layouts  10.4 us (5%)
    all_to_all x1, blocking collectives, local(): partial = lax.all_to_all(partial, 'dp', 0, 0)  29.5 us
    all_to_all x1, waiting for transfers between devices, local(): lax.all_to_all(out.reshape(slots, per_slot, piece), 'ep', 0, 0, axis_inde...  24 us
    ppermute x6, starting transfers between devices, blocks_over_dp(): lax.ppermute(block, 'dp', [(x, (x + d) % dp) for x in range(dp)])  21.3 us
    ppermute x6, waiting for transfers between devices, blocks_over_dp(): lax.ppermute(block, 'dp', [(x, (x + d) % dp) for x in range(dp)])  20.5 us
    all_to_all x1, starting transfers between devices, local(): lax.all_to_all(rows.reshape(slots, per_slot, piece), 'ep', 0, 0, axis_ind...  16.6 us
    all_to_all x1, starting transfers between devices, local(): lax.all_to_all(out.reshape(slots, per_slot, piece), 'ep', 0, 0, axis_inde...  12.7 us
    pallas_call x6, Pallas kernels, call(): pl.pallas_call(body, out_shape=tuple(outs), in_specs=in_specs or [VMEM] *...  12.4 us
    all_to_all x1, blocking collectives, local(): got = lax.all_to_all(send, 'dp', 0, 0)  9.54 us
  transfers between devices with their start and end apart: 19, of which 8 were waited for; matrix products, arithmetic and copies ran while one was open for 1% of the time, Pallas kernels for 0%

profile of v1, /device:TPU:8, one launch (start us, length us, event | category | flops | bytes accessed | tf_op | source)
XLA Modules:
  0.0 191.6 jit_solution(16364971103924266977)
XLA Ops:
  4.8 9.5 %all_to_all.30 = bf16[4,4,1024]{2,1,0:T(4,128)(2,1)S(1)} all-to-all(bf16[4,4,1024]{2,1,0:T(4,128)(2,1)S(1)} %shard_map.95), channel_id=1, replica_groups=mesh['ep'=128,'dp'=4] {'dp'}, dimensions={0} | all-to-all | bytes 65536 | tf_op jit(solution)/shard_map/all_to_all | solution.py:234
  14.3 1.9 shard_map.96
  16.2 16.6 %all-to-all-start.1 = ((bf16[64,8,896]{2,1,0:T(8,128)(2,1)}), bf16[64,8,896]{2,1,0:T(8,128)(2,1)S(1)}, u32[]{:S(2)}, u32[]{:S(2)}) async-start(bf16[64,8,896]{2,1,0:T(8,128)(2,1)} %bitcast.4), calls=%async_computation.1 | async-start | bytes 1835008 | tf_op jit(solution)/shard_map/all_to_all | solution.py:256
  33.1 2.5 %collective-permute-start = (bf16[896,256]{1,0:T(8,128)(2,1)S(1)}, bf16[896,256]{1,0:T(8,128)(2,1)S(1)}, u32[]{:S(2)}, u32[]{:S(2)}) collective-permute-start(bf16[896,256]{1,0:T(8,128)(2,1)S(1)} %pad_maximum_fusion.1), channel_id=1, source_target_pairs={{0,1},{1,2},{2,3},{3,0},{4,5},{5,6},{6,7},{7,4},{8,9},{9,10},{10,1... | collective-permute-start | bytes 1376264 | tf_op jit(solution)/shard_map/ppermute | solution.py:191
  35.6 4.0 %collective-permute-start.1 = (bf16[896,256]{1,0:T(8,128)(2,1)S(1)}, bf16[896,256]{1,0:T(8,128)(2,1)S(1)}, u32[]{:S(2)}, u32[]{:S(2)}) collective-permute-start(bf16[896,256]{1,0:T(8,128)(2,1)S(1)} %pad_maximum_fusion.2), channel_id=1, source_target_pairs={{0,2},{1,3},{2,0},{3,1},{4,6},{5,7},{6,4},{7,5},{8,10},{9,11},{10,... | collective-permute-start | bytes 1376264 | tf_op jit(solution)/shard_map/ppermute | solution.py:191
  39.7 3.0 %collective-permute-start.2 = (bf16[896,256]{1,0:T(8,128)(2,1)S(1)}, bf16[896,256]{1,0:T(8,128)(2,1)S(1)}, u32[]{:S(2)}, u32[]{:S(2)}) collective-permute-start(bf16[896,256]{1,0:T(8,128)(2,1)S(1)} %pad_maximum_fusion.3), channel_id=1, source_target_pairs={{0,3},{1,0},{2,1},{3,2},{4,7},{5,4},{6,5},{7,6},{8,11},{9,8},{10,9... | collective-permute-start | bytes 1376264 | tf_op jit(solution)/shard_map/ppermute | solution.py:191
  42.7 1.9 %collective-permute-start.3 = (bf16[896,256]{1,0:T(8,128)(2,1)S(1)}, bf16[896,256]{1,0:T(8,128)(2,1)S(1)}, u32[]{:S(2)}, u32[]{:S(2)}) collective-permute-start(bf16[896,256]{1,0:T(8,128)(2,1)S(1)} %pad_maximum_fusion.refs_0_), channel_id=1, source_target_pairs={{0,4},{4,0},{8,12},{12,8},{16,20},{20,16},{24,28},{28,24},{32,36},... | collective-permute-start | bytes 1376264 | tf_op jit(solution)/shard_map/ppermute | solution.py:244
  44.6 11.6 %collective-permute-done.refs_1_ = bf16[896,256]{1,0:T(8,128)(2,1)S(1)} collective-permute-done((bf16[896,256]{1,0:T(8,128)(2,1)S(1)}, bf16[896,256]{1,0:T(8,128)(2,1)S(1)}, u32[]{:S(2)}, u32[]{:S(2)}) %collective-permute-start) | collective-permute-done | bytes 458784 | tf_op jit(solution)/shard_map/ppermute | solution.py:191
  56.3 1.9 collective-permute-start.4
  58.2 2.4 %collective-permute-start.5 = (bf16[896,256]{1,0:T(8,128)(2,1)S(1)}, bf16[896,256]{1,0:T(8,128)(2,1)S(1)}, u32[]{:S(2)}, u32[]{:S(2)}) collective-permute-start(bf16[896,256]{1,0:T(8,128)(2,1)S(1)} %collective-permute-done.1.refs_2_), channel_id=1, source_target_pairs={{0,4},{4,0},{8,12},{12,8},{16,20},{20,16},{24,28},{28,24},{32,36},... | collective-permute-start | bytes 1376264 | tf_op jit(solution)/shard_map/ppermute | solution.py:244
  60.6 1.9 %collective-permute-start.6 = (bf16[896,256]{1,0:T(8,128)(2,1)S(1)}, bf16[896,256]{1,0:T(8,128)(2,1)S(1)}, u32[]{:S(2)}, u32[]{:S(2)}) collective-permute-start(bf16[896,256]{1,0:T(8,128)(2,1)S(1)} %collective-permute-done.2.refs_3_), channel_id=1, source_target_pairs={{0,4},{4,0},{8,12},{12,8},{16,20},{20,16},{24,28},{28,24},{32,36},... | collective-permute-start | bytes 1376264 | tf_op jit(solution)/shard_map/ppermute | solution.py:244
  68.2 6.0 %shard_map.97 = (bf16[4,128,2048]{2,1,0:T(8,128)(2,1)S(1)}, f32[8,128]{1,0:T(8,128)S(1)}) custom-call(s32[1]{0:T(128)} %bitcast.3.here_ref, bf16[512,896]{1,0:T(8,128)(2,1)S(1)} %bitcast.40, bf16[896,256]{1,0:T(8,128)(2,1)S(1)} %pad_maximum_fusion.refs_0_, bf16[896,256]{1,0:T(8,128)(2,1)S(1)} %collective-permute-done.refs_1_, ...), custom_call_target="tpu_custom_call" | custom-call | flops 1879048192 | bytes 6688772 | tf_op jit(solution)/shard_map/pallas_call | solution.py:23
  74.1 29.5 %all_to_all.31.got_ref = bf16[4,128,2048]{2,1,0:T(8,128)(2,1)S(1)} all-to-all(bf16[4,128,2048]{2,1,0:T(8,128)(2,1)S(1)} %get-tuple-element.8), channel_id=1, replica_groups=mesh['ep'=128,'dp'=4] {'dp'}, dimensions={0} | all-to-all | bytes 4194304 | tf_op jit(solution)/shard_map/all_to_all | solution.py:272
  103.7 1.4 shard_map.98
  105.1 3.5 %all-to-all-start.3 = ((bf16[4,128,1024]{2,1,0:T(8,128)(2,1)}), bf16[4,128,1024]{2,1,0:T(8,128)(2,1)S(1)}, u32[]{:S(2)}, u32[]{:S(2)}) async-start(bf16[4,128,1024]{2,1,0:T(8,128)(2,1)} %shard_map.98), calls=%async_computation.3 | async-start | bytes 2097152 | tf_op jit(solution)/shard_map/all_to_all | solution.py:274
  108.7 3.9 %collective-permute-start.7 = (bf16[128,896]{1,0:T(8,128)(2,1)S(1)}, bf16[128,896]{1,0:T(8,128)(2,1)S(1)}, u32[]{:S(2)}, u32[]{:S(2)}) collective-permute-start(bf16[128,896]{1,0:T(8,128)(2,1)S(1)} %get-tuple-element.11), channel_id=1, source_target_pairs={{0,1},{1,2},{2,3},{3,0},{4,5},{5,6},{6,7},{7,4},{8,9},{9,10},{10,1... | collective-permute-start | bytes 688136 | tf_op jit(solution)/shard_map/ppermute | solution.py:191
  112.6 4.6 %collective-permute-start.8 = (bf16[128,896]{1,0:T(8,128)(2,1)S(1)}, bf16[128,896]{1,0:T(8,128)(2,1)S(1)}, u32[]{:S(2)}, u32[]{:S(2)}) collective-permute-start(bf16[128,896]{1,0:T(8,128)(2,1)S(1)} %get-tuple-element.13), channel_id=1, source_target_pairs={{0,2},{1,3},{2,0},{3,1},{4,6},{5,7},{6,4},{7,5},{8,10},{9,11},{10,... | collective-permute-start | bytes 688136 | tf_op jit(solution)/shard_map/ppermute | solution.py:191
  117.2 3.4 %collective-permute-start.9 = (bf16[128,896]{1,0:T(8,128)(2,1)S(1)}, bf16[128,896]{1,0:T(8,128)(2,1)S(1)}, u32[]{:S(2)}, u32[]{:S(2)}) collective-permute-start(bf16[128,896]{1,0:T(8,128)(2,1)S(1)} %get-tuple-element.10), channel_id=1, source_target_pairs={{0,3},{1,0},{2,1},{3,2},{4,7},{5,4},{6,5},{7,6},{8,11},{9,8},{10,9... | collective-permute-start | bytes 688136 | tf_op jit(solution)/shard_map/ppermute | solution.py:191
  120.5 1.9 %collective-permute-start.10 = (bf16[128,896]{1,0:T(8,128)(2,1)S(1)}, bf16[128,896]{1,0:T(8,128)(2,1)S(1)}, u32[]{:S(2)}, u32[]{:S(2)}) collective-permute-start(bf16[128,896]{1,0:T(8,128)(2,1)S(1)} %get-tuple-element.12.refs_0_), channel_id=1, source_target_pairs={{0,4},{4,0},{8,12},{12,8},{16,20},{20,16},{24,28},{28,24},{32,36},... | collective-permute-start | bytes 688136 | tf_op jit(solution)/shard_map/ppermute | solution.py:247
  122.5 6.9 %collective-permute-done.7.refs_1_ = bf16[128,896]{1,0:T(8,128)(2,1)S(1)} collective-permute-done((bf16[128,896]{1,0:T(8,128)(2,1)S(1)}, bf16[128,896]{1,0:T(8,128)(2,1)S(1)}, u32[]{:S(2)}, u32[]{:S(2)}) %collective-permute-start.7) | collective-permute-done | bytes 229408 | tf_op jit(solution)/shard_map/ppermute | solution.py:191
  129.4 1.9 collective-permute-start.11
  131.3 2.0 %collective-permute-done.8.refs_2_ = bf16[128,896]{1,0:T(8,128)(2,1)S(1)} collective-permute-done((bf16[128,896]{1,0:T(8,128)(2,1)S(1)}, bf16[128,896]{1,0:T(8,128)(2,1)S(1)}, u32[]{:S(2)}, u32[]{:S(2)}) %collective-permute-start.8) | collective-permute-done | bytes 229408 | tf_op jit(solution)/shard_map/ppermute | solution.py:191
  133.3 1.9 collective-permute-start.12
  135.2 2.4 %collective-permute-start.13 = (bf16[128,896]{1,0:T(8,128)(2,1)S(1)}, bf16[128,896]{1,0:T(8,128)(2,1)S(1)}, u32[]{:S(2)}, u32[]{:S(2)}) collective-permute-start(bf16[128,896]{1,0:T(8,128)(2,1)S(1)} %collective-permute-done.9.refs_3_), channel_id=1, source_target_pairs={{0,4},{4,0},{8,12},{12,8},{16,20},{20,16},{24,28},{28,24},{32,36},... | collective-permute-start | bytes 688136 | tf_op jit(solution)/shard_map/ppermute | solution.py:247
  137.7 1.1 collective-permute-done.13.refs_7_
  138.7 2.3 %shard_map.99 = bf16[512,896]{1,0:T(8,128)(2,1)} custom-call(s32[1]{0:T(128)} %bitcast.3.here_ref, bf16[512,1024]{1,0:T(8,128)(2,1)S(1)} %bitcast.38, bf16[128,896]{1,0:T(8,128)(2,1)S(1)} %get-tuple-element.12.refs_0_, bf16[128,896]{1,0:T(8,128)(2,1)S(1)} %collective-permute-done.7.refs_1_, bf16[128,896]{1,0:T(8,128)(2,1)S(1)} %collective-permute-done.8.refs_2_, ...), custom_call_target="tpu_custom_call" | custom-call | flops 939524096 | bytes 3801092 | tf_op jit(solution)/shard_map/pallas_call | solution.py:23
  141.0 12.7 %all-to-all-start.4 = ((bf16[64,8,896]{2,1,0:T(8,128)(2,1)}), bf16[64,8,896]{2,1,0:T(8,128)(2,1)S(1)}, u32[]{:S(2)}, u32[]{:S(2)}) async-start(bf16[64,8,896]{2,1,0:T(8,128)(2,1)} %bitcast.19), calls=%async_computation.4 | async-start | bytes 1835008 | tf_op jit(solution)/shard_map/all_to_all | solution.py:288
  153.7 1.9 %collective-permute-start.14 = (f32[8,128]{1,0:T(8,128)S(1)}, f32[8,128]{1,0:T(8,128)S(1)}, u32[]{:S(2)}, u32[]{:S(2)}) collective-permute-start(f32[8,128]{1,0:T(8,128)S(1)} %get-tuple-element.9), channel_id=1, source_target_pairs={{0,4},{4,0},{8,12},{12,8},{16,20},{20,16},{24,28},{28,24},{32,36},... | collective-permute-start | bytes 12296 | tf_op jit(solution)/shard_map/ppermute | solution.py:295
  155.7 1.1 collective-permute-done.14
  156.8 24.0 %all-to-all-done.4 = bf16[64,8,896]{2,1,0:T(8,128)(2,1)S(1)} async-done(((bf16[64,8,896]{2,1,0:T(8,128)(2,1)}), bf16[64,8,896]{2,1,0:T(8,128)(2,1)S(1)}, u32[]{:S(2)}, u32[]{:S(2)}) %all-to-all-start.4) | async-done | bytes 917536 | tf_op jit(solution)/shard_map/all_to_all | solution.py:288
  181.7 3.8 %all-to-all-start.5 = ((bf16[4,4,896]{2,1,0:T(4,128)(2,1)}), bf16[4,4,896]{2,1,0:T(4,128)(2,1)S(1)}, u32[]{:S(2)}, u32[]{:S(2)}) async-start(bf16[4,4,896]{2,1,0:T(4,128)(2,1)} %reshape.70), calls=%async_computation.5 | async-start | bytes 57344 | tf_op jit(solution)/shard_map/all_to_all | solution.py:292
  186.1 4.9 %all-to-all-done.5 = bf16[4,4,896]{2,1,0:T(4,128)(2,1)S(1)} async-done(((bf16[4,4,896]{2,1,0:T(4,128)(2,1)}), bf16[4,4,896]{2,1,0:T(4,128)(2,1)S(1)}, u32[]{:S(2)}, u32[]{:S(2)}) %all-to-all-start.5) | async-done | bytes 28704 | tf_op jit(solution)/shard_map/all_to_all | solution.py:292
  (53 shorter events, 12.2 us)
Async XLA Ops:
  0.6 0.7 copy-start
  1.4 0.7 copy-start.1
  2.1 0.7 copy-start.2
  2.7 0.7 copy-start.3
  4.1 28.7 %copy-start.11 = (bf16[1,3584,128]{2,1,0:T(8,128)(2,1)S(1)}, bf16[1,3584,128]{2,1,0:T(8,128)(2,1)}, u32[]{:S(2)}) copy-start(bf16[1,3584,128]{2,1,0:T(8,128)(2,1)} %param.14) | copy-start | bytes 2752516
  4.1 28.7 %copy-start.12 = (bf16[1,3584,128]{2,1,0:T(8,128)(2,1)S(1)}, bf16[1,3584,128]{2,1,0:T(8,128)(2,1)}, u32[]{:S(2)}) copy-start(bf16[1,3584,128]{2,1,0:T(8,128)(2,1)} %param.13) | copy-start | bytes 2752516
  16.2 48.9 %all-to-all-start.1 = ((bf16[64,8,896]{2,1,0:T(8,128)(2,1)}), bf16[64,8,896]{2,1,0:T(8,128)(2,1)S(1)}, u32[]{:S(2)}, u32[]{:S(2)}) async-start(bf16[64,8,896]{2,1,0:T(8,128)(2,1)} %bitcast.4), calls=%async_computation.1 | async-start | bytes 1835008 | tf_op jit(solution)/shard_map/all_to_all | solution.py:256
  33.1 23.2 %collective-permute-start = (bf16[896,256]{1,0:T(8,128)(2,1)S(1)}, bf16[896,256]{1,0:T(8,128)(2,1)S(1)}, u32[]{:S(2)}, u32[]{:S(2)}) collective-permute-start(bf16[896,256]{1,0:T(8,128)(2,1)S(1)} %pad_maximum_fusion.1), channel_id=1, source_target_pairs={{0,1},{1,2},{2,3},{3,0},{4,5},{5,6},{6,7},{7,4},{8,9},{9,10},{10,1... | collective-permute-start | bytes 1376264 | tf_op jit(solution)/shard_map/ppermute | solution.py:191
  35.6 22.6 %collective-permute-start.1 = (bf16[896,256]{1,0:T(8,128)(2,1)S(1)}, bf16[896,256]{1,0:T(8,128)(2,1)S(1)}, u32[]{:S(2)}, u32[]{:S(2)}) collective-permute-start(bf16[896,256]{1,0:T(8,128)(2,1)S(1)} %pad_maximum_fusion.2), channel_id=1, source_target_pairs={{0,2},{1,3},{2,0},{3,1},{4,6},{5,7},{6,4},{7,5},{8,10},{9,11},{10,... | collective-permute-start | bytes 1376264 | tf_op jit(solution)/shard_map/ppermute | solution.py:191
  39.7 21.0 %collective-permute-start.2 = (bf16[896,256]{1,0:T(8,128)(2,1)S(1)}, bf16[896,256]{1,0:T(8,128)(2,1)S(1)}, u32[]{:S(2)}, u32[]{:S(2)}) collective-permute-start(bf16[896,256]{1,0:T(8,128)(2,1)S(1)} %pad_maximum_fusion.3), channel_id=1, source_target_pairs={{0,3},{1,0},{2,1},{3,2},{4,7},{5,4},{6,5},{7,6},{8,11},{9,8},{10,9... | collective-permute-start | bytes 1376264 | tf_op jit(solution)/shard_map/ppermute | solution.py:191
  42.7 19.8 %collective-permute-start.3 = (bf16[896,256]{1,0:T(8,128)(2,1)S(1)}, bf16[896,256]{1,0:T(8,128)(2,1)S(1)}, u32[]{:S(2)}, u32[]{:S(2)}) collective-permute-start(bf16[896,256]{1,0:T(8,128)(2,1)S(1)} %pad_maximum_fusion.refs_0_), channel_id=1, source_target_pairs={{0,4},{4,0},{8,12},{12,8},{16,20},{20,16},{24,28},{28,24},{32,36},... | collective-permute-start | bytes 1376264 | tf_op jit(solution)/shard_map/ppermute | solution.py:244
  56.3 6.3 %collective-permute-start.4 = (bf16[896,256]{1,0:T(8,128)(2,1)S(1)}, bf16[896,256]{1,0:T(8,128)(2,1)S(1)}, u32[]{:S(2)}, u32[]{:S(2)}) collective-permute-start(bf16[896,256]{1,0:T(8,128)(2,1)S(1)} %collective-permute-done.refs_1_), channel_id=1, source_target_pairs={{0,4},{4,0},{8,12},{12,8},{16,20},{20,16},{24,28},{28,24},{32,36},... | collective-permute-start | bytes 1376264 | tf_op jit(solution)/shard_map/ppermute | solution.py:244
  58.2 5.1 %collective-permute-start.5 = (bf16[896,256]{1,0:T(8,128)(2,1)S(1)}, bf16[896,256]{1,0:T(8,128)(2,1)S(1)}, u32[]{:S(2)}, u32[]{:S(2)}) collective-permute-start(bf16[896,256]{1,0:T(8,128)(2,1)S(1)} %collective-permute-done.1.refs_2_), channel_id=1, source_target_pairs={{0,4},{4,0},{8,12},{12,8},{16,20},{20,16},{24,28},{28,24},{32,36},... | collective-permute-start | bytes 1376264 | tf_op jit(solution)/shard_map/ppermute | solution.py:244
  60.6 3.7 %collective-permute-start.6 = (bf16[896,256]{1,0:T(8,128)(2,1)S(1)}, bf16[896,256]{1,0:T(8,128)(2,1)S(1)}, u32[]{:S(2)}, u32[]{:S(2)}) collective-permute-start(bf16[896,256]{1,0:T(8,128)(2,1)S(1)} %collective-permute-done.2.refs_3_), channel_id=1, source_target_pairs={{0,4},{4,0},{8,12},{12,8},{16,20},{20,16},{24,28},{28,24},{32,36},... | collective-permute-start | bytes 1376264 | tf_op jit(solution)/shard_map/ppermute | solution.py:244
  62.6 0.8 copy-start.5
  63.4 0.8 copy-start.7
  64.3 0.8 copy-start.9
  65.1 1.0 copy-start.6
  66.1 1.0 copy-start.8
  67.1 1.0 copy-start.10
  103.7 4.9 %copy-start.13 = (bf16[1,128,3584]{2,1,0:T(8,128)(2,1)S(1)}, bf16[1,128,3584]{2,1,0:T(8,128)(2,1)}, u32[]{:S(2)}) copy-start(bf16[1,128,3584]{2,1,0:T(8,128)(2,1)} %param.15) | copy-start | bytes 2752516
  105.1 33.7 %all-to-all-start.3 = ((bf16[4,128,1024]{2,1,0:T(8,128)(2,1)}), bf16[4,128,1024]{2,1,0:T(8,128)(2,1)S(1)}, u32[]{:S(2)}, u32[]{:S(2)}) async-start(bf16[4,128,1024]{2,1,0:T(8,128)(2,1)} %shard_map.98), calls=%async_computation.3 | async-start | bytes 2097152 | tf_op jit(solution)/shard_map/all_to_all | solution.py:274
  108.7 20.7 %collective-permute-start.7 = (bf16[128,896]{1,0:T(8,128)(2,1)S(1)}, bf16[128,896]{1,0:T(8,128)(2,1)S(1)}, u32[]{:S(2)}, u32[]{:S(2)}) collective-permute-start(bf16[128,896]{1,0:T(8,128)(2,1)S(1)} %get-tuple-element.11), channel_id=1, source_target_pairs={{0,1},{1,2},{2,3},{3,0},{4,5},{5,6},{6,7},{7,4},{8,9},{9,10},{10,1... | collective-permute-start | bytes 688136 | tf_op jit(solution)/shard_map/ppermute | solution.py:191
  112.6 20.7 %collective-permute-start.8 = (bf16[128,896]{1,0:T(8,128)(2,1)S(1)}, bf16[128,896]{1,0:T(8,128)(2,1)S(1)}, u32[]{:S(2)}, u32[]{:S(2)}) collective-permute-start(bf16[128,896]{1,0:T(8,128)(2,1)S(1)} %get-tuple-element.13), channel_id=1, source_target_pairs={{0,2},{1,3},{2,0},{3,1},{4,6},{5,7},{6,4},{7,5},{8,10},{9,11},{10,... | collective-permute-start | bytes 688136 | tf_op jit(solution)/shard_map/ppermute | solution.py:191
  117.2 18.0 %collective-permute-start.9 = (bf16[128,896]{1,0:T(8,128)(2,1)S(1)}, bf16[128,896]{1,0:T(8,128)(2,1)S(1)}, u32[]{:S(2)}, u32[]{:S(2)}) collective-permute-start(bf16[128,896]{1,0:T(8,128)(2,1)S(1)} %get-tuple-element.10), channel_id=1, source_target_pairs={{0,3},{1,0},{2,1},{3,2},{4,7},{5,4},{6,5},{7,6},{8,11},{9,8},{10,9... | collective-permute-start | bytes 688136 | tf_op jit(solution)/shard_map/ppermute | solution.py:191
  120.5 17.1 %collective-permute-start.10 = (bf16[128,896]{1,0:T(8,128)(2,1)S(1)}, bf16[128,896]{1,0:T(8,128)(2,1)S(1)}, u32[]{:S(2)}, u32[]{:S(2)}) collective-permute-start(bf16[128,896]{1,0:T(8,128)(2,1)S(1)} %get-tuple-element.12.refs_0_), channel_id=1, source_target_pairs={{0,4},{4,0},{8,12},{12,8},{16,20},{20,16},{24,28},{28,24},{32,36},... | collective-permute-start | bytes 688136 | tf_op jit(solution)/shard_map/ppermute | solution.py:247
  129.4 8.2 %collective-permute-start.11 = (bf16[128,896]{1,0:T(8,128)(2,1)S(1)}, bf16[128,896]{1,0:T(8,128)(2,1)S(1)}, u32[]{:S(2)}, u32[]{:S(2)}) collective-permute-start(bf16[128,896]{1,0:T(8,128)(2,1)S(1)} %collective-permute-done.7.refs_1_), channel_id=1, source_target_pairs={{0,4},{4,0},{8,12},{12,8},{16,20},{20,16},{24,28},{28,24},{32,36},... | collective-permute-start | bytes 688136 | tf_op jit(solution)/shard_map/ppermute | solution.py:247
  133.3 4.4 %collective-permute-start.12 = (bf16[128,896]{1,0:T(8,128)(2,1)S(1)}, bf16[128,896]{1,0:T(8,128)(2,1)S(1)}, u32[]{:S(2)}, u32[]{:S(2)}) collective-permute-start(bf16[128,896]{1,0:T(8,128)(2,1)S(1)} %collective-permute-done.8.refs_2_), channel_id=1, source_target_pairs={{0,4},{4,0},{8,12},{12,8},{16,20},{20,16},{24,28},{28,24},{32,36},... | collective-permute-start | bytes 688136 | tf_op jit(solution)/shard_map/ppermute | solution.py:247
  135.2 3.5 %collective-permute-start.13 = (bf16[128,896]{1,0:T(8,128)(2,1)S(1)}, bf16[128,896]{1,0:T(8,128)(2,1)S(1)}, u32[]{:S(2)}, u32[]{:S(2)}) collective-permute-start(bf16[128,896]{1,0:T(8,128)(2,1)S(1)} %collective-permute-done.9.refs_3_), channel_id=1, source_target_pairs={{0,4},{4,0},{8,12},{12,8},{16,20},{20,16},{24,28},{28,24},{32,36},... | collective-permute-start | bytes 688136 | tf_op jit(solution)/shard_map/ppermute | solution.py:247
  141.0 39.8 %all-to-all-start.4 = ((bf16[64,8,896]{2,1,0:T(8,128)(2,1)}), bf16[64,8,896]{2,1,0:T(8,128)(2,1)S(1)}, u32[]{:S(2)}, u32[]{:S(2)}) async-start(bf16[64,8,896]{2,1,0:T(8,128)(2,1)} %bitcast.19), calls=%async_computation.4 | async-start | bytes 1835008 | tf_op jit(solution)/shard_map/all_to_all | solution.py:288
  153.7 3.1 %collective-permute-start.14 = (f32[8,128]{1,0:T(8,128)S(1)}, f32[8,128]{1,0:T(8,128)S(1)}, u32[]{:S(2)}, u32[]{:S(2)}) collective-permute-start(f32[8,128]{1,0:T(8,128)S(1)} %get-tuple-element.9), channel_id=1, source_target_pairs={{0,4},{4,0},{8,12},{12,8},{16,20},{20,16},{24,28},{28,24},{32,36},... | collective-permute-start | bytes 12296 | tf_op jit(solution)/shard_map/ppermute | solution.py:295
  181.7 9.3 %all-to-all-start.5 = ((bf16[4,4,896]{2,1,0:T(4,128)(2,1)}), bf16[4,4,896]{2,1,0:T(4,128)(2,1)S(1)}, u32[]{:S(2)}, u32[]{:S(2)}) async-start(bf16[4,4,896]{2,1,0:T(4,128)(2,1)} %reshape.70), calls=%async_computation.5 | async-start | bytes 57344 | tf_op jit(solution)/shard_map/all_to_all | solution.py:292
  (1 other events, 0.7 us)

commit v2 on v1

--- a/solution.py
+++ b/solution.py
@@ -14,15 +14,24 @@
 
 VMEM = pl.BlockSpec(memory_space=pltpu.VMEM)
 HBM = pl.BlockSpec(memory_space=pltpu.HBM)
+ANY = pl.BlockSpec(memory_space=pl.ANY)
 SMEM = pl.BlockSpec(memory_space=pltpu.SMEM)
 
 
 def call(body, outs, args, flops=0, in_specs=None, out_specs=None, scratch=()):
+    if in_specs:
+        args = [
+            pltpu.with_memory_space_constraint(a, pltpu.HBM) if spec is HBM else a
+            for a, spec in zip(args, in_specs, strict=True)
+        ]
     moved = sum(a.size * a.dtype.itemsize for a in args)
     moved += sum(o.size * o.dtype.itemsize for o in outs)
     return pl.pallas_call(
         body,
-        out_shape=tuple(outs),
+        out_shape=tuple(
+            pltpu.HBM(o.shape, o.dtype) if spec is HBM else o
+            for o, spec in zip(outs, out_specs or [VMEM] * len(outs), strict=True)
+        ),
         in_specs=in_specs or [VMEM] * len(args),
         out_specs=tuple(out_specs or [VMEM] * len(outs)),
         scratch_shapes=list(scratch),
@@ -109,87 +118,94 @@
     out.wait()
 
 
-def gate_up_body(steps, capacity, here_ref, x_ref, *refs):
-    dp = (len(refs) - 4) // 2
-    w_refs = refs[: 2 * dp]
-    out_hbm, count_ref, part_ref, sems = refs[2 * dp :]
+def select_body(
+    steps, capacity, first, x_hbm, *refs
+):
+    kept_hbm, pick_ref, count_ref, total_ref, x_ref, kept_ref, sems = refs[-7:]
+    load = pltpu.make_async_copy(x_hbm, x_ref, sems.at[0])
+    load.start()
+    load.wait()
     total = x_ref.shape[0]
-    rows = total // dp
-    cols = w_refs[0].shape[1]
+    rows = kept_ref.shape[0]
     head = x_ref[:, :128]
-    used = (head[:, 0:1].astype(F32) < EMPTY).astype(F32)
+    lane8 = lax.broadcasted_iota(jnp.int32, (8, 128), 1)
+    leader = (lane8 == 0).astype(F32).astype(BF16)
+    front = lax.dot_general(leader, head, (((1,), (1,)), ((), ())), preferred_element_type=F32)
+    used = (front < EMPTY).astype(F32)
+    a = lax.broadcasted_iota(jnp.int32, (total, total), 0)
+    b = lax.broadcasted_iota(jnp.int32, (total, total), 1)
+    before = (a < b).astype(F32).astype(BF16)
+    rank = jnp.dot(used.astype(BF16), before, preferred_element_type=F32).astype(jnp.int32) - first
+    want = lax.broadcasted_iota(jnp.int32, (rows, total), 0)
+    pick = ((want == rank[0:1, :]) & (used[0:1, :] > 0.5)).astype(F32).astype(BF16)
+    pick_ref[...] = pick
+    kept_ref[...] = jnp.dot(pick, x_ref[...], preferred_element_type=F32).astype(BF16)
+    copies = []
+    for i in range(kept_hbm.shape[0]):
+        copy = pltpu.make_async_copy(kept_ref, kept_hbm.at[i], sems.at[1 + i])
+        copy.start()
+        copies.append(copy)
     row = lax.broadcasted_iota(jnp.int32, (total, 128), 0)
     lane = lax.broadcasted_iota(jnp.int32, (total, 128), 1)
-    counted = jnp.where((row // capacity) % steps == lane, used, 0.0)
-    count = jnp.sum(counted, axis=0, keepdims=True)
-    count_ref[...] = jnp.broadcast_to(count, count_ref.shape)
-    head = jnp.where(lane == 0, head.astype(F32) * used, head.astype(F32)).astype(BF16)
-    x = jnp.concatenate([head, x_ref[:, 128:]], axis=1)
-    copies = []
-    for b, w_ref in enumerate(w_refs):
-        h, d = b // dp, b % dp
-        block = lax.rem(here_ref[0] - d + dp, dp) + h * dp
-        part = jnp.dot(x, w_ref[...], preferred_element_type=F32).astype(BF16)
-        for i in range(dp):
-            part_ref[b, i] = part[i * rows : (i + 1) * rows]
-        at = pl.multiple_of(block * cols, cols)
-        out = pltpu.make_async_copy(part_ref.at[b], out_hbm.at[:, :, pl.ds(at, cols)], sems.at[b])
-        out.start()
-        copies.append(out)
-    for out in copies:
-        out.wait()
-
-
-def hidden_body(got_ref, out_ref):
-    parts, rows, cols = got_ref.shape
-    for b in range(cols // 256):
-        gate = jnp.zeros((rows, 128), F32)
-        up = jnp.zeros((rows, 128), F32)
-        for i in range(parts):
-            gate += got_ref[i, :, b * 256 : b * 256 + 128].astype(F32)
-            up += got_ref[i, :, b * 256 + 128 : b * 256 + 256].astype(F32)
-        hidden = (gate / (1.0 + jnp.exp(-gate)) * up).astype(BF16)
-        for i in range(parts):
-            out_ref[i, :, b * 128 : b * 128 + 128] = hidden
-
-
-def down_body(here_ref, hid_ref, *refs):
-    dp = (len(refs) - 4) // 2
-    w_refs = refs[: 2 * dp]
-    out_hbm, w_all, out_ref = refs[2 * dp : 2 * dp + 3]
-    sems = refs[2 * dp + 3]
-    hid = w_refs[0].shape[0]
-    for b, w_ref in enumerate(w_refs):
-        h, d = b // dp, b % dp
-        block = lax.rem(here_ref[0] - d + dp, dp) + h * dp
-        w_all[pl.ds(pl.multiple_of(block * hid, hid), hid), :] = w_ref[...]
+    its_step = ((row // capacity) % steps == lane).astype(F32).astype(BF16)
+    count_ref[...] = jnp.dot(used.astype(BF16), its_step, preferred_element_type=F32)
+    total_ref[...] = jnp.broadcast_to(jnp.sum(used, axis=1, keepdims=True), total_ref.shape).astype(jnp.int32)
+    for copy in copies:
+        copy.wait()
+
+
+def hidden_body(x_ref, gate_ref, up_ref, gate_there_ref, up_there_ref, out_hbm, out_ref, sems):
+    parts, rows, piece = x_ref.shape
+    hid = gate_ref.shape[1]
+    gate = jnp.zeros((rows, 2 * hid), F32)
+    up = jnp.zeros((rows, 2 * hid), F32)
+    for i in range(parts):
+        at = slice(i * piece, (i + 1) * piece)
+        x = x_ref[i]
+        gate_w = jnp.concatenate([gate_ref[at, :], gate_there_ref[at, :]], axis=1)
+        up_w = jnp.concatenate([up_ref[at, :], up_there_ref[at, :]], axis=1)
+        gate += jnp.dot(x, gate_w, preferred_element_type=F32)
+        up += jnp.dot(x, up_w, preferred_element_type=F32)
+    out_ref[...] = (gate / (1.0 + jnp.exp(-gate)) * up).astype(BF16)
+    copies = [pltpu.make_async_copy(out_ref, out_hbm.at[i], sems.at[i]) for i in range(parts)]
+    for copy in copies:
+        copy.start()
+    for copy in copies:
+        copy.wait()
+
+
+def down_body(here_ref, hid_ref, pick_ref, own_ref, there_ref, out_hbm, out_ref, sems):
+    dp, rows, _ = hid_ref.shape
+    out = jnp.zeros((rows, own_ref.shape[2]), F32)
+    for d in range(dp):
+        block = lax.rem(here_ref[0] - d + dp, dp)
+        w = jnp.concatenate([own_ref[d], there_ref[d]], axis=0)
+        out += jnp.dot(hid_ref[block], w, preferred_element_type=F32)
+    out = out.astype(BF16)
     total = out_ref.shape[0]
     pieces = 2
-    rows = total // pieces
+    size = total // pieces
     copies = []
     for i in range(pieces):
-        at = slice(i * rows, (i + 1) * rows)
-        out_ref[at] = jnp.dot(hid_ref[at], w_all[...], preferred_element_type=F32).astype(BF16)
-        out = pltpu.make_async_copy(out_ref.at[at], out_hbm.at[at], sems.at[i])
-        out.start()
-        copies.append(out)
-    for out in copies:
-        out.wait()
+        at = slice(i * size, (i + 1) * size)
+        spread = lax.dot_general(
+            pick_ref[:, at], out, (((0,), (0,)), ((), ())), preferred_element_type=F32
+        )
+        out_ref[at] = spread.astype(BF16)
+        copy = pltpu.make_async_copy(out_ref.at[at], out_hbm.at[at], sems.at[i])
+        copy.start()
+        copies.append(copy)
+    for copy in copies:
+        copy.wait()
 
 
 def combine_body(weight_ref, got_ref, out_ref):
+    dp, steps, _ = out_ref.shape
     out = lax.dot_general(
         weight_ref[...], got_ref[...], (((0,), (0,)), ((), ())), preferred_element_type=F32
-    )
-    out_ref[...] = out.astype(BF16)
-
-
-def blocks_over_dp(pick, here, dp):
-    out = [pick(here)]
-    for d in range(1, dp):
-        block = pick(lax.rem(here + d, dp))
-        out.append(lax.ppermute(block, "dp", [(x, (x + d) % dp) for x in range(dp)]))
-    return out
+    ).astype(BF16)
+    for i in range(dp):
+        out_ref[i] = out[i * steps : (i + 1) * steps]
 
 
 def local(tokens, route_weight, expert_ids, replica, placement, w_gate, w_up, w_down):
@@ -204,6 +220,7 @@
     capacity = 2
     per_slot = steps * capacity
     count = slots * per_slot
+    kept = count // 2
     same_core = [list(range(c, ep, 2)) for c in range(2)]
     swap = [(e, e ^ 1) for e in range(ep)]
     shape = jax.ShapeDtypeStruct
@@ -234,17 +251,14 @@
     got = lax.all_to_all(send, "dp", 0, 0)
 
     gate, up, down = w_gate[0], w_up[0], w_down[0]
-
-    def gate_up_of(x):
-        at = (x * piece, 0)
-        size = (piece, hid)
-        return jnp.concatenate([lax.dynamic_slice(gate, at, size), lax.dynamic_slice(up, at, size)], axis=1)
-
-    gate_up = blocks_over_dp(gate_up_of, here, dp)
-    gate_up_all = gate_up + [lax.ppermute(w, "ep", swap) for w in gate_up]
-    down_of = lambda x: lax.dynamic_slice(down, (0, x * piece), (hid, piece))
-    down_own = blocks_over_dp(down_of, here, dp)
-    down_all = down_own + [lax.ppermute(w, "ep", swap) for w in down_own]
+    gate_there = lax.ppermute(gate, "ep", swap)
+    up_there = lax.ppermute(up, "ep", swap)
+    down_own = []
+    for d in range(dp):
+        block = lax.dynamic_slice(down, (0, lax.rem(here + d, dp) * piece), (hid, piece))
+        down_own.append(lax.ppermute(block, "dp", [(x, (x + d) % dp) for x in range(dp)]) if d else block)
+    down_own = jnp.stack(down_own)
+    down_there = lax.ppermute(down_own, "ep", swap)
 
     rows, weight = call(
         functools.partial(pack_body, steps, capacity, top),
@@ -257,39 +271,55 @@
         rows.reshape(slots, per_slot, piece), "ep", 0, 0, axis_index_groups=same_core
     ).reshape(count, piece)
 
-    partial, used = call(
-        functools.partial(gate_up_body, steps, capacity),
-        [shape((dp, count // dp, 4 * dp * hid), BF16), shape((8, 128), F32)],
-        [here_at, arrived, *gate_up_all],
-        2 * count * piece * 4 * dp * hid,
-        in_specs=[SMEM] + [VMEM] * (2 * dp + 1),
-        out_specs=[HBM, VMEM],
-        scratch=[
-            pltpu.VMEM((2 * dp, dp, count // dp, 2 * hid), BF16),
-            pltpu.SemaphoreType.DMA((2 * dp,)),
-        ],
-    )
-    partial = lax.all_to_all(partial, "dp", 0, 0)
-    (hidden,) = call(hidden_body, [shape((dp, count // dp, 2 * dp * hid), BF16)], [partial])
-    hidden = lax.all_to_all(hidden, "dp", 0, 0).reshape(count, 2 * dp * hid)
-    (out,) = call(
-        down_body,
-        [shape((count, piece), BF16)],
-        [here_at, hidden, *down_all],
-        4 * count * piece * dp * hid,
-        in_specs=[SMEM] + [VMEM] * (2 * dp + 1),
-        out_specs=[HBM],
-        scratch=[
-            pltpu.VMEM((2 * dp * hid, piece), BF16),
-            pltpu.VMEM((count, piece), BF16),
-            pltpu.SemaphoreType.DMA((2,)),
-        ],
-    )
+    def expert_rows(first, after):
+        held, pick, used, total = call(
+            functools.partial(select_body, steps, capacity, first),
+            [
+                shape((dp, kept, piece), BF16),
+                shape((kept, count), BF16),
+                shape((8, 128), F32),
+                shape((8, 128), jnp.int32),
+            ],
+            [arrived, *after],
+            2 * kept * count * piece,
+            in_specs=[ANY] * (1 + len(after)),
+            out_specs=[HBM, VMEM, VMEM, VMEM],
+            scratch=[
+                pltpu.VMEM((count, piece), BF16),
+                pltpu.VMEM((kept, piece), BF16),
+                pltpu.SemaphoreType.DMA((1 + dp,)),
+            ],
+        )
+        held = lax.all_to_all(held, "dp", 0, 0)
+        (hidden,) = call(
+            hidden_body,
+            [shape((dp, kept, 2 * hid), BF16)],
+            [held, gate, up, gate_there, up_there],
+            8 * kept * width * hid,
+            out_specs=[HBM],
+            scratch=[pltpu.VMEM((kept, 2 * hid), BF16), pltpu.SemaphoreType.DMA((dp,))],
+        )
+        hidden = lax.all_to_all(hidden, "dp", 0, 0)
+        (out,) = call(
+            down_body,
+            [shape((count, piece), BF16)],
+            [here_at, hidden, pick, down_own, down_there],
+            4 * kept * piece * dp * hid,
+            in_specs=[SMEM] + [VMEM] * 4,
+            out_specs=[HBM],
+            scratch=[pltpu.VMEM((count, piece), BF16), pltpu.SemaphoreType.DMA((2,))],
+        )
+        return out, used, total
+
+    out, used, total = expert_rows(0, [down_there, gate_there, up_there])
+    out = lax.cond(total[0, 0] > kept, lambda o: o + expert_rows(kept, [])[0], lambda o: o, out)
     returned = lax.all_to_all(
         out.reshape(slots, per_slot, piece), "ep", 0, 0, axis_index_groups=same_core
     ).reshape(count, piece)
-    (mine,) = call(combine_body, [shape((dp * steps, piece), BF16)], [weight, returned])
-    mine = lax.all_to_all(mine.reshape(dp, steps, piece), "dp", 0, 0)
+    (mine,) = call(
+        combine_body, [shape((dp, steps, piece), BF16)], [weight, returned]
+    )
+    mine = lax.all_to_all(mine, "dp", 0, 0)
     moe_out = jnp.transpose(mine, (1, 0, 2)).reshape(steps, 1, width)
 
     used_there = lax.ppermute(used, "ep", swap)

time: 193 us -> 192 us (level)
  starting transfers between devices: 76.2 us -> 98.4 us
  waiting for transfers between devices: 51.9 us -> 42.3 us
  local copies, waits for them, and re-layouts: 10.4 us -> 2.19 us
  blocking collectives: 39.1 us -> 32.9 us
    all_to_all x1, starting transfers between devices: 12.7 us -> 57.7 us  [local(): lax.all_to_all(out.reshape(slots, per_slot, piece), 'ep', 0, 0, axis_inde...]
    ppermute x14 -> x6, starting transfers between devices: 37.6 us -> 15.2 us  [the longest x3 8.97 us: local(): lax.ppermute(block, 'dp', [(x, (x + d) % dp) for x in range(dp)])]
    ppermute x14 -> x6, waiting for transfers between devices: 21.8 us -> 4.73 us  [the longest x3 3.13 us: local(): lax.ppermute(block, 'dp', [(x, (x + d) % dp) for x in range(dp)])]
    unnamed x29 -> x15, local copies, waits for them, and re-layouts: 9.45 us -> 1.57 us
    all_to_all x2, waiting for transfers between devices: 4.92 us -> 11.8 us  [the longest x1 6.88 us: expert_rows(): hidden = lax.all_to_all(hidden, 'dp', 0, 0)]
    all_to_all x1, blocking collectives: 29.5 us -> 23.2 us  [expert_rows(): held = lax.all_to_all(held, 'dp', 0, 0)]
    all_to_all x1, waiting for transfers between devices: 0.01 us -> 4.75 us  [local(): lax.all_to_all(rows.reshape(slots, per_slot, piece), 'ep', 0, 0, axis_ind...]
    all_to_all x1, waiting for transfers between devices: 24 us -> 19.9 us  [local(): lax.all_to_all(out.reshape(slots, per_slot, piece), 'ep', 0, 0, axis_inde...]
  transfers between devices with their start and end apart: 19 -> 11, of which waited for: 8 -> 8; matrix products, arithmetic and copies ran while one was open for 1% -> 1% of each run, Pallas kernels for 0% -> 0%
where the time goes in v2:
time: 192 us; the launch traced here: 190 us
  starting transfers between devices  98.4 us (51%)
  waiting for transfers between devices  42.3 us (22%)
  blocking collectives  32.9 us (17%)
  Pallas kernels  12.5 us (7%)
  local copies, waits for them, and re-layouts  2.19 us (1%)
    all_to_all x1, starting transfers between devices, local(): lax.all_to_all(out.reshape(slots, per_slot, piece), 'ep', 0, 0, axis_inde...  57.7 us
    all_to_all x1, blocking collectives, expert_rows(): held = lax.all_to_all(held, 'dp', 0, 0)  23.2 us
    all_to_all x1, waiting for transfers between devices, local(): lax.all_to_all(out.reshape(slots, per_slot, piece), 'ep', 0, 0, axis_inde...  19.9 us
    all_to_all x1, starting transfers between devices, local(): lax.all_to_all(rows.reshape(slots, per_slot, piece), 'ep', 0, 0, axis_ind...  16.7 us
    pallas_call x6, Pallas kernels, call(): pl.pallas_call(body, out_shape=tuple((pltpu.HBM(o.shape, o.dtype) if spec...  12.5 us
    all_to_all x1, blocking collectives, local(): got = lax.all_to_all(send, 'dp', 0, 0)  9.75 us
    ppermute x3, starting transfers between devices, local(): lax.ppermute(block, 'dp', [(x, (x + d) % dp) for x in range(dp)])  8.97 us
    all_to_all x1, waiting for transfers between devices, expert_rows(): hidden = lax.all_to_all(hidden, 'dp', 0, 0)  6.88 us
  transfers between devices with their start and end apart: 11, of which 8 were waited for; matrix products, arithmetic and copies ran while one was open for 1% of the time, Pallas kernels for 0%

profile of v2, /device:TPU:8, one launch (start us, length us, event | category | flops | bytes accessed | tf_op | source)
XLA Modules:
  0.0 190.5 jit_solution(5256386678402230883)
XLA Ops:
  0.6 2.1 %shard_map.95 = bf16[4,4,1024]{2,1,0:T(4,128)(2,1)} custom-call(bf16[4,3584]{1,0:T(4,128)(2,1)} %bitcast.40, bf16[4,8]{1,0:T(4,128)(2,1)} %bitcast.41, s32[4,1,8]{2,1,0:T(1,128)} %ids_hbm.1, s32[4,1,8]{2,1,0:T(1,128)} %replica_hbm.1, s32[2,56]{1,0:T(2,128)} %bitcast.42), custom_call_target="tpu_custom_call" | custom-call | bytes 62208 | tf_op jit(solution)/shard_map/pallas_call | solution.py:29
  2.7 9.8 %all_to_all.40 = bf16[4,4,1024]{2,1,0:T(4,128)(2,1)S(1)} all-to-all(bf16[4,4,1024]{2,1,0:T(4,128)(2,1)} %shard_map.95), channel_id=1, replica_groups=mesh['ep'=128,'dp'=4] {'dp'}, dimensions={0} | all-to-all | bytes 65536 | tf_op jit(solution)/shard_map/all_to_all | solution.py:251
  12.5 1.8 shard_map.96
  14.4 16.7 %all-to-all-start.3 = ((bf16[64,8,896]{2,1,0:T(8,128)(2,1)}), bf16[64,8,896]{2,1,0:T(8,128)(2,1)S(1)}, u32[]{:S(2)}, u32[]{:S(2)}) async-start(bf16[64,8,896]{2,1,0:T(8,128)(2,1)} %bitcast.35), calls=%async_computation.3 | async-start | bytes 1835008 | tf_op jit(solution)/shard_map/all_to_all | solution.py:270
  31.2 2.5 %collective-permute-start = (bf16[128,896]{1,0:T(8,128)(2,1)S(1)}, bf16[128,896]{1,0:T(8,128)(2,1)S(1)}, u32[]{:S(2)}, u32[]{:S(2)}) collective-permute-start(bf16[128,896]{1,0:T(8,128)(2,1)S(1)} %get-tuple-element.48), channel_id=1, source_target_pairs={{0,1},{1,2},{2,3},{3,0},{4,5},{5,6},{6,7},{7,4},{8,9},{9,10},{10,1... | collective-permute-start | bytes 688136 | tf_op jit(solution)/shard_map/ppermute | solution.py:259
  33.7 4.6 %collective-permute-start.2 = (bf16[128,896]{1,0:T(8,128)(2,1)S(1)}, bf16[128,896]{1,0:T(8,128)(2,1)S(1)}, u32[]{:S(2)}, u32[]{:S(2)}) collective-permute-start(bf16[128,896]{1,0:T(8,128)(2,1)S(1)} %get-tuple-element.49), channel_id=1, source_target_pairs={{0,3},{1,0},{2,1},{3,2},{4,7},{5,4},{6,5},{7,6},{8,11},{9,8},{10,9... | collective-permute-start | bytes 688136 | tf_op jit(solution)/shard_map/ppermute | solution.py:259
  38.3 1.9 %collective-permute-start.1 = (bf16[128,896]{1,0:T(8,128)(2,1)S(1)}, bf16[128,896]{1,0:T(8,128)(2,1)S(1)}, u32[]{:S(2)}, u32[]{:S(2)}) collective-permute-start(bf16[128,896]{1,0:T(8,128)(2,1)S(1)} %get-tuple-element.50), channel_id=1, source_target_pairs={{0,2},{1,3},{2,0},{3,1},{4,6},{5,7},{6,4},{7,5},{8,10},{9,11},{10,... | collective-permute-start | bytes 688136 | tf_op jit(solution)/shard_map/ppermute | solution.py:259
  40.3 1.9 %collective-permute-start.4 = (bf16[3584,128]{1,0:T(8,128)(2,1)S(1)}, bf16[3584,128]{1,0:T(8,128)(2,1)S(1)}, u32[]{:S(2)}, u32[]{:S(2)}) collective-permute-start(bf16[3584,128]{1,0:T(8,128)(2,1)S(1)} %bitcast.30), channel_id=1, source_target_pairs={{0,4},{4,0},{8,12},{12,8},{16,20},{20,16},{24,28},{28,24},{32,36},... | collective-permute-start | bytes 2752520 | tf_op jit(solution)/shard_map/ppermute | solution.py:254
  42.2 2.4 %collective-permute-start.5 = (bf16[3584,128]{1,0:T(8,128)(2,1)}, bf16[3584,128]{1,0:T(8,128)(2,1)S(1)}, u32[]{:S(2)}, u32[]{:S(2)}) collective-permute-start(bf16[3584,128]{1,0:T(8,128)(2,1)} %bitcast.32), channel_id=1, source_target_pairs={{0,4},{4,0},{8,12},{12,8},{16,20},{20,16},{24,28},{28,24},{32,36},... | collective-permute-start | bytes 2752520 | tf_op jit(solution)/shard_map/ppermute | solution.py:255
  44.6 1.6 collective-permute-done.2
  46.2 1.5 collective-permute-done.1
  47.7 0.1 pad_maximum_fusion.own_ref
  47.9 1.9 %collective-permute-start.3 = (bf16[4,128,896]{2,1,0:T(8,128)(2,1)S(1)}, bf16[4,128,896]{2,1,0:T(8,128)(2,1)}, u32[]{:S(2)}, u32[]{:S(2)}) collective-permute-start(bf16[4,128,896]{2,1,0:T(8,128)(2,1)S(1)} %pad_maximum_fusion.own_ref), channel_id=1, source_target_pairs={{0,4},{4,0},{8,12},{12,8},{16,20},{20,16},{24,28},{28,24},{32,36},... | collective-permute-start | bytes 2752520 | tf_op jit(solution)/shard_map/ppermute | solution.py:261
  49.9 0.9 copy-done
  50.8 1.6 collective-permute-done.3.refs_0_.there_ref
  52.4 4.8 %all-to-all-done.3 = bf16[64,8,896]{2,1,0:T(8,128)(2,1)S(1)} async-done(((bf16[64,8,896]{2,1,0:T(8,128)(2,1)}), bf16[64,8,896]{2,1,0:T(8,128)(2,1)S(1)}, u32[]{:S(2)}, u32[]{:S(2)}) %all-to-all-start.3) | async-done | bytes 917536 | tf_op jit(solution)/shard_map/all_to_all | solution.py:270
  57.1 2.2 %shard_map.97 = (bf16[4,256,896]{2,1,0:T(8,128)(2,1)}, bf16[256,512]{1,0:T(8,128)(2,1)S(1)}, f32[8,128]{1,0:T(8,128)S(1)}, s32[8,128]{1,0:T(8,128)S(1)}) custom-call(bf16[512,896]{1,0:T(8,128)(2,1)S(1)} %bitcast.26, bf16[4,128,896]{2,1,0:T(8,128)(2,1)} %collective-permute-done.3.refs_0_.there_ref, ...), custom_call_target="tpu_custom_call" | custom-call | flops 234881024 | bytes 5775360 | tf_op jit(solution)/shard_map/pallas_call | solution.py:29
  59.4 23.2 %all_to_all.41.x_ref = bf16[4,256,896]{2,1,0:T(8,128)(2,1)S(1)} all-to-all(bf16[4,256,896]{2,1,0:T(8,128)(2,1)} %get-tuple-element.44), channel_id=1, replica_groups=mesh['ep'=128,'dp'=4] {'dp'}, dimensions={0} | all-to-all | bytes 3670016 | tf_op jit(solution)/shard_map/all_to_all | solution.py:293
  82.6 2.1 %shard_map.98 = bf16[4,256,256]{2,1,0:T(8,128)(2,1)} custom-call(bf16[4,256,896]{2,1,0:T(8,128)(2,1)S(1)} %all_to_all.41.x_ref, bf16[3584,128]{1,0:T(8,128)(2,1)S(1)} %bitcast.31, bf16[3584,128]{1,0:T(8,128)(2,1)S(1)} %bitcast.34, bf16[3584,128]{1,0:T(8,128)(2,1)S(1)} %collective-permute-done.4.refs_1_.gate_there_ref, bf16[3584,128]{1,0:T(8,128)(2,1)S(1)} %copy-done.1), custom_call_target="tpu_custom_call" | custom-call | flops 939524096 | bytes 6029312 | tf_op jit(solution)/shard_map/pallas_call | solution.py:29
  84.7 3.5 %all-to-all-start.5 = ((bf16[4,256,256]{2,1,0:T(8,128)(2,1)}), bf16[4,256,256]{2,1,0:T(8,128)(2,1)S(1)}, u32[]{:S(2)}, u32[]{:S(2)}) async-start(bf16[4,256,256]{2,1,0:T(8,128)(2,1)} %shard_map.98), calls=%async_computation.5 | async-start | bytes 1048576 | tf_op jit(solution)/shard_map/all_to_all | solution.py:302
  88.2 0.5 slice.6
  89.4 6.9 %all-to-all-done.5.hid_ref = bf16[4,256,256]{2,1,0:T(8,128)(2,1)S(1)} async-done(((bf16[4,256,256]{2,1,0:T(8,128)(2,1)}), bf16[4,256,256]{2,1,0:T(8,128)(2,1)S(1)}, u32[]{:S(2)}, u32[]{:S(2)}) %all-to-all-start.5) | async-done | bytes 524320 | tf_op jit(solution)/shard_map/all_to_all | solution.py:302
  96.3 3.4 %shard_map.99 = bf16[512,896]{1,0:T(8,128)(2,1)} custom-call(s32[1]{0:T(128)} %bitcast.14.here_ref, bf16[4,256,256]{2,1,0:T(8,128)(2,1)S(1)} %all-to-all-done.5.hid_ref, bf16[256,512]{1,0:T(8,128)(2,1)S(1)} %get-tuple-element.45.pick_ref, bf16[4,128,896]{2,1,0:T(8,128)(2,1)} %copy-done.3, bf16[4,128,896]{2,1,0:T(8,128)(2,1)} %collective-permute-done.3.refs_0_.there_ref), custom_call_target="tpu_custom_call" | custom-call | flops 469762048 | bytes 3538948 | tf_op jit(solution)/shard_map/pallas_call | solution.py:29
  99.7 57.7 %all-to-all-start.6 = ((bf16[64,8,896]{2,1,0:T(8,128)(2,1)}), bf16[64,8,896]{2,1,0:T(8,128)(2,1)S(1)}, u32[]{:S(2)}, u32[]{:S(2)}) async-start(bf16[64,8,896]{2,1,0:T(8,128)(2,1)} %bitcast.28), calls=%async_computation.6 | async-start | bytes 1835008 | tf_op jit(solution)/shard_map/all_to_all | solution.py:316
  157.4 1.9 %collective-permute-start.6 = (f32[8,128]{1,0:T(8,128)S(1)}, f32[8,128]{1,0:T(8,128)S(1)}, u32[]{:S(2)}, u32[]{:S(2)}) collective-permute-start(f32[8,128]{1,0:T(8,128)S(1)} %get-tuple-element.46), channel_id=1, source_target_pairs={{0,4},{4,0},{8,12},{12,8},{16,20},{20,16},{24,28},{28,24},{32,36},... | collective-permute-start | bytes 12296 | tf_op jit(solution)/shard_map/ppermute | solution.py:325
  159.3 1.1 collective-permute-done.6
  160.5 19.9 %all-to-all-done.6 = bf16[64,8,896]{2,1,0:T(8,128)(2,1)S(1)} async-done(((bf16[64,8,896]{2,1,0:T(8,128)(2,1)}), bf16[64,8,896]{2,1,0:T(8,128)(2,1)S(1)}, u32[]{:S(2)}, u32[]{:S(2)}) %all-to-all-start.6) | async-done | bytes 917536 | tf_op jit(solution)/shard_map/all_to_all | solution.py:316
  180.3 0.9 shard_map.100
  181.2 3.3 %all-to-all-start.7 = ((bf16[4,4,896]{2,1,0:T(4,128)(2,1)}), bf16[4,4,896]{2,1,0:T(4,128)(2,1)S(1)}, u32[]{:S(2)}, u32[]{:S(2)}) async-start(bf16[4,4,896]{2,1,0:T(4,128)(2,1)} %shard_map.100), calls=%async_computation.7 | async-start | bytes 57344 | tf_op jit(solution)/shard_map/all_to_all | solution.py:322
  184.5 0.5 convert_bitcast_fusion
  185.0 4.9 %all-to-all-done.7 = bf16[4,4,896]{2,1,0:T(4,128)(2,1)S(1)} async-done(((bf16[4,4,896]{2,1,0:T(4,128)(2,1)}), bf16[4,4,896]{2,1,0:T(4,128)(2,1)S(1)}, u32[]{:S(2)}, u32[]{:S(2)}) %all-to-all-start.7) | async-done | bytes 28704 | tf_op jit(solution)/shard_map/all_to_all | solution.py:322
  189.9 0.6 copy.13
  (20 shorter events, 0.2 us)
Async XLA Ops:
  0.6 30.5 %copy-start.12 = (bf16[1,128,3584]{2,1,0:T(8,128)(2,1)S(1)}, bf16[1,128,3584]{2,1,0:T(8,128)(2,1)}, u32[]{:S(2)}) copy-start(bf16[1,128,3584]{2,1,0:T(8,128)(2,1)} %param.17) | copy-start | bytes 2752516
  14.4 25.9 %copy-start.7 = (bf16[1,3584,128]{2,1,0:T(8,128)(2,1)S(1)}, bf16[1,3584,128]{2,1,0:T(8,128)(2,1)}, u32[]{:S(2)}) copy-start(bf16[1,3584,128]{2,1,0:T(8,128)(2,1)} %param.15) | copy-start | bytes 2752516
  14.4 42.8 %all-to-all-start.3 = ((bf16[64,8,896]{2,1,0:T(8,128)(2,1)}), bf16[64,8,896]{2,1,0:T(8,128)(2,1)S(1)}, u32[]{:S(2)}, u32[]{:S(2)}) async-start(bf16[64,8,896]{2,1,0:T(8,128)(2,1)} %bitcast.35), calls=%async_computation.3 | async-start | bytes 1835008 | tf_op jit(solution)/shard_map/all_to_all | solution.py:270
  31.2 13.4 %collective-permute-start = (bf16[128,896]{1,0:T(8,128)(2,1)S(1)}, bf16[128,896]{1,0:T(8,128)(2,1)S(1)}, u32[]{:S(2)}, u32[]{:S(2)}) collective-permute-start(bf16[128,896]{1,0:T(8,128)(2,1)S(1)} %get-tuple-element.48), channel_id=1, source_target_pairs={{0,1},{1,2},{2,3},{3,0},{4,5},{5,6},{6,7},{7,4},{8,9},{9,10},{10,1... | collective-permute-start | bytes 688136 | tf_op jit(solution)/shard_map/ppermute | solution.py:259
  33.7 12.5 %collective-permute-start.2 = (bf16[128,896]{1,0:T(8,128)(2,1)S(1)}, bf16[128,896]{1,0:T(8,128)(2,1)S(1)}, u32[]{:S(2)}, u32[]{:S(2)}) collective-permute-start(bf16[128,896]{1,0:T(8,128)(2,1)S(1)} %get-tuple-element.49), channel_id=1, source_target_pairs={{0,3},{1,0},{2,1},{3,2},{4,7},{5,4},{6,5},{7,6},{8,11},{9,8},{10,9... | collective-permute-start | bytes 688136 | tf_op jit(solution)/shard_map/ppermute | solution.py:259
  38.3 9.4 %collective-permute-start.1 = (bf16[128,896]{1,0:T(8,128)(2,1)S(1)}, bf16[128,896]{1,0:T(8,128)(2,1)S(1)}, u32[]{:S(2)}, u32[]{:S(2)}) collective-permute-start(bf16[128,896]{1,0:T(8,128)(2,1)S(1)} %get-tuple-element.50), channel_id=1, source_target_pairs={{0,2},{1,3},{2,0},{3,1},{4,6},{5,7},{6,4},{7,5},{8,10},{9,11},{10,... | collective-permute-start | bytes 688136 | tf_op jit(solution)/shard_map/ppermute | solution.py:259
  40.3 9.6 %collective-permute-start.4 = (bf16[3584,128]{1,0:T(8,128)(2,1)S(1)}, bf16[3584,128]{1,0:T(8,128)(2,1)S(1)}, u32[]{:S(2)}, u32[]{:S(2)}) collective-permute-start(bf16[3584,128]{1,0:T(8,128)(2,1)S(1)} %bitcast.30), channel_id=1, source_target_pairs={{0,4},{4,0},{8,12},{12,8},{16,20},{20,16},{24,28},{28,24},{32,36},... | collective-permute-start | bytes 2752520 | tf_op jit(solution)/shard_map/ppermute | solution.py:254
  42.2 7.6 %collective-permute-start.5 = (bf16[3584,128]{1,0:T(8,128)(2,1)}, bf16[3584,128]{1,0:T(8,128)(2,1)S(1)}, u32[]{:S(2)}, u32[]{:S(2)}) collective-permute-start(bf16[3584,128]{1,0:T(8,128)(2,1)} %bitcast.32), channel_id=1, source_target_pairs={{0,4},{4,0},{8,12},{12,8},{16,20},{20,16},{24,28},{28,24},{32,36},... | collective-permute-start | bytes 2752520 | tf_op jit(solution)/shard_map/ppermute | solution.py:255
  47.9 2.0 %copy-start.3 = (bf16[4,128,896]{2,1,0:T(8,128)(2,1)}, bf16[4,128,896]{2,1,0:T(8,128)(2,1)S(1)}, u32[]{:S(2)}) copy-start(bf16[4,128,896]{2,1,0:T(8,128)(2,1)S(1)} %pad_maximum_fusion.own_ref) | copy-start | bytes 2752516
  47.9 4.5 %collective-permute-start.3 = (bf16[4,128,896]{2,1,0:T(8,128)(2,1)S(1)}, bf16[4,128,896]{2,1,0:T(8,128)(2,1)}, u32[]{:S(2)}, u32[]{:S(2)}) collective-permute-start(bf16[4,128,896]{2,1,0:T(8,128)(2,1)S(1)} %pad_maximum_fusion.own_ref), channel_id=1, source_target_pairs={{0,4},{4,0},{8,12},{12,8},{16,20},{20,16},{24,28},{28,24},{32,36},... | collective-permute-start | bytes 2752520 | tf_op jit(solution)/shard_map/ppermute | solution.py:261
  49.8 0.9 copy-start
  59.4 23.2 %copy-start.1 = (bf16[3584,128]{1,0:T(8,128)(2,1)S(1)}, bf16[3584,128]{1,0:T(8,128)(2,1)}, u32[]{:S(2)}) copy-start(bf16[3584,128]{1,0:T(8,128)(2,1)} %copy-done) | copy-start | bytes 2752516
  59.4 23.2 %copy-start.8 = (bf16[1,3584,128]{2,1,0:T(8,128)(2,1)S(1)}, bf16[1,3584,128]{2,1,0:T(8,128)(2,1)}, u32[]{:S(2)}) copy-start(bf16[1,3584,128]{2,1,0:T(8,128)(2,1)} %param.15) | copy-start | bytes 2752516
  59.4 23.2 %copy-start.10 = (bf16[1,3584,128]{2,1,0:T(8,128)(2,1)S(1)}, bf16[1,3584,128]{2,1,0:T(8,128)(2,1)}, u32[]{:S(2)}) copy-start(bf16[1,3584,128]{2,1,0:T(8,128)(2,1)} %param.16) | copy-start | bytes 2752516
  84.7 11.5 %all-to-all-start.5 = ((bf16[4,256,256]{2,1,0:T(8,128)(2,1)}), bf16[4,256,256]{2,1,0:T(8,128)(2,1)S(1)}, u32[]{:S(2)}, u32[]{:S(2)}) async-start(bf16[4,256,256]{2,1,0:T(8,128)(2,1)} %shard_map.98), calls=%async_computation.5 | async-start | bytes 1048576 | tf_op jit(solution)/shard_map/all_to_all | solution.py:302
  99.7 80.7 %all-to-all-start.6 = ((bf16[64,8,896]{2,1,0:T(8,128)(2,1)}), bf16[64,8,896]{2,1,0:T(8,128)(2,1)S(1)}, u32[]{:S(2)}, u32[]{:S(2)}) async-start(bf16[64,8,896]{2,1,0:T(8,128)(2,1)} %bitcast.28), calls=%async_computation.6 | async-start | bytes 1835008 | tf_op jit(solution)/shard_map/all_to_all | solution.py:316
  157.4 3.1 %collective-permute-start.6 = (f32[8,128]{1,0:T(8,128)S(1)}, f32[8,128]{1,0:T(8,128)S(1)}, u32[]{:S(2)}, u32[]{:S(2)}) collective-permute-start(f32[8,128]{1,0:T(8,128)S(1)} %get-tuple-element.46), channel_id=1, source_target_pairs={{0,4},{4,0},{8,12},{12,8},{16,20},{20,16},{24,28},{28,24},{32,36},... | collective-permute-start | bytes 12296 | tf_op jit(solution)/shard_map/ppermute | solution.py:325
  181.2 8.7 %all-to-all-start.7 = ((bf16[4,4,896]{2,1,0:T(4,128)(2,1)}), bf16[4,4,896]{2,1,0:T(4,128)(2,1)S(1)}, u32[]{:S(2)}, u32[]{:S(2)}) async-start(bf16[4,4,896]{2,1,0:T(4,128)(2,1)} %shard_map.100), calls=%async_computation.7 | async-start | bytes 57344 | tf_op jit(solution)/shard_map/all_to_all | solution.py:322

commit v3 on v2

--- a/solution.py
+++ b/solution.py
@@ -18,7 +18,7 @@
 SMEM = pl.BlockSpec(memory_space=pltpu.SMEM)
 
 
-def call(body, outs, args, flops=0, in_specs=None, out_specs=None, scratch=()):
+def call(body, outs, args, flops=0, in_specs=None, out_specs=None, scratch=(), vmem=12):
     if in_specs:
         args = [
             pltpu.with_memory_space_constraint(a, pltpu.HBM) if spec is HBM else a
@@ -35,7 +35,7 @@
         in_specs=in_specs or [VMEM] * len(args),
         out_specs=tuple(out_specs or [VMEM] * len(outs)),
         scratch_shapes=list(scratch),
-        compiler_params=pltpu.CompilerParams(vmem_limit_bytes=40 * 1024 * 1024),
+        compiler_params=pltpu.CompilerParams(vmem_limit_bytes=vmem * 1024 * 1024),
         cost_estimate=pl.CostEstimate(flops=flops, bytes_accessed=moved, transcendentals=0),
     )(*args)
 
@@ -118,80 +118,78 @@
     out.wait()
 
 
-def select_body(
-    steps, capacity, first, x_hbm, *refs
-):
-    kept_hbm, pick_ref, count_ref, total_ref, x_ref, kept_ref, sems = refs[-7:]
-    load = pltpu.make_async_copy(x_hbm, x_ref, sems.at[0])
-    load.start()
-    load.wait()
+def split_body(steps, capacity, x_ref, *refs):
+    first_ref, second_ref, count_ref = refs[-3:]
     total = x_ref.shape[0]
-    rows = kept_ref.shape[0]
-    head = x_ref[:, :128]
-    lane8 = lax.broadcasted_iota(jnp.int32, (8, 128), 1)
-    leader = (lane8 == 0).astype(F32).astype(BF16)
-    front = lax.dot_general(leader, head, (((1,), (1,)), ((), ())), preferred_element_type=F32)
-    used = (front < EMPTY).astype(F32)
-    a = lax.broadcasted_iota(jnp.int32, (total, total), 0)
-    b = lax.broadcasted_iota(jnp.int32, (total, total), 1)
-    before = (a < b).astype(F32).astype(BF16)
-    rank = jnp.dot(used.astype(BF16), before, preferred_element_type=F32).astype(jnp.int32) - first
-    want = lax.broadcasted_iota(jnp.int32, (rows, total), 0)
-    pick = ((want == rank[0:1, :]) & (used[0:1, :] > 0.5)).astype(F32).astype(BF16)
-    pick_ref[...] = pick
-    kept_ref[...] = jnp.dot(pick, x_ref[...], preferred_element_type=F32).astype(BF16)
-    copies = []
-    for i in range(kept_hbm.shape[0]):
-        copy = pltpu.make_async_copy(kept_ref, kept_hbm.at[i], sems.at[1 + i])
-        copy.start()
-        copies.append(copy)
+    half = total // 2
+    head = x_ref[:, :128].astype(F32)
+    used = (head[:, 0:1] < EMPTY).astype(F32)
     row = lax.broadcasted_iota(jnp.int32, (total, 128), 0)
     lane = lax.broadcasted_iota(jnp.int32, (total, 128), 1)
-    its_step = ((row // capacity) % steps == lane).astype(F32).astype(BF16)
-    count_ref[...] = jnp.dot(used.astype(BF16), its_step, preferred_element_type=F32)
-    total_ref[...] = jnp.broadcast_to(jnp.sum(used, axis=1, keepdims=True), total_ref.shape).astype(jnp.int32)
-    for copy in copies:
-        copy.wait()
-
-
-def hidden_body(x_ref, gate_ref, up_ref, gate_there_ref, up_there_ref, out_hbm, out_ref, sems):
-    parts, rows, piece = x_ref.shape
-    hid = gate_ref.shape[1]
-    gate = jnp.zeros((rows, 2 * hid), F32)
-    up = jnp.zeros((rows, 2 * hid), F32)
-    for i in range(parts):
-        at = slice(i * piece, (i + 1) * piece)
-        x = x_ref[i]
+    counted = jnp.where((row // capacity) % steps == lane, used, 0.0)
+    count_ref[...] = jnp.broadcast_to(jnp.sum(counted, axis=0, keepdims=True), count_ref.shape)
+    head = jnp.where(lane == 0, head * used, head).astype(BF16)
+    for i, out_ref in enumerate((first_ref, second_ref)):
+        at = slice(i * half, (i + 1) * half)
+        out_ref[:, :128] = head[at]
+        out_ref[:, 128:] = x_ref[at, 128:]
+
+
+def add_products(here_ref, weights, parts, gate, up):
+    gate_ref, up_ref, gate_there_ref, up_there_ref = weights
+    dp = 4
+    for distance, first_ref, second_ref in parts:
+        piece = first_ref.shape[1]
+        block = lax.rem(here_ref[0] + distance, dp)
+        at = pl.ds(pl.multiple_of(block * piece, piece), piece)
         gate_w = jnp.concatenate([gate_ref[at, :], gate_there_ref[at, :]], axis=1)
         up_w = jnp.concatenate([up_ref[at, :], up_there_ref[at, :]], axis=1)
-        gate += jnp.dot(x, gate_w, preferred_element_type=F32)
-        up += jnp.dot(x, up_w, preferred_element_type=F32)
+        x = jnp.concatenate([first_ref[...], second_ref[...]], axis=0)
+        gate_part = jnp.dot(x, gate_w, preferred_element_type=F32)
+        up_part = jnp.dot(x, up_w, preferred_element_type=F32)
+        gate = gate_part if gate is None else gate + gate_part
+        up = up_part if up is None else up + up_part
+    return gate, up
+
+
+def own_piece_body(here_ref, first_ref, second_ref, *refs):
+    weights, (gate_out, up_out) = refs[:4], refs[4:]
+    gate_out[...], up_out[...] = add_products(here_ref, weights, [(0, first_ref, second_ref)], None, None)
+
+
+def near_pieces_body(
+    here_ref, left_first, left_second, right_first, right_second, gate_in, up_in, *refs
+):
+    weights, (gate_out, up_out) = refs[:4], refs[4:]
+    parts = [(3, left_first, left_second), (1, right_first, right_second)]
+    gate_out[...], up_out[...] = add_products(here_ref, weights, parts, gate_in[...], up_in[...])
+
+
+def last_piece_body(here_ref, first_ref, second_ref, gate_in, up_in, *refs):
+    weights, (out_hbm, out_ref, sems) = refs[:4], refs[4:]
+    parts = [(2, first_ref, second_ref)]
+    gate, up = add_products(here_ref, weights, parts, gate_in[...], up_in[...])
     out_ref[...] = (gate / (1.0 + jnp.exp(-gate)) * up).astype(BF16)
-    copies = [pltpu.make_async_copy(out_ref, out_hbm.at[i], sems.at[i]) for i in range(parts)]
+    copies = [pltpu.make_async_copy(out_ref, out_hbm.at[i], sems.at[i]) for i in range(out_hbm.shape[0])]
     for copy in copies:
         copy.start()
     for copy in copies:
         copy.wait()
 
 
-def down_body(here_ref, hid_ref, pick_ref, own_ref, there_ref, out_hbm, out_ref, sems):
-    dp, rows, _ = hid_ref.shape
-    out = jnp.zeros((rows, own_ref.shape[2]), F32)
-    for d in range(dp):
-        block = lax.rem(here_ref[0] - d + dp, dp)
-        w = jnp.concatenate([own_ref[d], there_ref[d]], axis=0)
-        out += jnp.dot(hid_ref[block], w, preferred_element_type=F32)
-    out = out.astype(BF16)
-    total = out_ref.shape[0]
+def down_body(here_ref, hid_ref, own_ref, there_ref, out_hbm, out_ref, sems):
+    dp, total, _ = hid_ref.shape
     pieces = 2
     size = total // pieces
     copies = []
     for i in range(pieces):
         at = slice(i * size, (i + 1) * size)
-        spread = lax.dot_general(
-            pick_ref[:, at], out, (((0,), (0,)), ((), ())), preferred_element_type=F32
-        )
-        out_ref[at] = spread.astype(BF16)
+        out = jnp.zeros((size, own_ref.shape[2]), F32)
+        for d in range(dp):
+            block = lax.rem(here_ref[0] - d + dp, dp)
+            w = jnp.concatenate([own_ref[d], there_ref[d]], axis=0)
+            out += jnp.dot(hid_ref[block, at], w, preferred_element_type=F32)
+        out_ref[at] = out.astype(BF16)
         copy = pltpu.make_async_copy(out_ref.at[at], out_hbm.at[at], sems.at[i])
         copy.start()
         copies.append(copy)
@@ -220,7 +218,6 @@
     capacity = 2
     per_slot = steps * capacity
     count = slots * per_slot
-    kept = count // 2
     same_core = [list(range(c, ep, 2)) for c in range(2)]
     swap = [(e, e ^ 1) for e in range(ep)]
     shape = jax.ShapeDtypeStruct
@@ -271,48 +268,54 @@
         rows.reshape(slots, per_slot, piece), "ep", 0, 0, axis_index_groups=same_core
     ).reshape(count, piece)
 
-    def expert_rows(first, after):
-        held, pick, used, total = call(
-            functools.partial(select_body, steps, capacity, first),
-            [
-                shape((dp, kept, piece), BF16),
-                shape((kept, count), BF16),
-                shape((8, 128), F32),
-                shape((8, 128), jnp.int32),
-            ],
-            [arrived, *after],
-            2 * kept * count * piece,
-            in_specs=[ANY] * (1 + len(after)),
-            out_specs=[HBM, VMEM, VMEM, VMEM],
-            scratch=[
-                pltpu.VMEM((count, piece), BF16),
-                pltpu.VMEM((kept, piece), BF16),
-                pltpu.SemaphoreType.DMA((1 + dp,)),
-            ],
-        )
-        held = lax.all_to_all(held, "dp", 0, 0)
-        (hidden,) = call(
-            hidden_body,
-            [shape((dp, kept, 2 * hid), BF16)],
-            [held, gate, up, gate_there, up_there],
-            8 * kept * width * hid,
-            out_specs=[HBM],
-            scratch=[pltpu.VMEM((kept, 2 * hid), BF16), pltpu.SemaphoreType.DMA((dp,))],
-        )
-        hidden = lax.all_to_all(hidden, "dp", 0, 0)
-        (out,) = call(
-            down_body,
-            [shape((count, piece), BF16)],
-            [here_at, hidden, pick, down_own, down_there],
-            4 * kept * piece * dp * hid,
-            in_specs=[SMEM] + [VMEM] * 4,
-            out_specs=[HBM],
-            scratch=[pltpu.VMEM((count, piece), BF16), pltpu.SemaphoreType.DMA((2,))],
-        )
-        return out, used, total
-
-    out, used, total = expert_rows(0, [down_there, gate_there, up_there])
-    out = lax.cond(total[0, 0] > kept, lambda o: o + expert_rows(kept, [])[0], lambda o: o, out)
+    after = [down_there, gate_there, up_there]
+    half = shape((count // 2, piece), BF16)
+    first, second, used = call(
+        functools.partial(split_body, steps, capacity),
+        [half, half, shape((8, 128), F32)],
+        [arrived, *after],
+        in_specs=[VMEM] + [ANY] * len(after),
+    )
+    ahead = [(x, (x + 1) % dp) for x in range(dp)]
+    behind = [(x, (x - 1) % dp) for x in range(dp)]
+    left_first = lax.ppermute(first, "dp", ahead)
+    right_second = lax.ppermute(second, "dp", behind)
+    left_second = lax.ppermute(second, "dp", ahead)
+    right_first = lax.ppermute(first, "dp", behind)
+    far_first = lax.ppermute(left_first, "dp", ahead)
+    far_second = lax.ppermute(right_second, "dp", behind)
+    weights = [gate, up, gate_there, up_there]
+    sums = [shape((count, 2 * hid), F32)] * 2
+    flops = 4 * count * piece * 2 * hid
+    gate_sum, up_sum = call(
+        own_piece_body, sums, [here_at, first, second, *weights], flops, in_specs=[SMEM] + [VMEM] * 6
+    )
+    gate_sum, up_sum = call(
+        near_pieces_body,
+        sums,
+        [here_at, left_first, left_second, right_first, right_second, gate_sum, up_sum, *weights],
+        2 * flops,
+        in_specs=[SMEM] + [VMEM] * 10,
+    )
+    (hidden,) = call(
+        last_piece_body,
+        [shape((dp, count, 2 * hid), BF16)],
+        [here_at, far_first, far_second, gate_sum, up_sum, *weights],
+        flops,
+        in_specs=[SMEM] + [VMEM] * 8,
+        out_specs=[HBM],
+        scratch=[pltpu.VMEM((count, 2 * hid), BF16), pltpu.SemaphoreType.DMA((dp,))],
+    )
+    hidden = lax.all_to_all(hidden, "dp", 0, 0)
+    (out,) = call(
+        down_body,
+        [shape((count, piece), BF16)],
+        [here_at, hidden, down_own, down_there],
+        4 * count * piece * dp * hid,
+        in_specs=[SMEM] + [VMEM] * 3,
+        out_specs=[HBM],
+        scratch=[pltpu.VMEM((count, piece), BF16), pltpu.SemaphoreType.DMA((2,))],
+    )
     returned = lax.all_to_all(
         out.reshape(slots, per_slot, piece), "ep", 0, 0, axis_index_groups=same_core
     ).reshape(count, piece)

time: 192 us -> 165 us (0.86)
  starting transfers between devices: 98.4 us -> 73.3 us
  blocking collectives: 32.9 us -> 27 us
  waiting for transfers between devices: 42.3 us -> 46.7 us
    all_to_all x1, starting transfers between devices: 57.7 us -> 14.8 us  [local(): lax.all_to_all(out.reshape(slots, per_slot, piece), 'ep', 0, 0, axis_inde...]
    ppermute x0 -> x6, starting transfers between devices: none -> 21.1 us  [the longest x1 5.13 us: local(): right_first = lax.ppermute(first, 'dp', behind)]
    ppermute x0 -> x6, waiting for transfers between devices: none -> 9.89 us  [the longest x1 4.14 us: local(): far_first = lax.ppermute(left_first, 'dp', ahead)]
    all_to_all x1 -> x0, waiting for transfers between devices: 6.88 us -> none  [expert_rows(): hidden = lax.all_to_all(hidden, 'dp', 0, 0)]
    all_to_all x1, blocking collectives: 23.2 us -> 17.2 us  [local(): hidden = lax.all_to_all(hidden, 'dp', 0, 0)]
    all_to_all x1 -> x0, starting transfers between devices: 3.48 us -> none  [expert_rows(): hidden = lax.all_to_all(hidden, 'dp', 0, 0)]
    all_to_all x1, waiting for transfers between devices: 19.9 us -> 22.3 us  [local(): lax.all_to_all(out.reshape(slots, per_slot, piece), 'ep', 0, 0, axis_inde...]
    unnamed x15 -> x19, local copies, waits for them, and re-layouts: 1.57 us -> 3.69 us
  transfers between devices with their start and end apart: 11 -> 16, of which waited for: 8 -> 11; matrix products, arithmetic and copies ran while one was open for 1% -> 0% of each run, Pallas kernels for 0% -> 1%
where the time goes in v3:
time: 165 us; the launch traced here: 164 us
  starting transfers between devices  73.3 us (44%)
  waiting for transfers between devices  46.7 us (28%)
  blocking collectives  27 us (16%)
  Pallas kernels  12 us (7%)
  local copies, waits for them, and re-layouts  3.79 us (2%)
    all_to_all x1, waiting for transfers between devices, local(): lax.all_to_all(out.reshape(slots, per_slot, piece), 'ep', 0, 0, axis_inde...  22.3 us
    all_to_all x1, blocking collectives, local(): hidden = lax.all_to_all(hidden, 'dp', 0, 0)  17.2 us
    all_to_all x1, starting transfers between devices, local(): lax.all_to_all(rows.reshape(slots, per_slot, piece), 'ep', 0, 0, axis_ind...  16.9 us
    all_to_all x1, starting transfers between devices, local(): lax.all_to_all(out.reshape(slots, per_slot, piece), 'ep', 0, 0, axis_inde...  14.8 us
    pallas_call x8, Pallas kernels, call(): pl.pallas_call(body, out_shape=tuple((pltpu.HBM(o.shape, o.dtype) if spec...  12 us
    all_to_all x1, blocking collectives, local(): got = lax.all_to_all(send, 'dp', 0, 0)  9.75 us
    ppermute x3, starting transfers between devices, local(): lax.ppermute(block, 'dp', [(x, (x + d) % dp) for x in range(dp)])  8.97 us
    ppermute x1, starting transfers between devices, local(): right_first = lax.ppermute(first, 'dp', behind)  5.13 us
  transfers between devices with their start and end apart: 16, of which 11 were waited for; matrix products, arithmetic and copies ran while one was open for 0% of the time, Pallas kernels for 1%

profile of v3, /device:TPU:8, one launch (start us, length us, event | category | flops | bytes accessed | tf_op | source)
XLA Modules:
  0.0 164.3 jit_solution(12467465270469743840)
XLA Ops:
  0.6 2.0 %shard_map.95 = bf16[4,4,1024]{2,1,0:T(4,128)(2,1)} custom-call(bf16[4,3584]{1,0:T(4,128)(2,1)} %bitcast.39, bf16[4,8]{1,0:T(4,128)(2,1)} %bitcast.40, s32[4,1,8]{2,1,0:T(1,128)} %ids_hbm.1, s32[4,1,8]{2,1,0:T(1,128)} %replica_hbm.1, s32[2,56]{1,0:T(2,128)} %bitcast.41), custom_call_target="tpu_custom_call" | custom-call | bytes 62208 | tf_op jit(solution)/shard_map/pallas_call | solution.py:29
  2.7 9.8 %all_to_all.25 = bf16[4,4,1024]{2,1,0:T(4,128)(2,1)S(1)} all-to-all(bf16[4,4,1024]{2,1,0:T(4,128)(2,1)} %shard_map.95), channel_id=1, replica_groups=mesh['ep'=128,'dp'=4] {'dp'}, dimensions={0} | all-to-all | bytes 65536 | tf_op jit(solution)/shard_map/all_to_all | solution.py:248
  12.4 1.9 %shard_map.96 = (bf16[512,896]{1,0:T(8,128)(2,1)}, bf16[512,16]{1,0:T(8,128)(2,1)S(1)}) custom-call(bf16[16,1024]{1,0:T(8,128)(2,1)S(1)} %reshape.50.got_ref), custom_call_target="tpu_custom_call" | custom-call | bytes 966656 | tf_op jit(solution)/shard_map/pallas_call | solution.py:29
  14.3 16.9 %all-to-all-start.1 = ((bf16[64,8,896]{2,1,0:T(8,128)(2,1)}), bf16[64,8,896]{2,1,0:T(8,128)(2,1)}, u32[]{:S(2)}, u32[]{:S(2)}) async-start(bf16[64,8,896]{2,1,0:T(8,128)(2,1)} %bitcast.34), calls=%async_computation.1 | async-start | bytes 1835008 | tf_op jit(solution)/shard_map/all_to_all | solution.py:267
  31.4 3.2 %collective-permute-start.2 = (bf16[128,896]{1,0:T(8,128)(2,1)S(1)}, bf16[128,896]{1,0:T(8,128)(2,1)S(1)}, u32[]{:S(2)}, u32[]{:S(2)}) collective-permute-start(bf16[128,896]{1,0:T(8,128)(2,1)S(1)} %get-tuple-element.22), channel_id=1, source_target_pairs={{0,3},{1,0},{2,1},{3,2},{4,7},{5,4},{6,5},{7,6},{8,11},{9,8},{10,9... | collective-permute-start | bytes 688136 | tf_op jit(solution)/shard_map/ppermute | solution.py:256
  34.6 2.8 %collective-permute-start = (bf16[128,896]{1,0:T(8,128)(2,1)S(1)}, bf16[128,896]{1,0:T(8,128)(2,1)S(1)}, u32[]{:S(2)}, u32[]{:S(2)}) collective-permute-start(bf16[128,896]{1,0:T(8,128)(2,1)S(1)} %get-tuple-element.21), channel_id=1, source_target_pairs={{0,1},{1,2},{2,3},{3,0},{4,5},{5,6},{6,7},{7,4},{8,9},{9,10},{10,1... | collective-permute-start | bytes 688136 | tf_op jit(solution)/shard_map/ppermute | solution.py:256
  37.4 3.0 %collective-permute-start.1 = (bf16[128,896]{1,0:T(8,128)(2,1)S(1)}, bf16[128,896]{1,0:T(8,128)(2,1)S(1)}, u32[]{:S(2)}, u32[]{:S(2)}) collective-permute-start(bf16[128,896]{1,0:T(8,128)(2,1)S(1)} %get-tuple-element.23), channel_id=1, source_target_pairs={{0,2},{1,3},{2,0},{3,1},{4,6},{5,7},{6,4},{7,5},{8,10},{9,11},{10,... | collective-permute-start | bytes 688136 | tf_op jit(solution)/shard_map/ppermute | solution.py:256
  40.4 1.9 %collective-permute-start.4 = (bf16[3584,128]{1,0:T(8,128)(2,1)S(1)}, bf16[3584,128]{1,0:T(8,128)(2,1)S(1)}, u32[]{:S(2)}, u32[]{:S(2)}) collective-permute-start(bf16[3584,128]{1,0:T(8,128)(2,1)S(1)} %bitcast.24), channel_id=1, source_target_pairs={{0,4},{4,0},{8,12},{12,8},{16,20},{20,16},{24,28},{28,24},{32,36},... | collective-permute-start | bytes 2752520 | tf_op jit(solution)/shard_map/ppermute | solution.py:251
  42.3 2.4 %collective-permute-start.5 = (bf16[3584,128]{1,0:T(8,128)(2,1)S(1)}, bf16[3584,128]{1,0:T(8,128)(2,1)S(1)}, u32[]{:S(2)}, u32[]{:S(2)}) collective-permute-start(bf16[3584,128]{1,0:T(8,128)(2,1)S(1)} %bitcast.28), channel_id=1, source_target_pairs={{0,4},{4,0},{8,12},{12,8},{16,20},{20,16},{24,28},{28,24},{32,36},... | collective-permute-start | bytes 2752520 | tf_op jit(solution)/shard_map/ppermute | solution.py:252
  44.7 3.6 %collective-permute-done = bf16[128,896]{1,0:T(8,128)(2,1)S(1)} collective-permute-done((bf16[128,896]{1,0:T(8,128)(2,1)S(1)}, bf16[128,896]{1,0:T(8,128)(2,1)S(1)}, u32[]{:S(2)}, u32[]{:S(2)}) %collective-permute-start) | collective-permute-done | bytes 229408 | tf_op jit(solution)/shard_map/ppermute | solution.py:256
  48.4 1.9 %collective-permute-start.3 = (bf16[4,128,896]{2,1,0:T(8,128)(2,1)S(1)}, bf16[4,128,896]{2,1,0:T(8,128)(2,1)S(1)}, u32[]{:S(2)}, u32[]{:S(2)}) collective-permute-start(bf16[4,128,896]{2,1,0:T(8,128)(2,1)S(1)} %pad_maximum_fusion.own_ref), channel_id=1, source_target_pairs={{0,4},{4,0},{8,12},{12,8},{16,20},{20,16},{24,28},{28,24},{32,36},... | collective-permute-start | bytes 2752520 | tf_op jit(solution)/shard_map/ppermute | solution.py:258
  51.3 1.5 collective-permute-done.3.refs_0_.there_ref
  53.7 3.4 %all-to-all-done.1 = bf16[64,8,896]{2,1,0:T(8,128)(2,1)} async-done(((bf16[64,8,896]{2,1,0:T(8,128)(2,1)}), bf16[64,8,896]{2,1,0:T(8,128)(2,1)}, u32[]{:S(2)}, u32[]{:S(2)}) %all-to-all-start.1) | async-done | bytes 917536 | tf_op jit(solution)/shard_map/all_to_all | solution.py:267
  58.4 1.5 shard_map.97
  59.8 2.5 %collective-permute-start.6 = (bf16[256,896]{1,0:T(8,128)(2,1)S(1)}, bf16[256,896]{1,0:T(8,128)(2,1)S(1)}, u32[]{:S(2)}, u32[]{:S(2)}) collective-permute-start(bf16[256,896]{1,0:T(8,128)(2,1)S(1)} %get-tuple-element.13.first_ref), channel_id=1, source_target_pairs={{0,1},{1,2},{2,3},{3,0},{4,5},{5,6},{6,7},{7,4},{8,9},{9,10},{10,1... | collective-permute-start | bytes 1376264 | tf_op jit(solution)/shard_map/ppermute | solution.py:281
  62.3 4.6 %collective-permute-start.8 = (bf16[256,896]{1,0:T(8,128)(2,1)S(1)}, bf16[256,896]{1,0:T(8,128)(2,1)S(1)}, u32[]{:S(2)}, u32[]{:S(2)}) collective-permute-start(bf16[256,896]{1,0:T(8,128)(2,1)S(1)} %get-tuple-element.14.second_ref), channel_id=1, source_target_pairs={{0,3},{1,0},{2,1},{3,2},{4,7},{5,4},{6,5},{7,6},{8,11},{9,8},{10,9... | collective-permute-start | bytes 1376264 | tf_op jit(solution)/shard_map/ppermute | solution.py:282
  66.9 1.9 %collective-permute-start.10 = (bf16[256,896]{1,0:T(8,128)(2,1)S(1)}, bf16[256,896]{1,0:T(8,128)(2,1)S(1)}, u32[]{:S(2)}, u32[]{:S(2)}) collective-permute-start(bf16[256,896]{1,0:T(8,128)(2,1)S(1)} %get-tuple-element.14.second_ref), channel_id=1, source_target_pairs={{0,1},{1,2},{2,3},{3,0},{4,5},{5,6},{6,7},{7,4},{8,9},{9,10},{10,1... | collective-permute-start | bytes 1376264 | tf_op jit(solution)/shard_map/ppermute | solution.py:283
  68.8 5.1 %collective-permute-start.11 = (bf16[256,896]{1,0:T(8,128)(2,1)S(1)}, bf16[256,896]{1,0:T(8,128)(2,1)S(1)}, u32[]{:S(2)}, u32[]{:S(2)}) collective-permute-start(bf16[256,896]{1,0:T(8,128)(2,1)S(1)} %get-tuple-element.13.first_ref), channel_id=1, source_target_pairs={{0,3},{1,0},{2,1},{3,2},{4,7},{5,4},{6,5},{7,6},{8,11},{9,8},{10,9... | collective-permute-start | bytes 1376264 | tf_op jit(solution)/shard_map/ppermute | solution.py:284
  74.0 1.4 collective-permute-done.6.left_first
  75.3 1.9 %collective-permute-start.7 = (bf16[256,896]{1,0:T(8,128)(2,1)S(1)}, bf16[256,896]{1,0:T(8,128)(2,1)S(1)}, u32[]{:S(2)}, u32[]{:S(2)}) collective-permute-start(bf16[256,896]{1,0:T(8,128)(2,1)S(1)} %collective-permute-done.6.left_first), channel_id=1, source_target_pairs={{0,1},{1,2},{2,3},{3,0},{4,5},{5,6},{6,7},{7,4},{8,9},{9,10},{10,1... | collective-permute-start | bytes 1376264 | tf_op jit(solution)/shard_map/ppermute | solution.py:285
  77.2 5.1 %collective-permute-start.9 = (bf16[256,896]{1,0:T(8,128)(2,1)S(1)}, bf16[256,896]{1,0:T(8,128)(2,1)S(1)}, u32[]{:S(2)}, u32[]{:S(2)}) collective-permute-start(bf16[256,896]{1,0:T(8,128)(2,1)S(1)} %collective-permute-done.8.right_second), channel_id=1, source_target_pairs={{0,3},{1,0},{2,1},{3,2},{4,7},{5,4},{6,5},{7,6},{8,11},{9,8},{10,9... | collective-permute-start | bytes 1376264 | tf_op jit(solution)/shard_map/ppermute | solution.py:286
  83.1 2.0 %collective-permute-done.10.left_second = bf16[256,896]{1,0:T(8,128)(2,1)S(1)} collective-permute-done((bf16[256,896]{1,0:T(8,128)(2,1)S(1)}, bf16[256,896]{1,0:T(8,128)(2,1)S(1)}, u32[]{:S(2)}, u32[]{:S(2)}) %collective-permute-start.10) | collective-permute-done | bytes 458784 | tf_op jit(solution)/shard_map/ppermute | solution.py:283
  86.3 1.2 shard_map.99
  87.6 4.1 %collective-permute-done.7.first_ref = bf16[256,896]{1,0:T(8,128)(2,1)S(1)} collective-permute-done((bf16[256,896]{1,0:T(8,128)(2,1)S(1)}, bf16[256,896]{1,0:T(8,128)(2,1)S(1)}, u32[]{:S(2)}, u32[]{:S(2)}) %collective-permute-start.7) | collective-permute-done | bytes 458784 | tf_op jit(solution)/shard_map/ppermute | solution.py:285
  92.9 1.8 %shard_map.100 = bf16[4,512,256]{2,1,0:T(8,128)(2,1)} custom-call(s32[1]{0:T(128)} %bitcast.3.here_ref, bf16[256,896]{1,0:T(8,128)(2,1)S(1)} %collective-permute-done.7.first_ref, bf16[256,896]{1,0:T(8,128)(2,1)S(1)} %collective-permute-done.9.second_ref, f32[512,256]{1,0:T(8,128)S(1)} %get-tuple-element.17.gate_in, f32[512,256]{1,0:T(8,128)S(1)} %get-tuple-element.18.up_in, ...), custom_call_target="tpu_custom_call" | custom-call | flops 469762048 | bytes 6684676 | tf_op jit(solution)/shard_map/pallas_call | solution.py:29
  94.7 17.2 %all_to_all.26.hid_ref = bf16[4,512,256]{2,1,0:T(8,128)(2,1)S(1)} all-to-all(bf16[4,512,256]{2,1,0:T(8,128)(2,1)} %shard_map.100), channel_id=1, replica_groups=mesh['ep'=128,'dp'=4] {'dp'}, dimensions={0} | all-to-all | bytes 2097152 | tf_op jit(solution)/shard_map/all_to_all | solution.py:309
  111.9 2.1 %shard_map.101 = bf16[512,896]{1,0:T(8,128)(2,1)} custom-call(s32[1]{0:T(128)} %bitcast.3.here_ref, bf16[4,512,256]{2,1,0:T(8,128)(2,1)S(1)} %all_to_all.26.hid_ref, bf16[4,128,896]{2,1,0:T(8,128)(2,1)S(1)} %copy-done.7, bf16[4,128,896]{2,1,0:T(8,128)(2,1)S(1)} %copy-done.5), custom_call_target="tpu_custom_call" | custom-call | flops 939524096 | bytes 3801092 | tf_op jit(solution)/shard_map/pallas_call | solution.py:29
  114.0 14.8 %all-to-all-start.3 = ((bf16[64,8,896]{2,1,0:T(8,128)(2,1)}), bf16[64,8,896]{2,1,0:T(8,128)(2,1)S(1)}, u32[]{:S(2)}, u32[]{:S(2)}) async-start(bf16[64,8,896]{2,1,0:T(8,128)(2,1)} %bitcast.33), calls=%async_computation.3 | async-start | bytes 1835008 | tf_op jit(solution)/shard_map/all_to_all | solution.py:319
  128.8 1.9 %collective-permute-start.12 = (f32[8,128]{1,0:T(8,128)S(1)}, f32[8,128]{1,0:T(8,128)S(1)}, u32[]{:S(2)}, u32[]{:S(2)}) collective-permute-start(f32[8,128]{1,0:T(8,128)S(1)} %get-tuple-element.19), channel_id=1, source_target_pairs={{0,4},{4,0},{8,12},{12,8},{16,20},{20,16},{24,28},{28,24},{32,36},... | collective-permute-start | bytes 12296 | tf_op jit(solution)/shard_map/ppermute | solution.py:328
  131.9 22.3 %all-to-all-done.3 = bf16[64,8,896]{2,1,0:T(8,128)(2,1)S(1)} async-done(((bf16[64,8,896]{2,1,0:T(8,128)(2,1)}), bf16[64,8,896]{2,1,0:T(8,128)(2,1)S(1)}, u32[]{:S(2)}, u32[]{:S(2)}) %all-to-all-start.3) | async-done | bytes 917536 | tf_op jit(solution)/shard_map/all_to_all | solution.py:319
  155.1 3.3 %all-to-all-start.4 = ((bf16[4,4,896]{2,1,0:T(4,128)(2,1)}), bf16[4,4,896]{2,1,0:T(4,128)(2,1)S(1)}, u32[]{:S(2)}, u32[]{:S(2)}) async-start(bf16[4,4,896]{2,1,0:T(4,128)(2,1)} %shard_map.102), calls=%async_computation.4 | async-start | bytes 57344 | tf_op jit(solution)/shard_map/all_to_all | solution.py:325
  158.8 4.9 %all-to-all-done.4 = bf16[4,4,896]{2,1,0:T(4,128)(2,1)S(1)} async-done(((bf16[4,4,896]{2,1,0:T(4,128)(2,1)}), bf16[4,4,896]{2,1,0:T(4,128)(2,1)S(1)}, u32[]{:S(2)}, u32[]{:S(2)}) %all-to-all-start.4) | async-done | bytes 28704 | tf_op jit(solution)/shard_map/all_to_all | solution.py:325
  (34 shorter events, 9.5 us)
Async XLA Ops:
  14.3 16.9 %copy-start.8 = (bf16[1,128,3584]{2,1,0:T(8,128)(2,1)S(1)}, bf16[1,128,3584]{2,1,0:T(8,128)(2,1)}, u32[]{:S(2)}) copy-start(bf16[1,128,3584]{2,1,0:T(8,128)(2,1)} %param.15) | copy-start | bytes 2752516
  14.3 42.9 %all-to-all-start.1 = ((bf16[64,8,896]{2,1,0:T(8,128)(2,1)}), bf16[64,8,896]{2,1,0:T(8,128)(2,1)}, u32[]{:S(2)}, u32[]{:S(2)}) async-start(bf16[64,8,896]{2,1,0:T(8,128)(2,1)} %bitcast.34), calls=%async_computation.1 | async-start | bytes 1835008 | tf_op jit(solution)/shard_map/all_to_all | solution.py:267
  31.2 9.1 %copy-start = (bf16[1,3584,128]{2,1,0:T(8,128)(2,1)S(1)}, bf16[1,3584,128]{2,1,0:T(8,128)(2,1)}, u32[]{:S(2)}) copy-start(bf16[1,3584,128]{2,1,0:T(8,128)(2,1)} %param.13) | copy-start | bytes 2752516
  31.3 11.0 %copy-start.1 = (bf16[1,3584,128]{2,1,0:T(8,128)(2,1)S(1)}, bf16[1,3584,128]{2,1,0:T(8,128)(2,1)}, u32[]{:S(2)}) copy-start(bf16[1,3584,128]{2,1,0:T(8,128)(2,1)} %param.14) | copy-start | bytes 2752516
  31.4 13.4 %collective-permute-start.2 = (bf16[128,896]{1,0:T(8,128)(2,1)S(1)}, bf16[128,896]{1,0:T(8,128)(2,1)S(1)}, u32[]{:S(2)}, u32[]{:S(2)}) collective-permute-start(bf16[128,896]{1,0:T(8,128)(2,1)S(1)} %get-tuple-element.22), channel_id=1, source_target_pairs={{0,3},{1,0},{2,1},{3,2},{4,7},{5,4},{6,5},{7,6},{8,11},{9,8},{10,9... | collective-permute-start | bytes 688136 | tf_op jit(solution)/shard_map/ppermute | solution.py:256
  34.6 13.7 %collective-permute-start = (bf16[128,896]{1,0:T(8,128)(2,1)S(1)}, bf16[128,896]{1,0:T(8,128)(2,1)S(1)}, u32[]{:S(2)}, u32[]{:S(2)}) collective-permute-start(bf16[128,896]{1,0:T(8,128)(2,1)S(1)} %get-tuple-element.21), channel_id=1, source_target_pairs={{0,1},{1,2},{2,3},{3,0},{4,5},{5,6},{6,7},{7,4},{8,9},{9,10},{10,1... | collective-permute-start | bytes 688136 | tf_op jit(solution)/shard_map/ppermute | solution.py:256
  37.4 10.9 %collective-permute-start.1 = (bf16[128,896]{1,0:T(8,128)(2,1)S(1)}, bf16[128,896]{1,0:T(8,128)(2,1)S(1)}, u32[]{:S(2)}, u32[]{:S(2)}) collective-permute-start(bf16[128,896]{1,0:T(8,128)(2,1)S(1)} %get-tuple-element.23), channel_id=1, source_target_pairs={{0,2},{1,3},{2,0},{3,1},{4,6},{5,7},{6,4},{7,5},{8,10},{9,11},{10,... | collective-permute-start | bytes 688136 | tf_op jit(solution)/shard_map/ppermute | solution.py:256
  40.4 10.9 %collective-permute-start.4 = (bf16[3584,128]{1,0:T(8,128)(2,1)S(1)}, bf16[3584,128]{1,0:T(8,128)(2,1)S(1)}, u32[]{:S(2)}, u32[]{:S(2)}) collective-permute-start(bf16[3584,128]{1,0:T(8,128)(2,1)S(1)} %bitcast.24), channel_id=1, source_target_pairs={{0,4},{4,0},{8,12},{12,8},{16,20},{20,16},{24,28},{28,24},{32,36},... | collective-permute-start | bytes 2752520 | tf_op jit(solution)/shard_map/ppermute | solution.py:251
  42.3 9.0 %collective-permute-start.5 = (bf16[3584,128]{1,0:T(8,128)(2,1)S(1)}, bf16[3584,128]{1,0:T(8,128)(2,1)S(1)}, u32[]{:S(2)}, u32[]{:S(2)}) collective-permute-start(bf16[3584,128]{1,0:T(8,128)(2,1)S(1)} %bitcast.28), channel_id=1, source_target_pairs={{0,4},{4,0},{8,12},{12,8},{16,20},{20,16},{24,28},{28,24},{32,36},... | collective-permute-start | bytes 2752520 | tf_op jit(solution)/shard_map/ppermute | solution.py:252
  48.4 4.4 %collective-permute-start.3 = (bf16[4,128,896]{2,1,0:T(8,128)(2,1)S(1)}, bf16[4,128,896]{2,1,0:T(8,128)(2,1)S(1)}, u32[]{:S(2)}, u32[]{:S(2)}) collective-permute-start(bf16[4,128,896]{2,1,0:T(8,128)(2,1)S(1)} %pad_maximum_fusion.own_ref), channel_id=1, source_target_pairs={{0,4},{4,0},{8,12},{12,8},{16,20},{20,16},{24,28},{28,24},{32,36},... | collective-permute-start | bytes 2752520 | tf_op jit(solution)/shard_map/ppermute | solution.py:258
  50.4 0.9 copy-start.6
  52.8 0.9 copy-start.3
  57.2 1.2 copy-start.4
  58.4 24.0 %copy-start.2 = (bf16[1,3584,128]{2,1,0:T(8,128)(2,1)S(1)}, bf16[1,3584,128]{2,1,0:T(8,128)(2,1)}, u32[]{:S(2)}) copy-start(bf16[1,3584,128]{2,1,0:T(8,128)(2,1)} %param.14) | copy-start | bytes 2752516
  59.8 15.5 %collective-permute-start.6 = (bf16[256,896]{1,0:T(8,128)(2,1)S(1)}, bf16[256,896]{1,0:T(8,128)(2,1)S(1)}, u32[]{:S(2)}, u32[]{:S(2)}) collective-permute-start(bf16[256,896]{1,0:T(8,128)(2,1)S(1)} %get-tuple-element.13.first_ref), channel_id=1, source_target_pairs={{0,1},{1,2},{2,3},{3,0},{4,5},{5,6},{6,7},{7,4},{8,9},{9,10},{10,1... | collective-permute-start | bytes 1376264 | tf_op jit(solution)/shard_map/ppermute | solution.py:281
  62.3 14.9 %collective-permute-start.8 = (bf16[256,896]{1,0:T(8,128)(2,1)S(1)}, bf16[256,896]{1,0:T(8,128)(2,1)S(1)}, u32[]{:S(2)}, u32[]{:S(2)}) collective-permute-start(bf16[256,896]{1,0:T(8,128)(2,1)S(1)} %get-tuple-element.14.second_ref), channel_id=1, source_target_pairs={{0,3},{1,0},{2,1},{3,2},{4,7},{5,4},{6,5},{7,6},{8,11},{9,8},{10,9... | collective-permute-start | bytes 1376264 | tf_op jit(solution)/shard_map/ppermute | solution.py:282
  66.9 18.3 %collective-permute-start.10 = (bf16[256,896]{1,0:T(8,128)(2,1)S(1)}, bf16[256,896]{1,0:T(8,128)(2,1)S(1)}, u32[]{:S(2)}, u32[]{:S(2)}) collective-permute-start(bf16[256,896]{1,0:T(8,128)(2,1)S(1)} %get-tuple-element.14.second_ref), channel_id=1, source_target_pairs={{0,1},{1,2},{2,3},{3,0},{4,5},{5,6},{6,7},{7,4},{8,9},{9,10},{10,1... | collective-permute-start | bytes 1376264 | tf_op jit(solution)/shard_map/ppermute | solution.py:283
  68.8 17.5 %collective-permute-start.11 = (bf16[256,896]{1,0:T(8,128)(2,1)S(1)}, bf16[256,896]{1,0:T(8,128)(2,1)S(1)}, u32[]{:S(2)}, u32[]{:S(2)}) collective-permute-start(bf16[256,896]{1,0:T(8,128)(2,1)S(1)} %get-tuple-element.13.first_ref), channel_id=1, source_target_pairs={{0,3},{1,0},{2,1},{3,2},{4,7},{5,4},{6,5},{7,6},{8,11},{9,8},{10,9... | collective-permute-start | bytes 1376264 | tf_op jit(solution)/shard_map/ppermute | solution.py:284
  75.3 16.4 %collective-permute-start.7 = (bf16[256,896]{1,0:T(8,128)(2,1)S(1)}, bf16[256,896]{1,0:T(8,128)(2,1)S(1)}, u32[]{:S(2)}, u32[]{:S(2)}) collective-permute-start(bf16[256,896]{1,0:T(8,128)(2,1)S(1)} %collective-permute-done.6.left_first), channel_id=1, source_target_pairs={{0,1},{1,2},{2,3},{3,0},{4,5},{5,6},{6,7},{7,4},{8,9},{9,10},{10,1... | collective-permute-start | bytes 1376264 | tf_op jit(solution)/shard_map/ppermute | solution.py:285
  77.2 15.7 %collective-permute-start.9 = (bf16[256,896]{1,0:T(8,128)(2,1)S(1)}, bf16[256,896]{1,0:T(8,128)(2,1)S(1)}, u32[]{:S(2)}, u32[]{:S(2)}) collective-permute-start(bf16[256,896]{1,0:T(8,128)(2,1)S(1)} %collective-permute-done.8.right_second), channel_id=1, source_target_pairs={{0,3},{1,0},{2,1},{3,2},{4,7},{5,4},{6,5},{7,6},{8,11},{9,8},{10,9... | collective-permute-start | bytes 1376264 | tf_op jit(solution)/shard_map/ppermute | solution.py:286
  94.7 17.2 %copy-start.5 = (bf16[4,128,896]{2,1,0:T(8,128)(2,1)S(1)}, bf16[4,128,896]{2,1,0:T(8,128)(2,1)}, u32[]{:S(2)}) copy-start(bf16[4,128,896]{2,1,0:T(8,128)(2,1)} %copy-done.3) | copy-start | bytes 2752516
  94.7 17.2 %copy-start.7 = (bf16[4,128,896]{2,1,0:T(8,128)(2,1)S(1)}, bf16[4,128,896]{2,1,0:T(8,128)(2,1)}, u32[]{:S(2)}) copy-start(bf16[4,128,896]{2,1,0:T(8,128)(2,1)} %copy-done.6) | copy-start | bytes 2752516
  114.0 40.2 %all-to-all-start.3 = ((bf16[64,8,896]{2,1,0:T(8,128)(2,1)}), bf16[64,8,896]{2,1,0:T(8,128)(2,1)S(1)}, u32[]{:S(2)}, u32[]{:S(2)}) async-start(bf16[64,8,896]{2,1,0:T(8,128)(2,1)} %bitcast.33), calls=%async_computation.3 | async-start | bytes 1835008 | tf_op jit(solution)/shard_map/all_to_all | solution.py:319
  128.8 3.1 %collective-permute-start.12 = (f32[8,128]{1,0:T(8,128)S(1)}, f32[8,128]{1,0:T(8,128)S(1)}, u32[]{:S(2)}, u32[]{:S(2)}) collective-permute-start(f32[8,128]{1,0:T(8,128)S(1)} %get-tuple-element.19), channel_id=1, source_target_pairs={{0,4},{4,0},{8,12},{12,8},{16,20},{20,16},{24,28},{28,24},{32,36},... | collective-permute-start | bytes 12296 | tf_op jit(solution)/shard_map/ppermute | solution.py:328
  155.1 8.7 %all-to-all-start.4 = ((bf16[4,4,896]{2,1,0:T(4,128)(2,1)}), bf16[4,4,896]{2,1,0:T(4,128)(2,1)S(1)}, u32[]{:S(2)}, u32[]{:S(2)}) async-start(bf16[4,4,896]{2,1,0:T(4,128)(2,1)} %shard_map.102), calls=%async_computation.4 | async-start | bytes 57344 | tf_op jit(solution)/shard_map/all_to_all | solution.py:325

commit v4 on v3

--- a/solution.py
+++ b/solution.py
@@ -135,40 +135,67 @@
         out_ref[:, 128:] = x_ref[at, 128:]
 
 
-def add_products(here_ref, weights, parts, gate, up):
-    gate_ref, up_ref, gate_there_ref, up_there_ref = weights
-    dp = 4
-    for distance, first_ref, second_ref in parts:
-        piece = first_ref.shape[1]
-        block = lax.rem(here_ref[0] + distance, dp)
-        at = pl.ds(pl.multiple_of(block * piece, piece), piece)
-        gate_w = jnp.concatenate([gate_ref[at, :], gate_there_ref[at, :]], axis=1)
-        up_w = jnp.concatenate([up_ref[at, :], up_there_ref[at, :]], axis=1)
-        x = jnp.concatenate([first_ref[...], second_ref[...]], axis=0)
-        gate_part = jnp.dot(x, gate_w, preferred_element_type=F32)
-        up_part = jnp.dot(x, up_w, preferred_element_type=F32)
-        gate = gate_part if gate is None else gate + gate_part
-        up = up_part if up is None else up + up_part
+def load_piece(here_ref, distance, weights, w_ref, sems):
+    piece = w_ref.shape[1]
+    dp = weights[0].shape[0] // piece
+    block = lax.rem(here_ref[0] + distance, dp)
+    at = pl.ds(pl.multiple_of(block * piece, piece), piece)
+    loads = [pltpu.make_async_copy(w.at[at], w_ref.at[i], sems.at[i]) for i, w in enumerate(weights)]
+    for load in loads:
+        load.start()
+    return loads
+
+
+def beside(loads, w_ref):
+    for load in loads:
+        load.wait()
+    gate_w = jnp.concatenate([w_ref[0], w_ref[2]], axis=1)
+    up_w = jnp.concatenate([w_ref[1], w_ref[3]], axis=1)
+    return gate_w, up_w
+
+
+def products(first_ref, second_ref, gate_w, up_w):
+    x = jnp.concatenate([first_ref[...], second_ref[...]], axis=0)
+    gate = jnp.dot(x, gate_w, preferred_element_type=F32)
+    up = jnp.dot(x, up_w, preferred_element_type=F32)
     return gate, up
 
 
 def own_piece_body(here_ref, first_ref, second_ref, *refs):
-    weights, (gate_out, up_out) = refs[:4], refs[4:]
-    gate_out[...], up_out[...] = add_products(here_ref, weights, [(0, first_ref, second_ref)], None, None)
+    weights, (gate_out, up_out, w_ref, sems) = refs[:4], refs[4:]
+    loads = load_piece(here_ref, 0, weights, w_ref, sems)
+    gate_out[...], up_out[...] = products(first_ref, second_ref, *beside(loads, w_ref))
 
 
 def near_pieces_body(
     here_ref, left_first, left_second, right_first, right_second, gate_in, up_in, *refs
 ):
-    weights, (gate_out, up_out) = refs[:4], refs[4:]
-    parts = [(3, left_first, left_second), (1, right_first, right_second)]
-    gate_out[...], up_out[...] = add_products(here_ref, weights, parts, gate_in[...], up_in[...])
-
-
-def last_piece_body(here_ref, first_ref, second_ref, gate_in, up_in, *refs):
-    weights, (out_hbm, out_ref, sems) = refs[:4], refs[4:]
-    parts = [(2, first_ref, second_ref)]
-    gate, up = add_products(here_ref, weights, parts, gate_in[...], up_in[...])
+    weights, (own_hbm, there_hbm) = refs[:4], refs[4:6]
+    gate_out, up_out, far_out, down_out, w_ref, sems, down_sems = refs[6:]
+    dp, hid, _ = own_hbm.shape
+    down_loads = []
+    for d in range(dp):
+        for i, source in enumerate((own_hbm, there_hbm)):
+            to = down_out.at[d, pl.ds(i * hid, hid)]
+            down_loads.append(pltpu.make_async_copy(source.at[d], to, down_sems.at[d, i]))
+    loads = [load_piece(here_ref, d, weights, w_ref.at[i], sems.at[i]) for i, d in enumerate((3, 1, 2))]
+    for load in down_loads:
+        load.start()
+    gate, up = products(left_first, left_second, *beside(loads[0], w_ref.at[0]))
+    gate_out[...] = gate_in[...] + gate
+    up_out[...] = up_in[...] + up
+    gate, up = products(right_first, right_second, *beside(loads[1], w_ref.at[1]))
+    gate_out[...] += gate
+    up_out[...] += up
+    far_out[0], far_out[1] = beside(loads[2], w_ref.at[2])
+    for load in down_loads:
+        load.wait()
+
+
+def last_piece_body(first_ref, second_ref, gate_in, up_in, far_ref, out_hbm, out_ref, sems):
+    gate, up = products(first_ref, second_ref, far_ref[0], far_ref[1])
+    gate += gate_in[...]
+    up += up_in[...]
     out_ref[...] = (gate / (1.0 + jnp.exp(-gate)) * up).astype(BF16)
     copies = [pltpu.make_async_copy(out_ref, out_hbm.at[i], sems.at[i]) for i in range(out_hbm.shape[0])]
     for copy in copies:
@@ -177,18 +204,17 @@
         copy.wait()
 
 
-def down_body(here_ref, hid_ref, own_ref, there_ref, out_hbm, out_ref, sems):
+def down_body(here_ref, hid_ref, w_ref, out_hbm, out_ref, sems):
     dp, total, _ = hid_ref.shape
     pieces = 2
     size = total // pieces
     copies = []
     for i in range(pieces):
         at = slice(i * size, (i + 1) * size)
-        out = jnp.zeros((size, own_ref.shape[2]), F32)
+        out = jnp.zeros((size, out_ref.shape[1]), F32)
         for d in range(dp):
             block = lax.rem(here_ref[0] - d + dp, dp)
-            w = jnp.concatenate([own_ref[d], there_ref[d]], axis=0)
-            out += jnp.dot(hid_ref[block, at], w, preferred_element_type=F32)
+            out += jnp.dot(hid_ref[block, at], w_ref[d], preferred_element_type=F32)
         out_ref[at] = out.astype(BF16)
         copy = pltpu.make_async_copy(out_ref.at[at], out_hbm.at[at], sems.at[i])
         copy.start()
@@ -274,7 +300,7 @@
         functools.partial(split_body, steps, capacity),
         [half, half, shape((8, 128), F32)],
         [arrived, *after],
-        in_specs=[VMEM] + [ANY] * len(after),
+        in_specs=[VMEM, HBM, ANY, ANY],
     )
     ahead = [(x, (x + 1) % dp) for x in range(dp)]
     behind = [(x, (x - 1) % dp) for x in range(dp)]
@@ -288,21 +314,31 @@
     sums = [shape((count, 2 * hid), F32)] * 2
     flops = 4 * count * piece * 2 * hid
     gate_sum, up_sum = call(
-        own_piece_body, sums, [here_at, first, second, *weights], flops, in_specs=[SMEM] + [VMEM] * 6
-    )
-    gate_sum, up_sum = call(
+        own_piece_body,
+        sums,
+        [here_at, first, second, *weights],
+        flops,
+        in_specs=[SMEM, VMEM, VMEM] + [HBM] * 4,
+        scratch=[pltpu.VMEM((4, piece, hid), BF16), pltpu.SemaphoreType.DMA((4,))],
+    )
+    gate_sum, up_sum, far_weights, down_weights = call(
         near_pieces_body,
-        sums,
-        [here_at, left_first, left_second, right_first, right_second, gate_sum, up_sum, *weights],
+        [*sums, shape((2, piece, 2 * hid), BF16), shape((dp, 2 * hid, piece), BF16)],
+        [here_at, left_first, left_second, right_first, right_second, gate_sum, up_sum, *weights, down_own, down_there],
         2 * flops,
-        in_specs=[SMEM] + [VMEM] * 10,
+        in_specs=[SMEM] + [VMEM] * 6 + [HBM] * 6,
+        scratch=[
+            pltpu.VMEM((3, 4, piece, hid), BF16),
+            pltpu.SemaphoreType.DMA((3, 4)),
+            pltpu.SemaphoreType.DMA((dp, 2)),
+        ],
+        vmem=16,
     )
     (hidden,) = call(
         last_piece_body,
         [shape((dp, count, 2 * hid), BF16)],
-        [here_at, far_first, far_second, gate_sum, up_sum, *weights],
+        [far_first, far_second, gate_sum, up_sum, far_weights],
         flops,
-        in_specs=[SMEM] + [VMEM] * 8,
         out_specs=[HBM],
         scratch=[pltpu.VMEM((count, 2 * hid), BF16), pltpu.SemaphoreType.DMA((dp,))],
     )
@@ -310,9 +346,9 @@
     (out,) = call(
         down_body,
         [shape((count, piece), BF16)],
-        [here_at, hidden, down_own, down_there],
+        [here_at, hidden, down_weights],
         4 * count * piece * dp * hid,
-        in_specs=[SMEM] + [VMEM] * 3,
+        in_specs=[SMEM, VMEM, VMEM],
         out_specs=[HBM],
         scratch=[pltpu.VMEM((count, piece), BF16), pltpu.SemaphoreType.DMA((2,))],
     )

time: 165 us -> 161 us (0.976)
  local copies, waits for them, and re-layouts: 3.79 us -> 0.73 us
  Pallas kernels: 12 us -> 13.8 us
  waiting for transfers between devices: 46.7 us -> 45 us
    unnamed x19 -> x9, local copies, waits for them, and re-layouts: 3.69 us -> 0.63 us
    ppermute x1, waiting for transfers between devices: 4.14 us -> 1.33 us  [local(): far_first = lax.ppermute(left_first, 'dp', ahead)]
    pallas_call x8, Pallas kernels: 12 us -> 13.8 us  [call(): pl.pallas_call(body, out_shape=tuple((pltpu.HBM(o.shape, o.dtype) if spec...]
  transfers between devices with their start and end apart: 16 -> 16, of which waited for: 11 -> 11; matrix products, arithmetic and copies ran while one was open for 0% -> 0% of each run, Pallas kernels for 1% -> 3%
where the time goes in v4:
time: 161 us
  starting transfers between devices  73.2 us (45%)
  waiting for transfers between devices  45 us (28%)
  blocking collectives  26.1 us (16%)
  Pallas kernels  13.8 us (9%)
    all_to_all x1, waiting for transfers between devices, local(): lax.all_to_all(out.reshape(slots, per_slot, piece), 'ep', 0, 0, axis_inde...  22.3 us
    all_to_all x1, starting transfers between devices, local(): lax.all_to_all(rows.reshape(slots, per_slot, piece), 'ep', 0, 0, axis_ind...  16.6 us
    all_to_all x1, blocking collectives, local(): hidden = lax.all_to_all(hidden, 'dp', 0, 0)  16.4 us
    all_to_all x1, starting transfers between devices, local(): lax.all_to_all(out.reshape(slots, per_slot, piece), 'ep', 0, 0, axis_inde...  14.9 us
    pallas_call x8, Pallas kernels, call(): pl.pallas_call(body, out_shape=tuple((pltpu.HBM(o.shape, o.dtype) if spec...  13.8 us
    all_to_all x1, blocking collectives, local(): got = lax.all_to_all(send, 'dp', 0, 0)  9.75 us
    ppermute x3, starting transfers between devices, local(): lax.ppermute(block, 'dp', [(x, (x + d) % dp) for x in range(dp)])  8.83 us
    ppermute x1, starting transfers between devices, local(): far_second = lax.ppermute(right_second, 'dp', behind)  5.44 us
  transfers between devices with their start and end apart: 16, of which 11 were waited for; matrix products, arithmetic and copies ran while one was open for 0% of the time, Pallas kernels for 3%

profile of v4, /device:TPU:8, one launch (start us, length us, event | category | flops | bytes accessed | tf_op | source)
XLA Modules:
  0.0 160.6 jit_solution(10332450204722507265)
XLA Ops:
  0.6 2.1 %shard_map.95 = bf16[4,4,1024]{2,1,0:T(4,128)(2,1)} custom-call(bf16[4,3584]{1,0:T(4,128)(2,1)} %bitcast.35, bf16[4,8]{1,0:T(4,128)(2,1)} %bitcast.36, s32[4,1,8]{2,1,0:T(1,128)} %ids_hbm.1, s32[4,1,8]{2,1,0:T(1,128)} %replica_hbm.1, s32[2,56]{1,0:T(2,128)} %bitcast.37), custom_call_target="tpu_custom_call" | custom-call | bytes 62208 | tf_op jit(solution)/shard_map/pallas_call | solution.py:29
  2.7 9.8 %all_to_all.25 = bf16[4,4,1024]{2,1,0:T(4,128)(2,1)S(1)} all-to-all(bf16[4,4,1024]{2,1,0:T(4,128)(2,1)} %shard_map.95), channel_id=1, replica_groups=mesh['ep'=128,'dp'=4] {'dp'}, dimensions={0} | all-to-all | bytes 65536 | tf_op jit(solution)/shard_map/all_to_all | solution.py:274
  12.5 1.9 %shard_map.96 = (bf16[512,896]{1,0:T(8,128)(2,1)}, bf16[512,16]{1,0:T(8,128)(2,1)S(1)}) custom-call(bf16[16,1024]{1,0:T(8,128)(2,1)S(1)} %reshape.50.got_ref), custom_call_target="tpu_custom_call" | custom-call | bytes 966656 | tf_op jit(solution)/shard_map/pallas_call | solution.py:29
  14.4 16.6 %all-to-all-start.1 = ((bf16[64,8,896]{2,1,0:T(8,128)(2,1)}), bf16[64,8,896]{2,1,0:T(8,128)(2,1)S(1)}, u32[]{:S(2)}, u32[]{:S(2)}) async-start(bf16[64,8,896]{2,1,0:T(8,128)(2,1)} %bitcast.30), calls=%async_computation.1 | async-start | bytes 1835008 | tf_op jit(solution)/shard_map/all_to_all | solution.py:293
  31.1 3.1 %collective-permute-start.2 = (bf16[128,896]{1,0:T(8,128)(2,1)S(1)}, bf16[128,896]{1,0:T(8,128)(2,1)S(1)}, u32[]{:S(2)}, u32[]{:S(2)}) collective-permute-start(bf16[128,896]{1,0:T(8,128)(2,1)S(1)} %get-tuple-element.26), channel_id=1, source_target_pairs={{0,3},{1,0},{2,1},{3,2},{4,7},{5,4},{6,5},{7,6},{8,11},{9,8},{10,9... | collective-permute-start | bytes 688136 | tf_op jit(solution)/shard_map/ppermute | solution.py:282
  34.2 2.8 %collective-permute-start = (bf16[128,896]{1,0:T(8,128)(2,1)S(1)}, bf16[128,896]{1,0:T(8,128)(2,1)S(1)}, u32[]{:S(2)}, u32[]{:S(2)}) collective-permute-start(bf16[128,896]{1,0:T(8,128)(2,1)S(1)} %get-tuple-element.25), channel_id=1, source_target_pairs={{0,1},{1,2},{2,3},{3,0},{4,5},{5,6},{6,7},{7,4},{8,9},{9,10},{10,1... | collective-permute-start | bytes 688136 | tf_op jit(solution)/shard_map/ppermute | solution.py:282
  37.0 3.0 %collective-permute-start.1 = (bf16[128,896]{1,0:T(8,128)(2,1)S(1)}, bf16[128,896]{1,0:T(8,128)(2,1)S(1)}, u32[]{:S(2)}, u32[]{:S(2)}) collective-permute-start(bf16[128,896]{1,0:T(8,128)(2,1)S(1)} %get-tuple-element.27), channel_id=1, source_target_pairs={{0,2},{1,3},{2,0},{3,1},{4,6},{5,7},{6,4},{7,5},{8,10},{9,11},{10,... | collective-permute-start | bytes 688136 | tf_op jit(solution)/shard_map/ppermute | solution.py:282
  40.0 1.9 %collective-permute-start.4 = (bf16[3584,128]{1,0:T(8,128)(2,1)}, bf16[3584,128]{1,0:T(8,128)(2,1)S(1)}, u32[]{:S(2)}, u32[]{:S(2)}) collective-permute-start(bf16[3584,128]{1,0:T(8,128)(2,1)} %bitcast.12.refs_0_), channel_id=1, source_target_pairs={{0,4},{4,0},{8,12},{12,8},{16,20},{20,16},{24,28},{28,24},{32,36},... | collective-permute-start | bytes 2752520 | tf_op jit(solution)/shard_map/ppermute | solution.py:277
  41.9 2.4 %collective-permute-start.5 = (bf16[3584,128]{1,0:T(8,128)(2,1)}, bf16[3584,128]{1,0:T(8,128)(2,1)S(1)}, u32[]{:S(2)}, u32[]{:S(2)}) collective-permute-start(bf16[3584,128]{1,0:T(8,128)(2,1)} %bitcast.26), channel_id=1, source_target_pairs={{0,4},{4,0},{8,12},{12,8},{16,20},{20,16},{24,28},{28,24},{32,36},... | collective-permute-start | bytes 2752520 | tf_op jit(solution)/shard_map/ppermute | solution.py:278
  44.3 3.6 %collective-permute-done = bf16[128,896]{1,0:T(8,128)(2,1)S(1)} collective-permute-done((bf16[128,896]{1,0:T(8,128)(2,1)S(1)}, bf16[128,896]{1,0:T(8,128)(2,1)S(1)}, u32[]{:S(2)}, u32[]{:S(2)}) %collective-permute-start) | collective-permute-done | bytes 229408 | tf_op jit(solution)/shard_map/ppermute | solution.py:282
  48.1 1.9 %collective-permute-start.3 = (bf16[4,128,896]{2,1,0:T(8,128)(2,1)S(1)}, bf16[4,128,896]{2,1,0:T(8,128)(2,1)}, u32[]{:S(2)}, u32[]{:S(2)}) collective-permute-start(bf16[4,128,896]{2,1,0:T(8,128)(2,1)S(1)} %pad_maximum_fusion.refs_4_), channel_id=1, source_target_pairs={{0,4},{4,0},{8,12},{12,8},{16,20},{20,16},{24,28},{28,24},{32,36},... | collective-permute-start | bytes 2752520 | tf_op jit(solution)/shard_map/ppermute | solution.py:284
  50.0 2.5 %collective-permute-done.3.refs_0_.refs_5_ = bf16[4,128,896]{2,1,0:T(8,128)(2,1)} collective-permute-done((bf16[4,128,896]{2,1,0:T(8,128)(2,1)S(1)}, bf16[4,128,896]{2,1,0:T(8,128)(2,1)}, u32[]{:S(2)}, u32[]{:S(2)}) %collective-permute-start.3) | collective-permute-done | bytes 917536 | tf_op jit(solution)/shard_map/ppermute | solution.py:284
  52.6 4.4 %all-to-all-done.1 = bf16[64,8,896]{2,1,0:T(8,128)(2,1)S(1)} async-done(((bf16[64,8,896]{2,1,0:T(8,128)(2,1)}), bf16[64,8,896]{2,1,0:T(8,128)(2,1)S(1)}, u32[]{:S(2)}, u32[]{:S(2)}) %all-to-all-start.1) | async-done | bytes 917536 | tf_op jit(solution)/shard_map/all_to_all | solution.py:293
  57.2 2.5 %collective-permute-start.6 = (bf16[256,896]{1,0:T(8,128)(2,1)S(1)}, bf16[256,896]{1,0:T(8,128)(2,1)S(1)}, u32[]{:S(2)}, u32[]{:S(2)}) collective-permute-start(bf16[256,896]{1,0:T(8,128)(2,1)S(1)} %get-tuple-element.15.first_ref), channel_id=1, source_target_pairs={{0,1},{1,2},{2,3},{3,0},{4,5},{5,6},{6,7},{7,4},{8,9},{9,10},{10,1... | collective-permute-start | bytes 1376264 | tf_op jit(solution)/shard_map/ppermute | solution.py:307
  59.7 4.6 %collective-permute-start.8 = (bf16[256,896]{1,0:T(8,128)(2,1)S(1)}, bf16[256,896]{1,0:T(8,128)(2,1)S(1)}, u32[]{:S(2)}, u32[]{:S(2)}) collective-permute-start(bf16[256,896]{1,0:T(8,128)(2,1)S(1)} %get-tuple-element.16.second_ref), channel_id=1, source_target_pairs={{0,3},{1,0},{2,1},{3,2},{4,7},{5,4},{6,5},{7,6},{8,11},{9,8},{10,9... | collective-permute-start | bytes 1376264 | tf_op jit(solution)/shard_map/ppermute | solution.py:308
  64.3 1.9 %collective-permute-start.10 = (bf16[256,896]{1,0:T(8,128)(2,1)S(1)}, bf16[256,896]{1,0:T(8,128)(2,1)S(1)}, u32[]{:S(2)}, u32[]{:S(2)}) collective-permute-start(bf16[256,896]{1,0:T(8,128)(2,1)S(1)} %get-tuple-element.16.second_ref), channel_id=1, source_target_pairs={{0,1},{1,2},{2,3},{3,0},{4,5},{5,6},{6,7},{7,4},{8,9},{9,10},{10,1... | collective-permute-start | bytes 1376264 | tf_op jit(solution)/shard_map/ppermute | solution.py:309
  66.2 5.1 %collective-permute-start.11 = (bf16[256,896]{1,0:T(8,128)(2,1)S(1)}, bf16[256,896]{1,0:T(8,128)(2,1)S(1)}, u32[]{:S(2)}, u32[]{:S(2)}) collective-permute-start(bf16[256,896]{1,0:T(8,128)(2,1)S(1)} %get-tuple-element.15.first_ref), channel_id=1, source_target_pairs={{0,3},{1,0},{2,1},{3,2},{4,7},{5,4},{6,5},{7,6},{8,11},{9,8},{10,9... | collective-permute-start | bytes 1376264 | tf_op jit(solution)/shard_map/ppermute | solution.py:310
  72.4 1.9 %collective-permute-start.7 = (bf16[256,896]{1,0:T(8,128)(2,1)S(1)}, bf16[256,896]{1,0:T(8,128)(2,1)S(1)}, u32[]{:S(2)}, u32[]{:S(2)}) collective-permute-start(bf16[256,896]{1,0:T(8,128)(2,1)S(1)} %collective-permute-done.6.left_first), channel_id=1, source_target_pairs={{0,1},{1,2},{2,3},{3,0},{4,5},{5,6},{6,7},{7,4},{8,9},{9,10},{10,1... | collective-permute-start | bytes 1376264 | tf_op jit(solution)/shard_map/ppermute | solution.py:311
  74.3 5.4 %collective-permute-start.9 = (bf16[256,896]{1,0:T(8,128)(2,1)S(1)}, bf16[256,896]{1,0:T(8,128)(2,1)S(1)}, u32[]{:S(2)}, u32[]{:S(2)}) collective-permute-start(bf16[256,896]{1,0:T(8,128)(2,1)S(1)} %collective-permute-done.8.right_second), channel_id=1, source_target_pairs={{0,3},{1,0},{2,1},{3,2},{4,7},{5,4},{6,5},{7,6},{8,11},{9,8},{10,9... | collective-permute-start | bytes 1376264 | tf_op jit(solution)/shard_map/ppermute | solution.py:312
  79.8 2.0 %shard_map.98 = (f32[512,256]{1,0:T(8,128)S(1)}, f32[512,256]{1,0:T(8,128)S(1)}) custom-call(s32[1]{0:T(128)} %bitcast.3.here_ref, bf16[256,896]{1,0:T(8,128)(2,1)S(1)} %get-tuple-element.15.first_ref, bf16[256,896]{1,0:T(8,128)(2,1)S(1)} %get-tuple-element.16.second_ref, bf16[3584,128]{1,0:T(8,128)(2,1)} %bitcast.12.refs_0_, bf16[3584,128]{1,0:T(8,128)(2,1)} %bitcast.27, ...), custom_call_target="tpu_custom_call" | custom-call | flops 469762048 | bytes 5636100 | tf_op jit(solution)/shard_map/pallas_call | solution.py:29
  82.2 1.9 %collective-permute-done.11.right_first = bf16[256,896]{1,0:T(8,128)(2,1)S(1)} collective-permute-done((bf16[256,896]{1,0:T(8,128)(2,1)S(1)}, bf16[256,896]{1,0:T(8,128)(2,1)S(1)}, u32[]{:S(2)}, u32[]{:S(2)}) %collective-permute-start.11) | collective-permute-done | bytes 458784 | tf_op jit(solution)/shard_map/ppermute | solution.py:310
  84.1 3.0 %shard_map.99 = (f32[512,256]{1,0:T(8,128)S(1)}, f32[512,256]{1,0:T(8,128)S(1)}, bf16[2,896,256]{2,1,0:T(8,128)(2,1)S(1)}, bf16[4,256,896]{2,1,0:T(8,128)(2,1)S(1)}) custom-call(s32[1]{0:T(128)} %bitcast.3.here_ref, bf16[256,896]{1,0:T(8,128)(2,1)S(1)} %collective-permute-done.6.left_first, bf16[256,896]{1,0:T(8,128)(2,1)S(1)} %collective-permute-done.10.left_second, ...), custom_call_target="tpu_custom_call" | custom-call | flops 939524096 | bytes 12189700 | tf_op jit(solution)/shard_map/pallas_call | solution.py:29
  87.1 1.3 collective-permute-done.7.first_ref
  88.4 1.5 collective-permute-done.9.second_ref
  89.9 1.8 %shard_map.100 = bf16[4,512,256]{2,1,0:T(8,128)(2,1)} custom-call(bf16[256,896]{1,0:T(8,128)(2,1)S(1)} %collective-permute-done.7.first_ref, bf16[256,896]{1,0:T(8,128)(2,1)S(1)} %collective-permute-done.9.second_ref, f32[512,256]{1,0:T(8,128)S(1)} %get-tuple-element.19.gate_in, f32[512,256]{1,0:T(8,128)S(1)} %get-tuple-element.20.up_in, ...), custom_call_target="tpu_custom_call" | custom-call | flops 469762048 | bytes 3932160 | tf_op jit(solution)/shard_map/pallas_call | solution.py:29
  91.7 16.4 %all_to_all.26.hid_ref = bf16[4,512,256]{2,1,0:T(8,128)(2,1)S(1)} all-to-all(bf16[4,512,256]{2,1,0:T(8,128)(2,1)} %shard_map.100), channel_id=1, replica_groups=mesh['ep'=128,'dp'=4] {'dp'}, dimensions={0} | all-to-all | bytes 2097152 | tf_op jit(solution)/shard_map/all_to_all | solution.py:345
  108.1 2.1 %shard_map.101 = bf16[512,896]{1,0:T(8,128)(2,1)} custom-call(s32[1]{0:T(128)} %bitcast.3.here_ref, bf16[4,512,256]{2,1,0:T(8,128)(2,1)S(1)} %all_to_all.26.hid_ref, bf16[4,256,896]{2,1,0:T(8,128)(2,1)S(1)} %get-tuple-element.22.w_ref), custom_call_target="tpu_custom_call" | custom-call | flops 939524096 | bytes 3801092 | tf_op jit(solution)/shard_map/pallas_call | solution.py:29
  110.1 14.9 %all-to-all-start.3 = ((bf16[64,8,896]{2,1,0:T(8,128)(2,1)}), bf16[64,8,896]{2,1,0:T(8,128)(2,1)S(1)}, u32[]{:S(2)}, u32[]{:S(2)}) async-start(bf16[64,8,896]{2,1,0:T(8,128)(2,1)} %bitcast.29), calls=%async_computation.3 | async-start | bytes 1835008 | tf_op jit(solution)/shard_map/all_to_all | solution.py:355
  125.1 1.9 %collective-permute-start.12 = (f32[8,128]{1,0:T(8,128)S(1)}, f32[8,128]{1,0:T(8,128)S(1)}, u32[]{:S(2)}, u32[]{:S(2)}) collective-permute-start(f32[8,128]{1,0:T(8,128)S(1)} %get-tuple-element.23), channel_id=1, source_target_pairs={{0,4},{4,0},{8,12},{12,8},{16,20},{20,16},{24,28},{28,24},{32,36},... | collective-permute-start | bytes 12296 | tf_op jit(solution)/shard_map/ppermute | solution.py:364
  128.1 22.3 %all-to-all-done.3 = bf16[64,8,896]{2,1,0:T(8,128)(2,1)S(1)} async-done(((bf16[64,8,896]{2,1,0:T(8,128)(2,1)}), bf16[64,8,896]{2,1,0:T(8,128)(2,1)S(1)}, u32[]{:S(2)}, u32[]{:S(2)}) %all-to-all-start.3) | async-done | bytes 917536 | tf_op jit(solution)/shard_map/all_to_all | solution.py:355
  151.3 3.3 %all-to-all-start.4 = ((bf16[4,4,896]{2,1,0:T(4,128)(2,1)}), bf16[4,4,896]{2,1,0:T(4,128)(2,1)S(1)}, u32[]{:S(2)}, u32[]{:S(2)}) async-start(bf16[4,4,896]{2,1,0:T(4,128)(2,1)} %shard_map.102), calls=%async_computation.4 | async-start | bytes 57344 | tf_op jit(solution)/shard_map/all_to_all | solution.py:361
  155.1 4.9 %all-to-all-done.4 = bf16[4,4,896]{2,1,0:T(4,128)(2,1)S(1)} async-done(((bf16[4,4,896]{2,1,0:T(4,128)(2,1)}), bf16[4,4,896]{2,1,0:T(4,128)(2,1)S(1)}, u32[]{:S(2)}, u32[]{:S(2)}) %all-to-all-start.4) | async-done | bytes 28704 | tf_op jit(solution)/shard_map/all_to_all | solution.py:361
  (24 shorter events, 5.1 us)
Async XLA Ops:
  0.6 30.4 %copy-start.3 = (bf16[1,128,3584]{2,1,0:T(8,128)(2,1)S(1)}, bf16[1,128,3584]{2,1,0:T(8,128)(2,1)}, u32[]{:S(2)}) copy-start(bf16[1,128,3584]{2,1,0:T(8,128)(2,1)} %param.15) | copy-start | bytes 2752516
  14.4 42.6 %all-to-all-start.1 = ((bf16[64,8,896]{2,1,0:T(8,128)(2,1)}), bf16[64,8,896]{2,1,0:T(8,128)(2,1)S(1)}, u32[]{:S(2)}, u32[]{:S(2)}) async-start(bf16[64,8,896]{2,1,0:T(8,128)(2,1)} %bitcast.30), calls=%async_computation.1 | async-start | bytes 1835008 | tf_op jit(solution)/shard_map/all_to_all | solution.py:293
  31.1 13.2 %collective-permute-start.2 = (bf16[128,896]{1,0:T(8,128)(2,1)S(1)}, bf16[128,896]{1,0:T(8,128)(2,1)S(1)}, u32[]{:S(2)}, u32[]{:S(2)}) collective-permute-start(bf16[128,896]{1,0:T(8,128)(2,1)S(1)} %get-tuple-element.26), channel_id=1, source_target_pairs={{0,3},{1,0},{2,1},{3,2},{4,7},{5,4},{6,5},{7,6},{8,11},{9,8},{10,9... | collective-permute-start | bytes 688136 | tf_op jit(solution)/shard_map/ppermute | solution.py:282
  34.2 13.7 %collective-permute-start = (bf16[128,896]{1,0:T(8,128)(2,1)S(1)}, bf16[128,896]{1,0:T(8,128)(2,1)S(1)}, u32[]{:S(2)}, u32[]{:S(2)}) collective-permute-start(bf16[128,896]{1,0:T(8,128)(2,1)S(1)} %get-tuple-element.25), channel_id=1, source_target_pairs={{0,1},{1,2},{2,3},{3,0},{4,5},{5,6},{6,7},{7,4},{8,9},{9,10},{10,1... | collective-permute-start | bytes 688136 | tf_op jit(solution)/shard_map/ppermute | solution.py:282
  37.0 10.9 %collective-permute-start.1 = (bf16[128,896]{1,0:T(8,128)(2,1)S(1)}, bf16[128,896]{1,0:T(8,128)(2,1)S(1)}, u32[]{:S(2)}, u32[]{:S(2)}) collective-permute-start(bf16[128,896]{1,0:T(8,128)(2,1)S(1)} %get-tuple-element.27), channel_id=1, source_target_pairs={{0,2},{1,3},{2,0},{3,1},{4,6},{5,7},{6,4},{7,5},{8,10},{9,11},{10,... | collective-permute-start | bytes 688136 | tf_op jit(solution)/shard_map/ppermute | solution.py:282
  40.0 10.0 %collective-permute-start.4 = (bf16[3584,128]{1,0:T(8,128)(2,1)}, bf16[3584,128]{1,0:T(8,128)(2,1)S(1)}, u32[]{:S(2)}, u32[]{:S(2)}) collective-permute-start(bf16[3584,128]{1,0:T(8,128)(2,1)} %bitcast.12.refs_0_), channel_id=1, source_target_pairs={{0,4},{4,0},{8,12},{12,8},{16,20},{20,16},{24,28},{28,24},{32,36},... | collective-permute-start | bytes 2752520 | tf_op jit(solution)/shard_map/ppermute | solution.py:277
  41.9 8.1 %collective-permute-start.5 = (bf16[3584,128]{1,0:T(8,128)(2,1)}, bf16[3584,128]{1,0:T(8,128)(2,1)S(1)}, u32[]{:S(2)}, u32[]{:S(2)}) collective-permute-start(bf16[3584,128]{1,0:T(8,128)(2,1)} %bitcast.26), channel_id=1, source_target_pairs={{0,4},{4,0},{8,12},{12,8},{16,20},{20,16},{24,28},{28,24},{32,36},... | collective-permute-start | bytes 2752520 | tf_op jit(solution)/shard_map/ppermute | solution.py:278
  48.1 2.0 %copy-start.2 = (bf16[4,128,896]{2,1,0:T(8,128)(2,1)}, bf16[4,128,896]{2,1,0:T(8,128)(2,1)S(1)}, u32[]{:S(2)}) copy-start(bf16[4,128,896]{2,1,0:T(8,128)(2,1)S(1)} %pad_maximum_fusion.refs_4_) | copy-start | bytes 2752516
  48.1 4.5 %collective-permute-start.3 = (bf16[4,128,896]{2,1,0:T(8,128)(2,1)S(1)}, bf16[4,128,896]{2,1,0:T(8,128)(2,1)}, u32[]{:S(2)}, u32[]{:S(2)}) collective-permute-start(bf16[4,128,896]{2,1,0:T(8,128)(2,1)S(1)} %pad_maximum_fusion.refs_4_), channel_id=1, source_target_pairs={{0,4},{4,0},{8,12},{12,8},{16,20},{20,16},{24,28},{28,24},{32,36},... | collective-permute-start | bytes 2752520 | tf_op jit(solution)/shard_map/ppermute | solution.py:284
  50.0 7.2 %copy-start = (bf16[3584,128]{1,0:T(8,128)(2,1)}, bf16[3584,128]{1,0:T(8,128)(2,1)S(1)}, u32[]{:S(2)}) copy-start(bf16[3584,128]{1,0:T(8,128)(2,1)S(1)} %collective-permute-done.4.refs_1_.refs_2_) | copy-start | bytes 2752516
  50.0 7.1 %copy-start.1 = (bf16[3584,128]{1,0:T(8,128)(2,1)}, bf16[3584,128]{1,0:T(8,128)(2,1)S(1)}, u32[]{:S(2)}) copy-start(bf16[3584,128]{1,0:T(8,128)(2,1)S(1)} %collective-permute-done.5.refs_2_.refs_3_) | copy-start | bytes 2752516
  57.2 15.2 %collective-permute-start.6 = (bf16[256,896]{1,0:T(8,128)(2,1)S(1)}, bf16[256,896]{1,0:T(8,128)(2,1)S(1)}, u32[]{:S(2)}, u32[]{:S(2)}) collective-permute-start(bf16[256,896]{1,0:T(8,128)(2,1)S(1)} %get-tuple-element.15.first_ref), channel_id=1, source_target_pairs={{0,1},{1,2},{2,3},{3,0},{4,5},{5,6},{6,7},{7,4},{8,9},{9,10},{10,1... | collective-permute-start | bytes 1376264 | tf_op jit(solution)/shard_map/ppermute | solution.py:307
  59.7 14.7 %collective-permute-start.8 = (bf16[256,896]{1,0:T(8,128)(2,1)S(1)}, bf16[256,896]{1,0:T(8,128)(2,1)S(1)}, u32[]{:S(2)}, u32[]{:S(2)}) collective-permute-start(bf16[256,896]{1,0:T(8,128)(2,1)S(1)} %get-tuple-element.16.second_ref), channel_id=1, source_target_pairs={{0,3},{1,0},{2,1},{3,2},{4,7},{5,4},{6,5},{7,6},{8,11},{9,8},{10,9... | collective-permute-start | bytes 1376264 | tf_op jit(solution)/shard_map/ppermute | solution.py:308
  64.3 18.0 %collective-permute-start.10 = (bf16[256,896]{1,0:T(8,128)(2,1)S(1)}, bf16[256,896]{1,0:T(8,128)(2,1)S(1)}, u32[]{:S(2)}, u32[]{:S(2)}) collective-permute-start(bf16[256,896]{1,0:T(8,128)(2,1)S(1)} %get-tuple-element.16.second_ref), channel_id=1, source_target_pairs={{0,1},{1,2},{2,3},{3,0},{4,5},{5,6},{6,7},{7,4},{8,9},{9,10},{10,1... | collective-permute-start | bytes 1376264 | tf_op jit(solution)/shard_map/ppermute | solution.py:309
  66.2 17.9 %collective-permute-start.11 = (bf16[256,896]{1,0:T(8,128)(2,1)S(1)}, bf16[256,896]{1,0:T(8,128)(2,1)S(1)}, u32[]{:S(2)}, u32[]{:S(2)}) collective-permute-start(bf16[256,896]{1,0:T(8,128)(2,1)S(1)} %get-tuple-element.15.first_ref), channel_id=1, source_target_pairs={{0,3},{1,0},{2,1},{3,2},{4,7},{5,4},{6,5},{7,6},{8,11},{9,8},{10,9... | collective-permute-start | bytes 1376264 | tf_op jit(solution)/shard_map/ppermute | solution.py:310
  72.4 16.0 %collective-permute-start.7 = (bf16[256,896]{1,0:T(8,128)(2,1)S(1)}, bf16[256,896]{1,0:T(8,128)(2,1)S(1)}, u32[]{:S(2)}, u32[]{:S(2)}) collective-permute-start(bf16[256,896]{1,0:T(8,128)(2,1)S(1)} %collective-permute-done.6.left_first), channel_id=1, source_target_pairs={{0,1},{1,2},{2,3},{3,0},{4,5},{5,6},{6,7},{7,4},{8,9},{9,10},{10,1... | collective-permute-start | bytes 1376264 | tf_op jit(solution)/shard_map/ppermute | solution.py:311
  74.3 15.6 %collective-permute-start.9 = (bf16[256,896]{1,0:T(8,128)(2,1)S(1)}, bf16[256,896]{1,0:T(8,128)(2,1)S(1)}, u32[]{:S(2)}, u32[]{:S(2)}) collective-permute-start(bf16[256,896]{1,0:T(8,128)(2,1)S(1)} %collective-permute-done.8.right_second), channel_id=1, source_target_pairs={{0,3},{1,0},{2,1},{3,2},{4,7},{5,4},{6,5},{7,6},{8,11},{9,8},{10,9... | collective-permute-start | bytes 1376264 | tf_op jit(solution)/shard_map/ppermute | solution.py:312
  110.1 40.3 %all-to-all-start.3 = ((bf16[64,8,896]{2,1,0:T(8,128)(2,1)}), bf16[64,8,896]{2,1,0:T(8,128)(2,1)S(1)}, u32[]{:S(2)}, u32[]{:S(2)}) async-start(bf16[64,8,896]{2,1,0:T(8,128)(2,1)} %bitcast.29), calls=%async_computation.3 | async-start | bytes 1835008 | tf_op jit(solution)/shard_map/all_to_all | solution.py:355
  125.1 3.1 %collective-permute-start.12 = (f32[8,128]{1,0:T(8,128)S(1)}, f32[8,128]{1,0:T(8,128)S(1)}, u32[]{:S(2)}, u32[]{:S(2)}) collective-permute-start(f32[8,128]{1,0:T(8,128)S(1)} %get-tuple-element.23), channel_id=1, source_target_pairs={{0,4},{4,0},{8,12},{12,8},{16,20},{20,16},{24,28},{28,24},{32,36},... | collective-permute-start | bytes 12296 | tf_op jit(solution)/shard_map/ppermute | solution.py:364
  151.3 8.7 %all-to-all-start.4 = ((bf16[4,4,896]{2,1,0:T(4,128)(2,1)}), bf16[4,4,896]{2,1,0:T(4,128)(2,1)S(1)}, u32[]{:S(2)}, u32[]{:S(2)}) async-start(bf16[4,4,896]{2,1,0:T(4,128)(2,1)} %shard_map.102), calls=%async_computation.4 | async-start | bytes 57344 | tf_op jit(solution)/shard_map/all_to_all | solution.py:361

commit v5 on v4

--- a/solution.py
+++ b/solution.py
@@ -41,8 +41,8 @@
 
 
 def route_body(
-    tok_hbm, weight_hbm, ids_hbm, replica_hbm, place_hbm, send_hbm,
-    tok_ref, weight_ref, ids_ref, replica_ref, place_ref, send_ref, sems,
+    tok_hbm, weight_hbm, ids_hbm, replica_hbm, place_hbm, send_ref,
+    tok_ref, weight_ref, ids_ref, replica_ref, place_ref, sems,
 ):
     pairs = [
         (place_hbm, place_ref),
@@ -76,9 +76,6 @@
     for x in range(dp):
         send_ref[x, :, :piece] = tok_ref[:, x * piece : (x + 1) * piece]
         send_ref[x, :, piece:] = tail
-    out = pltpu.make_async_copy(send_ref, send_hbm, sems.at[len(pairs)])
-    out.start()
-    out.wait()
 
 
 def pack_body(steps, capacity, top, got_ref, rows_hbm, weight_ref, rows_ref, sems):
@@ -108,14 +105,21 @@
     pick = taken.astype(F32)
     used = jnp.sum(pick, axis=1, keepdims=True)
     pick = pick.astype(BF16)
-    head = jnp.dot(pick, got_ref[:, :128], preferred_element_type=F32)
-    lane = lax.broadcasted_iota(jnp.int32, (count, 128), 1)
-    head = jnp.where((lane == 0) & (used < 0.5), EMPTY, head)
-    rows_ref[:, :128] = head.astype(BF16)
-    rows_ref[:, 128:] = jnp.dot(pick, got_ref[:, 128:piece], preferred_element_type=F32).astype(BF16)
-    out = pltpu.make_async_copy(rows_ref, rows_hbm, sems.at[0])
-    out.start()
-    out.wait()
+    got = got_ref[:, :piece]
+    halves = 4
+    size = count // halves
+    copies = []
+    lane = lax.broadcasted_iota(jnp.int32, (size, 128), 1)
+    for i in range(halves):
+        at = slice(i * size, (i + 1) * size)
+        rows = jnp.dot(pick[at], got, preferred_element_type=F32)
+        rows_ref[at, :128] = jnp.where((lane == 0) & (used[at] < 0.5), EMPTY, rows[:, :128]).astype(BF16)
+        rows_ref[at, 128:] = rows[:, 128:].astype(BF16)
+        out = pltpu.make_async_copy(rows_ref.at[at], rows_hbm.at[at], sems.at[i])
+        out.start()
+        copies.append(out)
+    for out in copies:
+        out.wait()
 
 
 def split_body(steps, capacity, x_ref, *refs):
@@ -192,16 +196,13 @@
         load.wait()
 
 
-def last_piece_body(first_ref, second_ref, gate_in, up_in, far_ref, out_hbm, out_ref, sems):
+def last_piece_body(first_ref, second_ref, gate_in, up_in, far_ref, out_ref):
     gate, up = products(first_ref, second_ref, far_ref[0], far_ref[1])
     gate += gate_in[...]
     up += up_in[...]
-    out_ref[...] = (gate / (1.0 + jnp.exp(-gate)) * up).astype(BF16)
-    copies = [pltpu.make_async_copy(out_ref, out_hbm.at[i], sems.at[i]) for i in range(out_hbm.shape[0])]
-    for copy in copies:
-        copy.start()
-    for copy in copies:
-        copy.wait()
+    hidden = (gate / (1.0 + jnp.exp(-gate)) * up).astype(BF16)
+    for i in range(out_ref.shape[0]):
+        out_ref[i] = hidden
 
 
 def down_body(here_ref, hid_ref, w_ref, out_hbm, out_ref, sems):
@@ -260,15 +261,13 @@
             placement.T,
         ],
         in_specs=[HBM] * 5,
-        out_specs=[HBM],
         scratch=[
             pltpu.VMEM((steps, width), BF16),
             pltpu.VMEM((steps, top), BF16),
             pltpu.VMEM((steps, 1, top), jnp.int32),
             pltpu.VMEM((steps, 1, top), jnp.int32),
             pltpu.VMEM(placement.shape[::-1], jnp.int32),
-            pltpu.VMEM((dp, steps, piece + 128), BF16),
-            pltpu.SemaphoreType.DMA((6,)),
+            pltpu.SemaphoreType.DMA((5,)),
         ],
     )
     got = lax.all_to_all(send, "dp", 0, 0)
@@ -288,7 +287,7 @@
         [shape((count, piece), BF16), shape((count, dp * steps), BF16)],
         [got.reshape(dp * steps, piece + 128)],
         out_specs=[HBM, VMEM],
-        scratch=[pltpu.VMEM((count, piece), BF16), pltpu.SemaphoreType.DMA((1,))],
+        scratch=[pltpu.VMEM((count, piece), BF16), pltpu.SemaphoreType.DMA((4,))],
     )
     arrived = lax.all_to_all(
         rows.reshape(slots, per_slot, piece), "ep", 0, 0, axis_index_groups=same_core
@@ -339,8 +338,6 @@
         [shape((dp, count, 2 * hid), BF16)],
         [far_first, far_second, gate_sum, up_sum, far_weights],
         flops,
-        out_specs=[HBM],
-        scratch=[pltpu.VMEM((count, 2 * hid), BF16), pltpu.SemaphoreType.DMA((dp,))],
     )
     hidden = lax.all_to_all(hidden, "dp", 0, 0)
     (out,) = call(

time: 161 us -> 159 us (0.988)
  Pallas kernels: 13.8 us -> 12 us
    pallas_call x8, Pallas kernels: 13.8 us -> 12 us  [call(): pl.pallas_call(body, out_shape=tuple((pltpu.HBM(o.shape, o.dtype) if spec...]
where the time goes in v5:
time: 159 us; the launch traced here: 158 us
  starting transfers between devices  73.2 us (46%)
  waiting for transfers between devices  45 us (28%)
  blocking collectives  25.7 us (16%)
  Pallas kernels  12 us (8%)
    all_to_all x1, waiting for transfers between devices, local(): lax.all_to_all(out.reshape(slots, per_slot, piece), 'ep', 0, 0, axis_inde...  22.3 us
    all_to_all x1, starting transfers between devices, local(): lax.all_to_all(rows.reshape(slots, per_slot, piece), 'ep', 0, 0, axis_ind...  16.6 us
    all_to_all x1, blocking collectives, local(): hidden = lax.all_to_all(hidden, 'dp', 0, 0)  16.2 us
    all_to_all x1, starting transfers between devices, local(): lax.all_to_all(out.reshape(slots, per_slot, piece), 'ep', 0, 0, axis_inde...  14.9 us
    pallas_call x8, Pallas kernels, call(): pl.pallas_call(body, out_shape=tuple((pltpu.HBM(o.shape, o.dtype) if spec...  12 us
    all_to_all x1, blocking collectives, local(): got = lax.all_to_all(send, 'dp', 0, 0)  9.54 us
    ppermute x3, starting transfers between devices, local(): lax.ppermute(block, 'dp', [(x, (x + d) % dp) for x in range(dp)])  8.83 us
    ppermute x1, starting transfers between devices, local(): far_second = lax.ppermute(right_second, 'dp', behind)  5.44 us
  transfers between devices with their start and end apart: 16, of which 11 were waited for; matrix products, arithmetic and copies ran while one was open for 0% of the time, Pallas kernels for 3%

profile of v5, /device:TPU:8, one launch (start us, length us, event | category | flops | bytes accessed | tf_op | source)
XLA Modules:
  0.0 158.3 jit_solution(17278101605580448075)
XLA Ops:
  0.6 1.5 shard_map.95
  2.1 9.5 %all_to_all.25 = bf16[4,4,1024]{2,1,0:T(4,128)(2,1)S(1)} all-to-all(bf16[4,4,1024]{2,1,0:T(4,128)(2,1)S(1)} %shard_map.95), channel_id=1, replica_groups=mesh['ep'=128,'dp'=4] {'dp'}, dimensions={0} | all-to-all | bytes 65536 | tf_op jit(solution)/shard_map/all_to_all | solution.py:273
  11.7 1.7 %shard_map.96 = (bf16[512,896]{1,0:T(8,128)(2,1)}, bf16[512,16]{1,0:T(8,128)(2,1)S(1)}) custom-call(bf16[16,1024]{1,0:T(8,128)(2,1)S(1)} %reshape.50.got_ref), custom_call_target="tpu_custom_call" | custom-call | bytes 966656 | tf_op jit(solution)/shard_map/pallas_call | solution.py:29
  13.4 16.6 %all-to-all-start.1 = ((bf16[64,8,896]{2,1,0:T(8,128)(2,1)}), bf16[64,8,896]{2,1,0:T(8,128)(2,1)S(1)}, u32[]{:S(2)}, u32[]{:S(2)}) async-start(bf16[64,8,896]{2,1,0:T(8,128)(2,1)} %bitcast.30), calls=%async_computation.1 | async-start | bytes 1835008 | tf_op jit(solution)/shard_map/all_to_all | solution.py:292
  30.1 3.1 %collective-permute-start.2 = (bf16[128,896]{1,0:T(8,128)(2,1)S(1)}, bf16[128,896]{1,0:T(8,128)(2,1)S(1)}, u32[]{:S(2)}, u32[]{:S(2)}) collective-permute-start(bf16[128,896]{1,0:T(8,128)(2,1)S(1)} %get-tuple-element.26), channel_id=1, source_target_pairs={{0,3},{1,0},{2,1},{3,2},{4,7},{5,4},{6,5},{7,6},{8,11},{9,8},{10,9... | collective-permute-start | bytes 688136 | tf_op jit(solution)/shard_map/ppermute | solution.py:281
  33.2 2.8 %collective-permute-start = (bf16[128,896]{1,0:T(8,128)(2,1)S(1)}, bf16[128,896]{1,0:T(8,128)(2,1)S(1)}, u32[]{:S(2)}, u32[]{:S(2)}) collective-permute-start(bf16[128,896]{1,0:T(8,128)(2,1)S(1)} %get-tuple-element.25), channel_id=1, source_target_pairs={{0,1},{1,2},{2,3},{3,0},{4,5},{5,6},{6,7},{7,4},{8,9},{9,10},{10,1... | collective-permute-start | bytes 688136 | tf_op jit(solution)/shard_map/ppermute | solution.py:281
  36.0 3.0 %collective-permute-start.1 = (bf16[128,896]{1,0:T(8,128)(2,1)S(1)}, bf16[128,896]{1,0:T(8,128)(2,1)S(1)}, u32[]{:S(2)}, u32[]{:S(2)}) collective-permute-start(bf16[128,896]{1,0:T(8,128)(2,1)S(1)} %get-tuple-element.27), channel_id=1, source_target_pairs={{0,2},{1,3},{2,0},{3,1},{4,6},{5,7},{6,4},{7,5},{8,10},{9,11},{10,... | collective-permute-start | bytes 688136 | tf_op jit(solution)/shard_map/ppermute | solution.py:281
  38.9 1.9 %collective-permute-start.4 = (bf16[3584,128]{1,0:T(8,128)(2,1)}, bf16[3584,128]{1,0:T(8,128)(2,1)S(1)}, u32[]{:S(2)}, u32[]{:S(2)}) collective-permute-start(bf16[3584,128]{1,0:T(8,128)(2,1)} %bitcast.12.refs_0_), channel_id=1, source_target_pairs={{0,4},{4,0},{8,12},{12,8},{16,20},{20,16},{24,28},{28,24},{32,36},... | collective-permute-start | bytes 2752520 | tf_op jit(solution)/shard_map/ppermute | solution.py:276
  40.9 2.4 %collective-permute-start.5 = (bf16[3584,128]{1,0:T(8,128)(2,1)}, bf16[3584,128]{1,0:T(8,128)(2,1)S(1)}, u32[]{:S(2)}, u32[]{:S(2)}) collective-permute-start(bf16[3584,128]{1,0:T(8,128)(2,1)} %bitcast.26), channel_id=1, source_target_pairs={{0,4},{4,0},{8,12},{12,8},{16,20},{20,16},{24,28},{28,24},{32,36},... | collective-permute-start | bytes 2752520 | tf_op jit(solution)/shard_map/ppermute | solution.py:277
  43.3 3.6 %collective-permute-done = bf16[128,896]{1,0:T(8,128)(2,1)S(1)} collective-permute-done((bf16[128,896]{1,0:T(8,128)(2,1)S(1)}, bf16[128,896]{1,0:T(8,128)(2,1)S(1)}, u32[]{:S(2)}, u32[]{:S(2)}) %collective-permute-start) | collective-permute-done | bytes 229408 | tf_op jit(solution)/shard_map/ppermute | solution.py:281
  47.0 1.9 %collective-permute-start.3 = (bf16[4,128,896]{2,1,0:T(8,128)(2,1)S(1)}, bf16[4,128,896]{2,1,0:T(8,128)(2,1)}, u32[]{:S(2)}, u32[]{:S(2)}) collective-permute-start(bf16[4,128,896]{2,1,0:T(8,128)(2,1)S(1)} %pad_maximum_fusion.refs_4_), channel_id=1, source_target_pairs={{0,4},{4,0},{8,12},{12,8},{16,20},{20,16},{24,28},{28,24},{32,36},... | collective-permute-start | bytes 2752520 | tf_op jit(solution)/shard_map/ppermute | solution.py:283
  49.0 2.5 %collective-permute-done.3.refs_0_.refs_5_ = bf16[4,128,896]{2,1,0:T(8,128)(2,1)} collective-permute-done((bf16[4,128,896]{2,1,0:T(8,128)(2,1)S(1)}, bf16[4,128,896]{2,1,0:T(8,128)(2,1)}, u32[]{:S(2)}, u32[]{:S(2)}) %collective-permute-start.3) | collective-permute-done | bytes 917536 | tf_op jit(solution)/shard_map/ppermute | solution.py:283
  51.5 4.4 %all-to-all-done.1 = bf16[64,8,896]{2,1,0:T(8,128)(2,1)S(1)} async-done(((bf16[64,8,896]{2,1,0:T(8,128)(2,1)}), bf16[64,8,896]{2,1,0:T(8,128)(2,1)S(1)}, u32[]{:S(2)}, u32[]{:S(2)}) %all-to-all-start.1) | async-done | bytes 917536 | tf_op jit(solution)/shard_map/all_to_all | solution.py:292
  56.2 2.5 %collective-permute-start.6 = (bf16[256,896]{1,0:T(8,128)(2,1)S(1)}, bf16[256,896]{1,0:T(8,128)(2,1)S(1)}, u32[]{:S(2)}, u32[]{:S(2)}) collective-permute-start(bf16[256,896]{1,0:T(8,128)(2,1)S(1)} %get-tuple-element.15.first_ref), channel_id=1, source_target_pairs={{0,1},{1,2},{2,3},{3,0},{4,5},{5,6},{6,7},{7,4},{8,9},{9,10},{10,1... | collective-permute-start | bytes 1376264 | tf_op jit(solution)/shard_map/ppermute | solution.py:306
  58.6 4.6 %collective-permute-start.8 = (bf16[256,896]{1,0:T(8,128)(2,1)S(1)}, bf16[256,896]{1,0:T(8,128)(2,1)S(1)}, u32[]{:S(2)}, u32[]{:S(2)}) collective-permute-start(bf16[256,896]{1,0:T(8,128)(2,1)S(1)} %get-tuple-element.16.second_ref), channel_id=1, source_target_pairs={{0,3},{1,0},{2,1},{3,2},{4,7},{5,4},{6,5},{7,6},{8,11},{9,8},{10,9... | collective-permute-start | bytes 1376264 | tf_op jit(solution)/shard_map/ppermute | solution.py:307
  63.2 1.9 %collective-permute-start.10 = (bf16[256,896]{1,0:T(8,128)(2,1)S(1)}, bf16[256,896]{1,0:T(8,128)(2,1)S(1)}, u32[]{:S(2)}, u32[]{:S(2)}) collective-permute-start(bf16[256,896]{1,0:T(8,128)(2,1)S(1)} %get-tuple-element.16.second_ref), channel_id=1, source_target_pairs={{0,1},{1,2},{2,3},{3,0},{4,5},{5,6},{6,7},{7,4},{8,9},{9,10},{10,1... | collective-permute-start | bytes 1376264 | tf_op jit(solution)/shard_map/ppermute | solution.py:308
  65.2 5.1 %collective-permute-start.11 = (bf16[256,896]{1,0:T(8,128)(2,1)S(1)}, bf16[256,896]{1,0:T(8,128)(2,1)S(1)}, u32[]{:S(2)}, u32[]{:S(2)}) collective-permute-start(bf16[256,896]{1,0:T(8,128)(2,1)S(1)} %get-tuple-element.15.first_ref), channel_id=1, source_target_pairs={{0,3},{1,0},{2,1},{3,2},{4,7},{5,4},{6,5},{7,6},{8,11},{9,8},{10,9... | collective-permute-start | bytes 1376264 | tf_op jit(solution)/shard_map/ppermute | solution.py:309
  71.4 1.9 %collective-permute-start.7 = (bf16[256,896]{1,0:T(8,128)(2,1)S(1)}, bf16[256,896]{1,0:T(8,128)(2,1)S(1)}, u32[]{:S(2)}, u32[]{:S(2)}) collective-permute-start(bf16[256,896]{1,0:T(8,128)(2,1)S(1)} %collective-permute-done.6.left_first), channel_id=1, source_target_pairs={{0,1},{1,2},{2,3},{3,0},{4,5},{5,6},{6,7},{7,4},{8,9},{9,10},{10,1... | collective-permute-start | bytes 1376264 | tf_op jit(solution)/shard_map/ppermute | solution.py:310
  73.3 5.4 %collective-permute-start.9 = (bf16[256,896]{1,0:T(8,128)(2,1)S(1)}, bf16[256,896]{1,0:T(8,128)(2,1)S(1)}, u32[]{:S(2)}, u32[]{:S(2)}) collective-permute-start(bf16[256,896]{1,0:T(8,128)(2,1)S(1)} %collective-permute-done.8.right_second), channel_id=1, source_target_pairs={{0,3},{1,0},{2,1},{3,2},{4,7},{5,4},{6,5},{7,6},{8,11},{9,8},{10,9... | collective-permute-start | bytes 1376264 | tf_op jit(solution)/shard_map/ppermute | solution.py:311
  78.8 2.0 %shard_map.98 = (f32[512,256]{1,0:T(8,128)S(1)}, f32[512,256]{1,0:T(8,128)S(1)}) custom-call(s32[1]{0:T(128)} %bitcast.3.here_ref, bf16[256,896]{1,0:T(8,128)(2,1)S(1)} %get-tuple-element.15.first_ref, bf16[256,896]{1,0:T(8,128)(2,1)S(1)} %get-tuple-element.16.second_ref, bf16[3584,128]{1,0:T(8,128)(2,1)} %bitcast.12.refs_0_, bf16[3584,128]{1,0:T(8,128)(2,1)} %bitcast.27, ...), custom_call_target="tpu_custom_call" | custom-call | flops 469762048 | bytes 5636100 | tf_op jit(solution)/shard_map/pallas_call | solution.py:29
  81.2 1.9 %collective-permute-done.11.right_first = bf16[256,896]{1,0:T(8,128)(2,1)S(1)} collective-permute-done((bf16[256,896]{1,0:T(8,128)(2,1)S(1)}, bf16[256,896]{1,0:T(8,128)(2,1)S(1)}, u32[]{:S(2)}, u32[]{:S(2)}) %collective-permute-start.11) | collective-permute-done | bytes 458784 | tf_op jit(solution)/shard_map/ppermute | solution.py:309
  83.1 3.0 %shard_map.99 = (f32[512,256]{1,0:T(8,128)S(1)}, f32[512,256]{1,0:T(8,128)S(1)}, bf16[2,896,256]{2,1,0:T(8,128)(2,1)S(1)}, bf16[4,256,896]{2,1,0:T(8,128)(2,1)S(1)}) custom-call(s32[1]{0:T(128)} %bitcast.3.here_ref, bf16[256,896]{1,0:T(8,128)(2,1)S(1)} %collective-permute-done.6.left_first, bf16[256,896]{1,0:T(8,128)(2,1)S(1)} %collective-permute-done.10.left_second, ...), custom_call_target="tpu_custom_call" | custom-call | flops 939524096 | bytes 12189700 | tf_op jit(solution)/shard_map/pallas_call | solution.py:29
  86.1 1.3 collective-permute-done.7.first_ref
  87.4 1.5 collective-permute-done.9.second_ref
  89.6 16.2 %all_to_all.26.hid_ref = bf16[4,512,256]{2,1,0:T(8,128)(2,1)S(1)} all-to-all(bf16[4,512,256]{2,1,0:T(8,128)(2,1)S(1)} %shard_map.100), channel_id=1, replica_groups=mesh['ep'=128,'dp'=4] {'dp'}, dimensions={0} | all-to-all | bytes 2097152 | tf_op jit(solution)/shard_map/all_to_all | solution.py:342
  105.8 2.1 %shard_map.101 = bf16[512,896]{1,0:T(8,128)(2,1)} custom-call(s32[1]{0:T(128)} %bitcast.3.here_ref, bf16[4,512,256]{2,1,0:T(8,128)(2,1)S(1)} %all_to_all.26.hid_ref, bf16[4,256,896]{2,1,0:T(8,128)(2,1)S(1)} %get-tuple-element.22.w_ref), custom_call_target="tpu_custom_call" | custom-call | flops 939524096 | bytes 3801092 | tf_op jit(solution)/shard_map/pallas_call | solution.py:29
  107.9 14.9 %all-to-all-start.3 = ((bf16[64,8,896]{2,1,0:T(8,128)(2,1)}), bf16[64,8,896]{2,1,0:T(8,128)(2,1)S(1)}, u32[]{:S(2)}, u32[]{:S(2)}) async-start(bf16[64,8,896]{2,1,0:T(8,128)(2,1)} %bitcast.29), calls=%async_computation.3 | async-start | bytes 1835008 | tf_op jit(solution)/shard_map/all_to_all | solution.py:352
  122.8 1.9 %collective-permute-start.12 = (f32[8,128]{1,0:T(8,128)S(1)}, f32[8,128]{1,0:T(8,128)S(1)}, u32[]{:S(2)}, u32[]{:S(2)}) collective-permute-start(f32[8,128]{1,0:T(8,128)S(1)} %get-tuple-element.23), channel_id=1, source_target_pairs={{0,4},{4,0},{8,12},{12,8},{16,20},{20,16},{24,28},{28,24},{32,36},... | collective-permute-start | bytes 12296 | tf_op jit(solution)/shard_map/ppermute | solution.py:361
  124.7 1.1 collective-permute-done.12
  125.8 22.3 %all-to-all-done.3 = bf16[64,8,896]{2,1,0:T(8,128)(2,1)S(1)} async-done(((bf16[64,8,896]{2,1,0:T(8,128)(2,1)}), bf16[64,8,896]{2,1,0:T(8,128)(2,1)S(1)}, u32[]{:S(2)}, u32[]{:S(2)}) %all-to-all-start.3) | async-done | bytes 917536 | tf_op jit(solution)/shard_map/all_to_all | solution.py:352
  149.0 3.3 %all-to-all-start.4 = ((bf16[4,4,896]{2,1,0:T(4,128)(2,1)}), bf16[4,4,896]{2,1,0:T(4,128)(2,1)S(1)}, u32[]{:S(2)}, u32[]{:S(2)}) async-start(bf16[4,4,896]{2,1,0:T(4,128)(2,1)} %shard_map.102), calls=%async_computation.4 | async-start | bytes 57344 | tf_op jit(solution)/shard_map/all_to_all | solution.py:358
  152.8 4.9 %all-to-all-done.4 = bf16[4,4,896]{2,1,0:T(4,128)(2,1)S(1)} async-done(((bf16[4,4,896]{2,1,0:T(4,128)(2,1)}), bf16[4,4,896]{2,1,0:T(4,128)(2,1)S(1)}, u32[]{:S(2)}, u32[]{:S(2)}) %all-to-all-start.4) | async-done | bytes 28704 | tf_op jit(solution)/shard_map/all_to_all | solution.py:358
  (24 shorter events, 4.7 us)
Async XLA Ops:
  0.6 29.4 %copy-start.3 = (bf16[1,128,3584]{2,1,0:T(8,128)(2,1)S(1)}, bf16[1,128,3584]{2,1,0:T(8,128)(2,1)}, u32[]{:S(2)}) copy-start(bf16[1,128,3584]{2,1,0:T(8,128)(2,1)} %param.15) | copy-start | bytes 2752516
  13.4 42.6 %all-to-all-start.1 = ((bf16[64,8,896]{2,1,0:T(8,128)(2,1)}), bf16[64,8,896]{2,1,0:T(8,128)(2,1)S(1)}, u32[]{:S(2)}, u32[]{:S(2)}) async-start(bf16[64,8,896]{2,1,0:T(8,128)(2,1)} %bitcast.30), calls=%async_computation.1 | async-start | bytes 1835008 | tf_op jit(solution)/shard_map/all_to_all | solution.py:292
  30.1 13.2 %collective-permute-start.2 = (bf16[128,896]{1,0:T(8,128)(2,1)S(1)}, bf16[128,896]{1,0:T(8,128)(2,1)S(1)}, u32[]{:S(2)}, u32[]{:S(2)}) collective-permute-start(bf16[128,896]{1,0:T(8,128)(2,1)S(1)} %get-tuple-element.26), channel_id=1, source_target_pairs={{0,3},{1,0},{2,1},{3,2},{4,7},{5,4},{6,5},{7,6},{8,11},{9,8},{10,9... | collective-permute-start | bytes 688136 | tf_op jit(solution)/shard_map/ppermute | solution.py:281
  33.2 13.7 %collective-permute-start = (bf16[128,896]{1,0:T(8,128)(2,1)S(1)}, bf16[128,896]{1,0:T(8,128)(2,1)S(1)}, u32[]{:S(2)}, u32[]{:S(2)}) collective-permute-start(bf16[128,896]{1,0:T(8,128)(2,1)S(1)} %get-tuple-element.25), channel_id=1, source_target_pairs={{0,1},{1,2},{2,3},{3,0},{4,5},{5,6},{6,7},{7,4},{8,9},{9,10},{10,1... | collective-permute-start | bytes 688136 | tf_op jit(solution)/shard_map/ppermute | solution.py:281
  36.0 10.9 %collective-permute-start.1 = (bf16[128,896]{1,0:T(8,128)(2,1)S(1)}, bf16[128,896]{1,0:T(8,128)(2,1)S(1)}, u32[]{:S(2)}, u32[]{:S(2)}) collective-permute-start(bf16[128,896]{1,0:T(8,128)(2,1)S(1)} %get-tuple-element.27), channel_id=1, source_target_pairs={{0,2},{1,3},{2,0},{3,1},{4,6},{5,7},{6,4},{7,5},{8,10},{9,11},{10,... | collective-permute-start | bytes 688136 | tf_op jit(solution)/shard_map/ppermute | solution.py:281
  38.9 10.0 %collective-permute-start.4 = (bf16[3584,128]{1,0:T(8,128)(2,1)}, bf16[3584,128]{1,0:T(8,128)(2,1)S(1)}, u32[]{:S(2)}, u32[]{:S(2)}) collective-permute-start(bf16[3584,128]{1,0:T(8,128)(2,1)} %bitcast.12.refs_0_), channel_id=1, source_target_pairs={{0,4},{4,0},{8,12},{12,8},{16,20},{20,16},{24,28},{28,24},{32,36},... | collective-permute-start | bytes 2752520 | tf_op jit(solution)/shard_map/ppermute | solution.py:276
  40.9 8.1 %collective-permute-start.5 = (bf16[3584,128]{1,0:T(8,128)(2,1)}, bf16[3584,128]{1,0:T(8,128)(2,1)S(1)}, u32[]{:S(2)}, u32[]{:S(2)}) collective-permute-start(bf16[3584,128]{1,0:T(8,128)(2,1)} %bitcast.26), channel_id=1, source_target_pairs={{0,4},{4,0},{8,12},{12,8},{16,20},{20,16},{24,28},{28,24},{32,36},... | collective-permute-start | bytes 2752520 | tf_op jit(solution)/shard_map/ppermute | solution.py:277
  47.0 2.0 %copy-start.2 = (bf16[4,128,896]{2,1,0:T(8,128)(2,1)}, bf16[4,128,896]{2,1,0:T(8,128)(2,1)S(1)}, u32[]{:S(2)}) copy-start(bf16[4,128,896]{2,1,0:T(8,128)(2,1)S(1)} %pad_maximum_fusion.refs_4_) | copy-start | bytes 2752516
  47.0 4.5 %collective-permute-start.3 = (bf16[4,128,896]{2,1,0:T(8,128)(2,1)S(1)}, bf16[4,128,896]{2,1,0:T(8,128)(2,1)}, u32[]{:S(2)}, u32[]{:S(2)}) collective-permute-start(bf16[4,128,896]{2,1,0:T(8,128)(2,1)S(1)} %pad_maximum_fusion.refs_4_), channel_id=1, source_target_pairs={{0,4},{4,0},{8,12},{12,8},{16,20},{20,16},{24,28},{28,24},{32,36},... | collective-permute-start | bytes 2752520 | tf_op jit(solution)/shard_map/ppermute | solution.py:283
  49.0 7.2 %copy-start = (bf16[3584,128]{1,0:T(8,128)(2,1)}, bf16[3584,128]{1,0:T(8,128)(2,1)S(1)}, u32[]{:S(2)}) copy-start(bf16[3584,128]{1,0:T(8,128)(2,1)S(1)} %collective-permute-done.4.refs_1_.refs_2_) | copy-start | bytes 2752516
  49.0 7.1 %copy-start.1 = (bf16[3584,128]{1,0:T(8,128)(2,1)}, bf16[3584,128]{1,0:T(8,128)(2,1)S(1)}, u32[]{:S(2)}) copy-start(bf16[3584,128]{1,0:T(8,128)(2,1)S(1)} %collective-permute-done.5.refs_2_.refs_3_) | copy-start | bytes 2752516
  56.2 15.2 %collective-permute-start.6 = (bf16[256,896]{1,0:T(8,128)(2,1)S(1)}, bf16[256,896]{1,0:T(8,128)(2,1)S(1)}, u32[]{:S(2)}, u32[]{:S(2)}) collective-permute-start(bf16[256,896]{1,0:T(8,128)(2,1)S(1)} %get-tuple-element.15.first_ref), channel_id=1, source_target_pairs={{0,1},{1,2},{2,3},{3,0},{4,5},{5,6},{6,7},{7,4},{8,9},{9,10},{10,1... | collective-permute-start | bytes 1376264 | tf_op jit(solution)/shard_map/ppermute | solution.py:306
  58.6 14.7 %collective-permute-start.8 = (bf16[256,896]{1,0:T(8,128)(2,1)S(1)}, bf16[256,896]{1,0:T(8,128)(2,1)S(1)}, u32[]{:S(2)}, u32[]{:S(2)}) collective-permute-start(bf16[256,896]{1,0:T(8,128)(2,1)S(1)} %get-tuple-element.16.second_ref), channel_id=1, source_target_pairs={{0,3},{1,0},{2,1},{3,2},{4,7},{5,4},{6,5},{7,6},{8,11},{9,8},{10,9... | collective-permute-start | bytes 1376264 | tf_op jit(solution)/shard_map/ppermute | solution.py:307
  63.2 18.0 %collective-permute-start.10 = (bf16[256,896]{1,0:T(8,128)(2,1)S(1)}, bf16[256,896]{1,0:T(8,128)(2,1)S(1)}, u32[]{:S(2)}, u32[]{:S(2)}) collective-permute-start(bf16[256,896]{1,0:T(8,128)(2,1)S(1)} %get-tuple-element.16.second_ref), channel_id=1, source_target_pairs={{0,1},{1,2},{2,3},{3,0},{4,5},{5,6},{6,7},{7,4},{8,9},{9,10},{10,1... | collective-permute-start | bytes 1376264 | tf_op jit(solution)/shard_map/ppermute | solution.py:308
  65.2 18.0 %collective-permute-start.11 = (bf16[256,896]{1,0:T(8,128)(2,1)S(1)}, bf16[256,896]{1,0:T(8,128)(2,1)S(1)}, u32[]{:S(2)}, u32[]{:S(2)}) collective-permute-start(bf16[256,896]{1,0:T(8,128)(2,1)S(1)} %get-tuple-element.15.first_ref), channel_id=1, source_target_pairs={{0,3},{1,0},{2,1},{3,2},{4,7},{5,4},{6,5},{7,6},{8,11},{9,8},{10,9... | collective-permute-start | bytes 1376264 | tf_op jit(solution)/shard_map/ppermute | solution.py:309
  71.4 16.0 %collective-permute-start.7 = (bf16[256,896]{1,0:T(8,128)(2,1)S(1)}, bf16[256,896]{1,0:T(8,128)(2,1)S(1)}, u32[]{:S(2)}, u32[]{:S(2)}) collective-permute-start(bf16[256,896]{1,0:T(8,128)(2,1)S(1)} %collective-permute-done.6.left_first), channel_id=1, source_target_pairs={{0,1},{1,2},{2,3},{3,0},{4,5},{5,6},{6,7},{7,4},{8,9},{9,10},{10,1... | collective-permute-start | bytes 1376264 | tf_op jit(solution)/shard_map/ppermute | solution.py:310
  73.3 15.6 %collective-permute-start.9 = (bf16[256,896]{1,0:T(8,128)(2,1)S(1)}, bf16[256,896]{1,0:T(8,128)(2,1)S(1)}, u32[]{:S(2)}, u32[]{:S(2)}) collective-permute-start(bf16[256,896]{1,0:T(8,128)(2,1)S(1)} %collective-permute-done.8.right_second), channel_id=1, source_target_pairs={{0,3},{1,0},{2,1},{3,2},{4,7},{5,4},{6,5},{7,6},{8,11},{9,8},{10,9... | collective-permute-start | bytes 1376264 | tf_op jit(solution)/shard_map/ppermute | solution.py:311
  107.9 40.3 %all-to-all-start.3 = ((bf16[64,8,896]{2,1,0:T(8,128)(2,1)}), bf16[64,8,896]{2,1,0:T(8,128)(2,1)S(1)}, u32[]{:S(2)}, u32[]{:S(2)}) async-start(bf16[64,8,896]{2,1,0:T(8,128)(2,1)} %bitcast.29), calls=%async_computation.3 | async-start | bytes 1835008 | tf_op jit(solution)/shard_map/all_to_all | solution.py:352
  122.8 3.1 %collective-permute-start.12 = (f32[8,128]{1,0:T(8,128)S(1)}, f32[8,128]{1,0:T(8,128)S(1)}, u32[]{:S(2)}, u32[]{:S(2)}) collective-permute-start(f32[8,128]{1,0:T(8,128)S(1)} %get-tuple-element.23), channel_id=1, source_target_pairs={{0,4},{4,0},{8,12},{12,8},{16,20},{20,16},{24,28},{28,24},{32,36},... | collective-permute-start | bytes 12296 | tf_op jit(solution)/shard_map/ppermute | solution.py:361
  149.0 8.7 %all-to-all-start.4 = ((bf16[4,4,896]{2,1,0:T(4,128)(2,1)}), bf16[4,4,896]{2,1,0:T(4,128)(2,1)S(1)}, u32[]{:S(2)}, u32[]{:S(2)}) async-start(bf16[4,4,896]{2,1,0:T(4,128)(2,1)} %shard_map.102), calls=%async_computation.4 | async-start | bytes 57344 | tf_op jit(solution)/shard_map/all_to_all | solution.py:358

commit v6 on v5

--- a/solution.py
+++ b/solution.py
@@ -196,13 +196,23 @@
         load.wait()
 
 
-def last_piece_body(first_ref, second_ref, gate_in, up_in, far_ref, out_ref):
-    gate, up = products(first_ref, second_ref, far_ref[0], far_ref[1])
-    gate += gate_in[...]
-    up += up_in[...]
-    hidden = (gate / (1.0 + jnp.exp(-gate)) * up).astype(BF16)
+def finish(x_ref, gate_in, up_in, far_ref, at):
+    gate = gate_in[at] + jnp.dot(x_ref[...], far_ref[0], preferred_element_type=F32)
+    up = up_in[at] + jnp.dot(x_ref[...], far_ref[1], preferred_element_type=F32)
+    return (gate / (1.0 + jnp.exp(-gate)) * up).astype(BF16)
+
+
+def first_half_body(x_ref, gate_in, up_in, far_ref, out_ref):
+    rows = x_ref.shape[0]
+    out_ref[...] = finish(x_ref, gate_in, up_in, far_ref, slice(0, rows))
+
+
+def second_half_body(x_ref, gate_in, up_in, far_ref, first_ref, out_ref):
+    rows = x_ref.shape[0]
+    hidden = finish(x_ref, gate_in, up_in, far_ref, slice(rows, 2 * rows))
     for i in range(out_ref.shape[0]):
-        out_ref[i] = hidden
+        out_ref[i, :rows] = first_ref[...]
+        out_ref[i, rows:] = hidden
 
 
 def down_body(here_ref, hid_ref, w_ref, out_hbm, out_ref, sems):
@@ -333,11 +343,17 @@
         ],
         vmem=16,
     )
+    (first_hidden,) = call(
+        first_half_body,
+        [shape((count // 2, 2 * hid), BF16)],
+        [far_first, gate_sum, up_sum, far_weights],
+        flops // 2,
+    )
     (hidden,) = call(
-        last_piece_body,
+        second_half_body,
         [shape((dp, count, 2 * hid), BF16)],
-        [far_first, far_second, gate_sum, up_sum, far_weights],
-        flops,
+        [far_second, gate_sum, up_sum, far_weights, first_hidden],
+        flops // 2,
     )
     hidden = lax.all_to_all(hidden, "dp", 0, 0)
     (out,) = call(

time: 159 us -> 159 us (level)
    ppermute x1, starting transfers between devices: 5.13 us -> 1.92 us  [local(): right_first = lax.ppermute(first, 'dp', behind)]
    ppermute x1, waiting for transfers between devices: 0.01 us -> 2.84 us  [local(): right_second = lax.ppermute(second, 'dp', behind)]
    ppermute x1, starting transfers between devices: 1.92 us -> 3.92 us  [local(): left_second = lax.ppermute(second, 'dp', ahead)]
    pallas_call x8 -> x9, Pallas kernels: 12 us -> 12.2 us  [call(): pl.pallas_call(body, out_shape=tuple((pltpu.HBM(o.shape, o.dtype) if spec...]
where the time goes in v6:
time: 159 us; the launch traced here: 158 us
  starting transfers between devices  73.3 us (46%)
  waiting for transfers between devices  45 us (28%)
  blocking collectives  25.2 us (16%)
  Pallas kernels  12.2 us (8%)
    all_to_all x1, waiting for transfers between devices, local(): lax.all_to_all(out.reshape(slots, per_slot, piece), 'ep', 0, 0, axis_inde...  22.3 us
    all_to_all x1, starting transfers between devices, local(): lax.all_to_all(rows.reshape(slots, per_slot, piece), 'ep', 0, 0, axis_ind...  16.6 us
    all_to_all x1, starting transfers between devices, local(): lax.all_to_all(out.reshape(slots, per_slot, piece), 'ep', 0, 0, axis_inde...  16.1 us
    all_to_all x1, blocking collectives, local(): hidden = lax.all_to_all(hidden, 'dp', 0, 0)  15.7 us
    pallas_call x9, Pallas kernels, call(): pl.pallas_call(body, out_shape=tuple((pltpu.HBM(o.shape, o.dtype) if spec...  12.2 us
    all_to_all x1, blocking collectives, local(): got = lax.all_to_all(send, 'dp', 0, 0)  9.54 us
    ppermute x3, starting transfers between devices, local(): lax.ppermute(block, 'dp', [(x, (x + d) % dp) for x in range(dp)])  8.83 us
    ppermute x1, starting transfers between devices, local(): far_second = lax.ppermute(right_second, 'dp', behind)  5.59 us
  transfers between devices with their start and end apart: 16, of which 11 were waited for; matrix products, arithmetic and copies ran while one was open for 0% of the time, Pallas kernels for 3%

profile of v6, /device:TPU:8, one launch (start us, length us, event | category | flops | bytes accessed | tf_op | source)
XLA Modules:
  0.0 158.0 jit_solution(5045014029225448465)
XLA Ops:
  0.6 1.5 shard_map.95
  2.1 9.5 %all_to_all.25 = bf16[4,4,1024]{2,1,0:T(4,128)(2,1)S(1)} all-to-all(bf16[4,4,1024]{2,1,0:T(4,128)(2,1)S(1)} %shard_map.95), channel_id=1, replica_groups=mesh['ep'=128,'dp'=4] {'dp'}, dimensions={0} | all-to-all | bytes 65536 | tf_op jit(solution)/shard_map/all_to_all | solution.py:283
  11.7 1.7 %shard_map.96 = (bf16[512,896]{1,0:T(8,128)(2,1)}, bf16[512,16]{1,0:T(8,128)(2,1)S(1)}) custom-call(bf16[16,1024]{1,0:T(8,128)(2,1)S(1)} %reshape.50.got_ref), custom_call_target="tpu_custom_call" | custom-call | bytes 966656 | tf_op jit(solution)/shard_map/pallas_call | solution.py:29
  13.4 16.6 %all-to-all-start.1 = ((bf16[64,8,896]{2,1,0:T(8,128)(2,1)}), bf16[64,8,896]{2,1,0:T(8,128)(2,1)S(1)}, u32[]{:S(2)}, u32[]{:S(2)}) async-start(bf16[64,8,896]{2,1,0:T(8,128)(2,1)} %bitcast.30), calls=%async_computation.1 | async-start | bytes 1835008 | tf_op jit(solution)/shard_map/all_to_all | solution.py:302
  30.1 3.1 %collective-permute-start.2 = (bf16[128,896]{1,0:T(8,128)(2,1)S(1)}, bf16[128,896]{1,0:T(8,128)(2,1)S(1)}, u32[]{:S(2)}, u32[]{:S(2)}) collective-permute-start(bf16[128,896]{1,0:T(8,128)(2,1)S(1)} %get-tuple-element.26), channel_id=1, source_target_pairs={{0,3},{1,0},{2,1},{3,2},{4,7},{5,4},{6,5},{7,6},{8,11},{9,8},{10,9... | collective-permute-start | bytes 688136 | tf_op jit(solution)/shard_map/ppermute | solution.py:291
  33.2 2.8 %collective-permute-start = (bf16[128,896]{1,0:T(8,128)(2,1)S(1)}, bf16[128,896]{1,0:T(8,128)(2,1)S(1)}, u32[]{:S(2)}, u32[]{:S(2)}) collective-permute-start(bf16[128,896]{1,0:T(8,128)(2,1)S(1)} %get-tuple-element.25), channel_id=1, source_target_pairs={{0,1},{1,2},{2,3},{3,0},{4,5},{5,6},{6,7},{7,4},{8,9},{9,10},{10,1... | collective-permute-start | bytes 688136 | tf_op jit(solution)/shard_map/ppermute | solution.py:291
  36.0 3.0 %collective-permute-start.1 = (bf16[128,896]{1,0:T(8,128)(2,1)S(1)}, bf16[128,896]{1,0:T(8,128)(2,1)S(1)}, u32[]{:S(2)}, u32[]{:S(2)}) collective-permute-start(bf16[128,896]{1,0:T(8,128)(2,1)S(1)} %get-tuple-element.27), channel_id=1, source_target_pairs={{0,2},{1,3},{2,0},{3,1},{4,6},{5,7},{6,4},{7,5},{8,10},{9,11},{10,... | collective-permute-start | bytes 688136 | tf_op jit(solution)/shard_map/ppermute | solution.py:291
  38.9 1.9 %collective-permute-start.4 = (bf16[3584,128]{1,0:T(8,128)(2,1)}, bf16[3584,128]{1,0:T(8,128)(2,1)S(1)}, u32[]{:S(2)}, u32[]{:S(2)}) collective-permute-start(bf16[3584,128]{1,0:T(8,128)(2,1)} %bitcast.12.refs_0_), channel_id=1, source_target_pairs={{0,4},{4,0},{8,12},{12,8},{16,20},{20,16},{24,28},{28,24},{32,36},... | collective-permute-start | bytes 2752520 | tf_op jit(solution)/shard_map/ppermute | solution.py:286
  40.9 2.4 %collective-permute-start.5 = (bf16[3584,128]{1,0:T(8,128)(2,1)}, bf16[3584,128]{1,0:T(8,128)(2,1)S(1)}, u32[]{:S(2)}, u32[]{:S(2)}) collective-permute-start(bf16[3584,128]{1,0:T(8,128)(2,1)} %bitcast.26), channel_id=1, source_target_pairs={{0,4},{4,0},{8,12},{12,8},{16,20},{20,16},{24,28},{28,24},{32,36},... | collective-permute-start | bytes 2752520 | tf_op jit(solution)/shard_map/ppermute | solution.py:287
  43.3 3.6 %collective-permute-done = bf16[128,896]{1,0:T(8,128)(2,1)S(1)} collective-permute-done((bf16[128,896]{1,0:T(8,128)(2,1)S(1)}, bf16[128,896]{1,0:T(8,128)(2,1)S(1)}, u32[]{:S(2)}, u32[]{:S(2)}) %collective-permute-start) | collective-permute-done | bytes 229408 | tf_op jit(solution)/shard_map/ppermute | solution.py:291
  47.0 1.9 %collective-permute-start.3 = (bf16[4,128,896]{2,1,0:T(8,128)(2,1)S(1)}, bf16[4,128,896]{2,1,0:T(8,128)(2,1)}, u32[]{:S(2)}, u32[]{:S(2)}) collective-permute-start(bf16[4,128,896]{2,1,0:T(8,128)(2,1)S(1)} %pad_maximum_fusion.refs_4_), channel_id=1, source_target_pairs={{0,4},{4,0},{8,12},{12,8},{16,20},{20,16},{24,28},{28,24},{32,36},... | collective-permute-start | bytes 2752520 | tf_op jit(solution)/shard_map/ppermute | solution.py:293
  49.0 2.5 %collective-permute-done.3.refs_0_.refs_5_ = bf16[4,128,896]{2,1,0:T(8,128)(2,1)} collective-permute-done((bf16[4,128,896]{2,1,0:T(8,128)(2,1)S(1)}, bf16[4,128,896]{2,1,0:T(8,128)(2,1)}, u32[]{:S(2)}, u32[]{:S(2)}) %collective-permute-start.3) | collective-permute-done | bytes 917536 | tf_op jit(solution)/shard_map/ppermute | solution.py:293
  51.5 4.4 %all-to-all-done.1 = bf16[64,8,896]{2,1,0:T(8,128)(2,1)S(1)} async-done(((bf16[64,8,896]{2,1,0:T(8,128)(2,1)}), bf16[64,8,896]{2,1,0:T(8,128)(2,1)S(1)}, u32[]{:S(2)}, u32[]{:S(2)}) %all-to-all-start.1) | async-done | bytes 917536 | tf_op jit(solution)/shard_map/all_to_all | solution.py:302
  56.2 2.5 %collective-permute-start.8 = (bf16[256,896]{1,0:T(8,128)(2,1)S(1)}, bf16[256,896]{1,0:T(8,128)(2,1)S(1)}, u32[]{:S(2)}, u32[]{:S(2)}) collective-permute-start(bf16[256,896]{1,0:T(8,128)(2,1)S(1)} %get-tuple-element.16.first_ref), channel_id=1, source_target_pairs={{0,1},{1,2},{2,3},{3,0},{4,5},{5,6},{6,7},{7,4},{8,9},{9,10},{10,1... | collective-permute-start | bytes 1376264 | tf_op jit(solution)/shard_map/ppermute | solution.py:316
  58.6 4.6 %collective-permute-start.6 = (bf16[256,896]{1,0:T(8,128)(2,1)S(1)}, bf16[256,896]{1,0:T(8,128)(2,1)S(1)}, u32[]{:S(2)}, u32[]{:S(2)}) collective-permute-start(bf16[256,896]{1,0:T(8,128)(2,1)S(1)} %get-tuple-element.15.second_ref), channel_id=1, source_target_pairs={{0,3},{1,0},{2,1},{3,2},{4,7},{5,4},{6,5},{7,6},{8,11},{9,8},{10,9... | collective-permute-start | bytes 1376264 | tf_op jit(solution)/shard_map/ppermute | solution.py:317
  63.2 1.9 %collective-permute-start.10 = (bf16[256,896]{1,0:T(8,128)(2,1)S(1)}, bf16[256,896]{1,0:T(8,128)(2,1)S(1)}, u32[]{:S(2)}, u32[]{:S(2)}) collective-permute-start(bf16[256,896]{1,0:T(8,128)(2,1)S(1)} %get-tuple-element.16.first_ref), channel_id=1, source_target_pairs={{0,3},{1,0},{2,1},{3,2},{4,7},{5,4},{6,5},{7,6},{8,11},{9,8},{10,9... | collective-permute-start | bytes 1376264 | tf_op jit(solution)/shard_map/ppermute | solution.py:319
  65.2 3.9 %collective-permute-start.9 = (bf16[256,896]{1,0:T(8,128)(2,1)S(1)}, bf16[256,896]{1,0:T(8,128)(2,1)S(1)}, u32[]{:S(2)}, u32[]{:S(2)}) collective-permute-start(bf16[256,896]{1,0:T(8,128)(2,1)S(1)} %get-tuple-element.15.second_ref), channel_id=1, source_target_pairs={{0,1},{1,2},{2,3},{3,0},{4,5},{5,6},{6,7},{7,4},{8,9},{9,10},{10,1... | collective-permute-start | bytes 1376264 | tf_op jit(solution)/shard_map/ppermute | solution.py:318
  69.4 1.9 %collective-permute-start.11 = (bf16[256,896]{1,0:T(8,128)(2,1)S(1)}, bf16[256,896]{1,0:T(8,128)(2,1)S(1)}, u32[]{:S(2)}, u32[]{:S(2)}) collective-permute-start(bf16[256,896]{1,0:T(8,128)(2,1)S(1)} %collective-permute-done.8.left_first), channel_id=1, source_target_pairs={{0,1},{1,2},{2,3},{3,0},{4,5},{5,6},{6,7},{7,4},{8,9},{9,10},{10,1... | collective-permute-start | bytes 1376264 | tf_op jit(solution)/shard_map/ppermute | solution.py:320
  71.3 2.8 %collective-permute-done.6.right_second = bf16[256,896]{1,0:T(8,128)(2,1)S(1)} collective-permute-done((bf16[256,896]{1,0:T(8,128)(2,1)S(1)}, bf16[256,896]{1,0:T(8,128)(2,1)S(1)}, u32[]{:S(2)}, u32[]{:S(2)}) %collective-permute-start.6) | collective-permute-done | bytes 458784 | tf_op jit(solution)/shard_map/ppermute | solution.py:317
  74.2 5.6 %collective-permute-start.7 = (bf16[256,896]{1,0:T(8,128)(2,1)S(1)}, bf16[256,896]{1,0:T(8,128)(2,1)S(1)}, u32[]{:S(2)}, u32[]{:S(2)}) collective-permute-start(bf16[256,896]{1,0:T(8,128)(2,1)S(1)} %collective-permute-done.6.right_second), channel_id=1, source_target_pairs={{0,3},{1,0},{2,1},{3,2},{4,7},{5,4},{6,5},{7,6},{8,11},{9,8},{10,9... | collective-permute-start | bytes 1376264 | tf_op jit(solution)/shard_map/ppermute | solution.py:321
  79.8 2.0 %shard_map.98 = (f32[512,256]{1,0:T(8,128)S(1)}, f32[512,256]{1,0:T(8,128)S(1)}) custom-call(s32[1]{0:T(128)} %bitcast.3.here_ref, bf16[256,896]{1,0:T(8,128)(2,1)S(1)} %get-tuple-element.16.first_ref, bf16[256,896]{1,0:T(8,128)(2,1)S(1)} %get-tuple-element.15.second_ref, bf16[3584,128]{1,0:T(8,128)(2,1)} %bitcast.12.refs_0_, bf16[3584,128]{1,0:T(8,128)(2,1)} %bitcast.27, ...), custom_call_target="tpu_custom_call" | custom-call | flops 469762048 | bytes 5636100 | tf_op jit(solution)/shard_map/pallas_call | solution.py:29
  81.8 1.5 collective-permute-done.10.right_first
  83.3 3.0 %shard_map.99 = (f32[512,256]{1,0:T(8,128)S(1)}, f32[512,256]{1,0:T(8,128)S(1)}, bf16[2,896,256]{2,1,0:T(8,128)(2,1)S(1)}, bf16[4,256,896]{2,1,0:T(8,128)(2,1)S(1)}) custom-call(s32[1]{0:T(128)} %bitcast.3.here_ref, bf16[256,896]{1,0:T(8,128)(2,1)S(1)} %collective-permute-done.8.left_first, bf16[256,896]{1,0:T(8,128)(2,1)S(1)} %collective-permute-done.9.left_second, ...), custom_call_target="tpu_custom_call" | custom-call | flops 939524096 | bytes 12189700 | tf_op jit(solution)/shard_map/pallas_call | solution.py:29
  86.3 1.1 collective-permute-done.11.x_ref
  88.7 15.7 %all_to_all.26.hid_ref = bf16[4,512,256]{2,1,0:T(8,128)(2,1)S(1)} all-to-all(bf16[4,512,256]{2,1,0:T(8,128)(2,1)S(1)} %shard_map.101), channel_id=1, replica_groups=mesh['ep'=128,'dp'=4] {'dp'}, dimensions={0} | all-to-all | bytes 2097152 | tf_op jit(solution)/shard_map/all_to_all | solution.py:358
  104.4 2.1 %shard_map.102 = bf16[512,896]{1,0:T(8,128)(2,1)} custom-call(s32[1]{0:T(128)} %bitcast.3.here_ref, bf16[4,512,256]{2,1,0:T(8,128)(2,1)S(1)} %all_to_all.26.hid_ref, bf16[4,256,896]{2,1,0:T(8,128)(2,1)S(1)} %get-tuple-element.22.w_ref), custom_call_target="tpu_custom_call" | custom-call | flops 939524096 | bytes 3801092 | tf_op jit(solution)/shard_map/pallas_call | solution.py:29
  106.5 16.1 %all-to-all-start.3 = ((bf16[64,8,896]{2,1,0:T(8,128)(2,1)}), bf16[64,8,896]{2,1,0:T(8,128)(2,1)S(1)}, u32[]{:S(2)}, u32[]{:S(2)}) async-start(bf16[64,8,896]{2,1,0:T(8,128)(2,1)} %bitcast.29), calls=%async_computation.3 | async-start | bytes 1835008 | tf_op jit(solution)/shard_map/all_to_all | solution.py:368
  122.5 1.9 %collective-permute-start.12 = (f32[8,128]{1,0:T(8,128)S(1)}, f32[8,128]{1,0:T(8,128)S(1)}, u32[]{:S(2)}, u32[]{:S(2)}) collective-permute-start(f32[8,128]{1,0:T(8,128)S(1)} %get-tuple-element.23), channel_id=1, source_target_pairs={{0,4},{4,0},{8,12},{12,8},{16,20},{20,16},{24,28},{28,24},{32,36},... | collective-permute-start | bytes 12296 | tf_op jit(solution)/shard_map/ppermute | solution.py:377
  124.5 1.1 collective-permute-done.12
  125.6 22.3 %all-to-all-done.3 = bf16[64,8,896]{2,1,0:T(8,128)(2,1)S(1)} async-done(((bf16[64,8,896]{2,1,0:T(8,128)(2,1)}), bf16[64,8,896]{2,1,0:T(8,128)(2,1)S(1)}, u32[]{:S(2)}, u32[]{:S(2)}) %all-to-all-start.3) | async-done | bytes 917536 | tf_op jit(solution)/shard_map/all_to_all | solution.py:368
  148.8 3.3 %all-to-all-start.4 = ((bf16[4,4,896]{2,1,0:T(4,128)(2,1)}), bf16[4,4,896]{2,1,0:T(4,128)(2,1)S(1)}, u32[]{:S(2)}, u32[]{:S(2)}) async-start(bf16[4,4,896]{2,1,0:T(4,128)(2,1)} %shard_map.103), calls=%async_computation.4 | async-start | bytes 57344 | tf_op jit(solution)/shard_map/all_to_all | solution.py:374
  152.6 4.9 %all-to-all-done.4 = bf16[4,4,896]{2,1,0:T(4,128)(2,1)S(1)} async-done(((bf16[4,4,896]{2,1,0:T(4,128)(2,1)}), bf16[4,4,896]{2,1,0:T(4,128)(2,1)S(1)}, u32[]{:S(2)}, u32[]{:S(2)}) %all-to-all-start.4) | async-done | bytes 28704 | tf_op jit(solution)/shard_map/all_to_all | solution.py:374
  (25 shorter events, 4.1 us)
Async XLA Ops:
  0.6 29.4 %copy-start.3 = (bf16[1,128,3584]{2,1,0:T(8,128)(2,1)S(1)}, bf16[1,128,3584]{2,1,0:T(8,128)(2,1)}, u32[]{:S(2)}) copy-start(bf16[1,128,3584]{2,1,0:T(8,128)(2,1)} %param.15) | copy-start | bytes 2752516
  13.4 42.6 %all-to-all-start.1 = ((bf16[64,8,896]{2,1,0:T(8,128)(2,1)}), bf16[64,8,896]{2,1,0:T(8,128)(2,1)S(1)}, u32[]{:S(2)}, u32[]{:S(2)}) async-start(bf16[64,8,896]{2,1,0:T(8,128)(2,1)} %bitcast.30), calls=%async_computation.1 | async-start | bytes 1835008 | tf_op jit(solution)/shard_map/all_to_all | solution.py:302
  30.1 13.2 %collective-permute-start.2 = (bf16[128,896]{1,0:T(8,128)(2,1)S(1)}, bf16[128,896]{1,0:T(8,128)(2,1)S(1)}, u32[]{:S(2)}, u32[]{:S(2)}) collective-permute-start(bf16[128,896]{1,0:T(8,128)(2,1)S(1)} %get-tuple-element.26), channel_id=1, source_target_pairs={{0,3},{1,0},{2,1},{3,2},{4,7},{5,4},{6,5},{7,6},{8,11},{9,8},{10,9... | collective-permute-start | bytes 688136 | tf_op jit(solution)/shard_map/ppermute | solution.py:291
  33.2 13.7 %collective-permute-start = (bf16[128,896]{1,0:T(8,128)(2,1)S(1)}, bf16[128,896]{1,0:T(8,128)(2,1)S(1)}, u32[]{:S(2)}, u32[]{:S(2)}) collective-permute-start(bf16[128,896]{1,0:T(8,128)(2,1)S(1)} %get-tuple-element.25), channel_id=1, source_target_pairs={{0,1},{1,2},{2,3},{3,0},{4,5},{5,6},{6,7},{7,4},{8,9},{9,10},{10,1... | collective-permute-start | bytes 688136 | tf_op jit(solution)/shard_map/ppermute | solution.py:291
  36.0 10.9 %collective-permute-start.1 = (bf16[128,896]{1,0:T(8,128)(2,1)S(1)}, bf16[128,896]{1,0:T(8,128)(2,1)S(1)}, u32[]{:S(2)}, u32[]{:S(2)}) collective-permute-start(bf16[128,896]{1,0:T(8,128)(2,1)S(1)} %get-tuple-element.27), channel_id=1, source_target_pairs={{0,2},{1,3},{2,0},{3,1},{4,6},{5,7},{6,4},{7,5},{8,10},{9,11},{10,... | collective-permute-start | bytes 688136 | tf_op jit(solution)/shard_map/ppermute | solution.py:291
  38.9 10.0 %collective-permute-start.4 = (bf16[3584,128]{1,0:T(8,128)(2,1)}, bf16[3584,128]{1,0:T(8,128)(2,1)S(1)}, u32[]{:S(2)}, u32[]{:S(2)}) collective-permute-start(bf16[3584,128]{1,0:T(8,128)(2,1)} %bitcast.12.refs_0_), channel_id=1, source_target_pairs={{0,4},{4,0},{8,12},{12,8},{16,20},{20,16},{24,28},{28,24},{32,36},... | collective-permute-start | bytes 2752520 | tf_op jit(solution)/shard_map/ppermute | solution.py:286
  40.9 8.1 %collective-permute-start.5 = (bf16[3584,128]{1,0:T(8,128)(2,1)}, bf16[3584,128]{1,0:T(8,128)(2,1)S(1)}, u32[]{:S(2)}, u32[]{:S(2)}) collective-permute-start(bf16[3584,128]{1,0:T(8,128)(2,1)} %bitcast.26), channel_id=1, source_target_pairs={{0,4},{4,0},{8,12},{12,8},{16,20},{20,16},{24,28},{28,24},{32,36},... | collective-permute-start | bytes 2752520 | tf_op jit(solution)/shard_map/ppermute | solution.py:287
  47.0 2.0 %copy-start.2 = (bf16[4,128,896]{2,1,0:T(8,128)(2,1)}, bf16[4,128,896]{2,1,0:T(8,128)(2,1)S(1)}, u32[]{:S(2)}) copy-start(bf16[4,128,896]{2,1,0:T(8,128)(2,1)S(1)} %pad_maximum_fusion.refs_4_) | copy-start | bytes 2752516
  47.0 4.5 %collective-permute-start.3 = (bf16[4,128,896]{2,1,0:T(8,128)(2,1)S(1)}, bf16[4,128,896]{2,1,0:T(8,128)(2,1)}, u32[]{:S(2)}, u32[]{:S(2)}) collective-permute-start(bf16[4,128,896]{2,1,0:T(8,128)(2,1)S(1)} %pad_maximum_fusion.refs_4_), channel_id=1, source_target_pairs={{0,4},{4,0},{8,12},{12,8},{16,20},{20,16},{24,28},{28,24},{32,36},... | collective-permute-start | bytes 2752520 | tf_op jit(solution)/shard_map/ppermute | solution.py:293
  49.0 7.2 %copy-start = (bf16[3584,128]{1,0:T(8,128)(2,1)}, bf16[3584,128]{1,0:T(8,128)(2,1)S(1)}, u32[]{:S(2)}) copy-start(bf16[3584,128]{1,0:T(8,128)(2,1)S(1)} %collective-permute-done.4.refs_1_.refs_2_) | copy-start | bytes 2752516
  49.0 7.1 %copy-start.1 = (bf16[3584,128]{1,0:T(8,128)(2,1)}, bf16[3584,128]{1,0:T(8,128)(2,1)S(1)}, u32[]{:S(2)}) copy-start(bf16[3584,128]{1,0:T(8,128)(2,1)S(1)} %collective-permute-done.5.refs_2_.refs_3_) | copy-start | bytes 2752516
  56.2 13.3 %collective-permute-start.8 = (bf16[256,896]{1,0:T(8,128)(2,1)S(1)}, bf16[256,896]{1,0:T(8,128)(2,1)S(1)}, u32[]{:S(2)}, u32[]{:S(2)}) collective-permute-start(bf16[256,896]{1,0:T(8,128)(2,1)S(1)} %get-tuple-element.16.first_ref), channel_id=1, source_target_pairs={{0,1},{1,2},{2,3},{3,0},{4,5},{5,6},{6,7},{7,4},{8,9},{9,10},{10,1... | collective-permute-start | bytes 1376264 | tf_op jit(solution)/shard_map/ppermute | solution.py:316
  58.6 15.5 %collective-permute-start.6 = (bf16[256,896]{1,0:T(8,128)(2,1)S(1)}, bf16[256,896]{1,0:T(8,128)(2,1)S(1)}, u32[]{:S(2)}, u32[]{:S(2)}) collective-permute-start(bf16[256,896]{1,0:T(8,128)(2,1)S(1)} %get-tuple-element.15.second_ref), channel_id=1, source_target_pairs={{0,3},{1,0},{2,1},{3,2},{4,7},{5,4},{6,5},{7,6},{8,11},{9,8},{10,9... | collective-permute-start | bytes 1376264 | tf_op jit(solution)/shard_map/ppermute | solution.py:317
  63.2 20.1 %collective-permute-start.10 = (bf16[256,896]{1,0:T(8,128)(2,1)S(1)}, bf16[256,896]{1,0:T(8,128)(2,1)S(1)}, u32[]{:S(2)}, u32[]{:S(2)}) collective-permute-start(bf16[256,896]{1,0:T(8,128)(2,1)S(1)} %get-tuple-element.16.first_ref), channel_id=1, source_target_pairs={{0,3},{1,0},{2,1},{3,2},{4,7},{5,4},{6,5},{7,6},{8,11},{9,8},{10,9... | collective-permute-start | bytes 1376264 | tf_op jit(solution)/shard_map/ppermute | solution.py:319
  65.2 18.2 %collective-permute-start.9 = (bf16[256,896]{1,0:T(8,128)(2,1)S(1)}, bf16[256,896]{1,0:T(8,128)(2,1)S(1)}, u32[]{:S(2)}, u32[]{:S(2)}) collective-permute-start(bf16[256,896]{1,0:T(8,128)(2,1)S(1)} %get-tuple-element.15.second_ref), channel_id=1, source_target_pairs={{0,1},{1,2},{2,3},{3,0},{4,5},{5,6},{6,7},{7,4},{8,9},{9,10},{10,1... | collective-permute-start | bytes 1376264 | tf_op jit(solution)/shard_map/ppermute | solution.py:318
  69.4 18.0 %collective-permute-start.11 = (bf16[256,896]{1,0:T(8,128)(2,1)S(1)}, bf16[256,896]{1,0:T(8,128)(2,1)S(1)}, u32[]{:S(2)}, u32[]{:S(2)}) collective-permute-start(bf16[256,896]{1,0:T(8,128)(2,1)S(1)} %collective-permute-done.8.left_first), channel_id=1, source_target_pairs={{0,1},{1,2},{2,3},{3,0},{4,5},{5,6},{6,7},{7,4},{8,9},{9,10},{10,1... | collective-permute-start | bytes 1376264 | tf_op jit(solution)/shard_map/ppermute | solution.py:320
  74.2 14.0 %collective-permute-start.7 = (bf16[256,896]{1,0:T(8,128)(2,1)S(1)}, bf16[256,896]{1,0:T(8,128)(2,1)S(1)}, u32[]{:S(2)}, u32[]{:S(2)}) collective-permute-start(bf16[256,896]{1,0:T(8,128)(2,1)S(1)} %collective-permute-done.6.right_second), channel_id=1, source_target_pairs={{0,3},{1,0},{2,1},{3,2},{4,7},{5,4},{6,5},{7,6},{8,11},{9,8},{10,9... | collective-permute-start | bytes 1376264 | tf_op jit(solution)/shard_map/ppermute | solution.py:321
  106.5 41.4 %all-to-all-start.3 = ((bf16[64,8,896]{2,1,0:T(8,128)(2,1)}), bf16[64,8,896]{2,1,0:T(8,128)(2,1)S(1)}, u32[]{:S(2)}, u32[]{:S(2)}) async-start(bf16[64,8,896]{2,1,0:T(8,128)(2,1)} %bitcast.29), calls=%async_computation.3 | async-start | bytes 1835008 | tf_op jit(solution)/shard_map/all_to_all | solution.py:368
  122.5 3.1 %collective-permute-start.12 = (f32[8,128]{1,0:T(8,128)S(1)}, f32[8,128]{1,0:T(8,128)S(1)}, u32[]{:S(2)}, u32[]{:S(2)}) collective-permute-start(f32[8,128]{1,0:T(8,128)S(1)} %get-tuple-element.23), channel_id=1, source_target_pairs={{0,4},{4,0},{8,12},{12,8},{16,20},{20,16},{24,28},{28,24},{32,36},... | collective-permute-start | bytes 12296 | tf_op jit(solution)/shard_map/ppermute | solution.py:377
  148.8 8.7 %all-to-all-start.4 = ((bf16[4,4,896]{2,1,0:T(4,128)(2,1)}), bf16[4,4,896]{2,1,0:T(4,128)(2,1)S(1)}, u32[]{:S(2)}, u32[]{:S(2)}) async-start(bf16[4,4,896]{2,1,0:T(4,128)(2,1)} %shard_map.103), calls=%async_computation.4 | async-start | bytes 57344 | tf_op jit(solution)/shard_map/all_to_all | solution.py:374
